TPU v7x, 1024 devices: a whole 4x8x16 slice. The times are simulated.
1024 devices in a mesh: mesh: 32 (over y, x), sub: 32 (over z, core).
Axes of the slice: x: 4, y: 8, z: 16, core: 2. Of those that a mesh axis runs over, the one named last changes fastest.
Arguments:
- displacement: float32 [3, 2, 256, 4096], P(None, None, 'mesh', 'sub'), may hold values from -4 to 4
- velocity: float32 [3, 2, 256, 4096], P(None, None, 'mesh', 'sub'), may hold values from -6 to 6
- node_mass: float32 [2, 256, 4096], P(None, 'mesh', 'sub'), may hold values from 0.5 to 2
- moduli: float32 [2, 256, 4096], P(None, 'mesh', 'sub'), may hold values from 0.5 to 2
- stiffness: float32 [24, 24], replicated, may hold values from -0.45 to 12, as said below
- surface_ref: float32 [3, 256, 4096], P(None, 'mesh', 'sub'), may hold values from -6 to 6
- facets: float32 [32, 32, 6, 1024], P('mesh', 'sub'), may hold values from -6 to 6
- penalty: float32 [32, 32, 1024], P('mesh', 'sub'), may hold values from 0.5 to 4
- owners: int32 [2, 32, 32, 8, 1], P(None, 'mesh', 'sub'), may hold values from 0 to 31; in each aligned block of 8 rows (0 to 7, 8 to 15, ..., all dimensions but the last counted through in order) at most 2 rows name the same one
- facet_pairs: int32 [2, 256, 4096], P(None, 'mesh', 'sub'), may hold values from 0 to 1023
Outputs:
- final_displacement: float32 [3, 2, 256, 4096], P(None, None, 'mesh', 'sub')
- final_velocity: float32 [3, 2, 256, 4096], P(None, None, 'mesh', 'sub')
Inputs may be any that keep to these rules, and one draw needn't show every extreme that they name: `owners`: in every step no device sends more than 2 of its blocks to one owner, and some device sends exactly 2 to one owner. `stiffness`: Symmetric.
All inputs are finite; a program needn't handle non-finite values.
Results may differ from a plain program's by a relative error of at most 0.0001.
Values sent between devices are 32-bit elements; how exact they have to be, the bound alone decides.
No kernel may reach another device: no remote copies, remote signals or barrier semaphores. Data moves between devices by JAX's collectives and lax.ppermute only.
A program may use at most 64 MiB of HBM per device.

v0:
```python
import math

import jax
import jax.numpy as jnp
from jax import lax
from jax.sharding import PartitionSpec as P

TIME_STEP = 0.1
CORNER_SHIFTS = (
    (0, 0, 0),
    (0, 0, 1),
    (0, 1, 0),
    (0, 1, 1),
    (1, 0, 0),
    (1, 0, 1),
    (1, 1, 0),
    (1, 1, 1),
)


def with_halo(shard, sides, width):
    for axis, dim in sides:
        size, length = (lax.axis_size(axis), shard.shape[dim])
        up = [(i, (i + 1) % size) for i in range(size)]
        down = [(j, i) for i, j in up]
        last = lax.slice_in_dim(shard, length - width, length, axis=dim)
        leading = lax.slice_in_dim(shard, 0, width, axis=dim)
        before = lax.ppermute(last, axis, up)
        after = lax.ppermute(leading, axis, down)
        shard = jnp.concatenate([before, shard, after], axis=dim)
    return shard


def joined_along(tiles, dim):
    lengths = list(tiles.shape[1:])
    lengths[dim] *= tiles.shape[0]
    return jnp.moveaxis(tiles, 0, dim).reshape(lengths)


def sent_to_all(shard, axis):
    copies = jnp.broadcast_to(shard, (lax.axis_size(axis), *shard.shape))
    return lax.all_to_all(copies, axis, split_axis=0, concat_axis=0, tiled=True)


def gathered_copies(shard, axis, dim):
    return joined_along(sent_to_all(shard, axis), dim)


def in_one_piece(arrays, axis, dim, along):
    widths = [math.prod(a.shape[along:]) for a in arrays]
    both = jnp.concatenate(
        [a.reshape(*a.shape[:along], w) for a, w in zip(arrays, widths)], axis=along
    )
    result = gathered_copies(both, axis, dim)
    tiles = jnp.split(result, [sum(widths[:k]) for k in range(1, len(widths))], axis=along)
    return tuple(
        (b.reshape(*result.shape[:along], *a.shape[along:]) for a, b in zip(arrays, tiles))
    )


def node_forces(node_patch, patch_moduli, stiffness):
    layers = node_patch.shape[1]
    row_count = node_patch.shape[2] - 2
    col_count = node_patch.shape[3] - 2
    element_scale = jnp.zeros((layers - 1, row_count + 1, col_count + 1), jnp.float32)
    corners = []
    for shift_z, shift_x, shift_y in CORNER_SHIFTS:
        element_scale = (
            element_scale
            + patch_moduli[
                shift_z : shift_z + layers - 1,
                shift_x : shift_x + row_count + 1,
                shift_y : shift_y + col_count + 1,
            ]
        )
        corners.append(
            node_patch[
                :,
                shift_z : shift_z + layers - 1,
                shift_x : shift_x + row_count + 1,
                shift_y : shift_y + col_count + 1,
            ]
        )
    element_scale = element_scale * 0.125
    stacked = jnp.concatenate(corners, axis=0).reshape(24, -1)
    forces = (
        jnp.dot(stiffness, stacked, precision=lax.Precision.HIGHEST).reshape(
            24, layers - 1, row_count + 1, col_count + 1
        )
        * element_scale[None]
    )
    summed = jnp.zeros((3, layers, row_count, col_count), jnp.float32)
    for corner, (shift_z, shift_x, shift_y) in enumerate(CORNER_SHIFTS):
        contribution = forces[
            3 * corner : 3 * corner + 3,
            :,
            1 - shift_x : 1 - shift_x + row_count,
            1 - shift_y : 1 - shift_y + col_count,
        ]
        summed = summed.at[:, shift_z : shift_z + layers - 1].add(contribution)
    return summed


def contact_push(points, facet_rows, stiffness_row):
    normal_gap = jnp.sum(facet_rows[3:6] * (points - facet_rows[0:3]), axis=0)
    return facet_rows[3:6] * (stiffness_row * jnp.maximum(-normal_gap, 0.0))[None]


def shards(
    displacement,
    velocity,
    node_mass,
    moduli,
    stiffness,
    surface_ref,
    facets,
    penalty,
    owners,
    facet_pairs,
):
    steps = owners.shape[0]
    row_count = displacement.shape[2]
    col_count = displacement.shape[3]
    table_width = facets.shape[3]
    ext_moduli = with_halo(moduli, (("mesh", 1), ("sub", 2)), 1)
    every_table, every_stiff = in_one_piece((facets, penalty), "mesh", 0, 2)
    wide_table = every_table[:, 0].transpose(1, 0, 2).reshape(6, -1)
    wide_stiff = every_stiff[:, 0].reshape(-1)
    for step_index in range(steps):
        node_patch = with_halo(displacement, (("mesh", 2), ("sub", 3)), 1)
        internal = node_forces(node_patch, ext_moduli, stiffness)
        points = surface_ref + displacement[:, 0]
        pair_rows = facet_pairs[step_index]
        destination = owners[step_index, 0, 0, :, 0]
        lookup = (destination[:, None] * table_width + pair_rows).reshape(-1)
        facet_rows = jnp.take(wide_table, lookup, axis=1)
        pushed = contact_push(points.reshape(3, -1), facet_rows, jnp.take(wide_stiff, lookup))
        surface_push = pushed.reshape(3, row_count, col_count)
        net_force = (-internal).at[:, 0].add(surface_push)
        velocity = velocity + TIME_STEP * net_force / node_mass[None]
        displacement = displacement + TIME_STEP * velocity
    return (displacement, velocity)


def solution(mesh):
    in_specs = (
        P(None, None, "mesh", "sub"),
        P(None, None, "mesh", "sub"),
        P(None, "mesh", "sub"),
        P(None, "mesh", "sub"),
        P(),
        P(None, "mesh", "sub"),
        P("mesh", "sub", None, None),
        P("mesh", "sub", None),
        P(None, "mesh", "sub", None, None),
        P(None, "mesh", "sub"),
    )
    out_specs = (P(None, None, "mesh", "sub"), P(None, None, "mesh", "sub"))
    return jax.shard_map(shards, mesh=mesh, in_specs=in_specs, out_specs=out_specs, check_vma=False)
```

profile of v0, /device:TPU:14, one launch (start us, length us, event | category | flops | bytes accessed | tf_op | source)
XLA Modules:
  0.0 128.3 jit_solution(14237407400541299326)
XLA Ops:
  0.6 0.8 fusion.25
  1.4 3.4 %collective-permute-start.4 = (f32[2,1,128]{2,1,0:T(1,128)S(1)}, f32[2,1,128]{2,1,0:T(1,128)S(1)}, u32[]{:S(2)}, u32[]{:S(2)}) collective-permute-start(f32[2,1,128]{2,1,0:T(1,128)S(1)} %get-tuple-element.246), channel_id=1, source_target_pairs={{0,32},{32,64},{64,96},{96,128},{128,160},{160,192},{192,224},{224... | collective-permute-start | bytes 3080 | tf_op jit(solution)/shard_map/ppermute | solution.py:28
  4.8 2.4 %collective-permute-start.5 = (f32[2,1,128]{2,1,0:T(1,128)S(1)}, f32[2,1,128]{2,1,0:T(1,128)S(1)}, u32[]{:S(2)}, u32[]{:S(2)}) collective-permute-start(f32[2,1,128]{2,1,0:T(1,128)S(1)} %get-tuple-element.247), channel_id=1, source_target_pairs={{32,0},{64,32},{96,64},{128,96},{160,128},{192,160},{224,192},{256... | collective-permute-start | bytes 3080 | tf_op jit(solution)/shard_map/ppermute | solution.py:29
  7.3 0.8 fusion.23
  8.1 5.5 %collective-permute-start = (f32[3,2,1,128]{3,2,1,0:T(1,128)S(1)}, f32[3,2,1,128]{3,2,1,0:T(1,128)S(1)}, u32[]{:S(2)}, u32[]{:S(2)}) collective-permute-start(f32[3,2,1,128]{3,2,1,0:T(1,128)S(1)} %get-tuple-element.236), channel_id=1, source_target_pairs={{0,32},{32,64},{64,96},{96,128},{128,160},{160,192},{192,224},{224... | collective-permute-start | bytes 9224 | tf_op jit(solution)/shard_map/ppermute | solution.py:28
  13.6 1.9 %collective-permute-start.1 = (f32[3,2,1,128]{3,2,1,0:T(1,128)S(1)}, f32[3,2,1,128]{3,2,1,0:T(1,128)S(1)}, u32[]{:S(2)}, u32[]{:S(2)}) collective-permute-start(f32[3,2,1,128]{3,2,1,0:T(1,128)S(1)} %get-tuple-element.237), channel_id=1, source_target_pairs={{32,0},{64,32},{96,64},{128,96},{160,128},{192,160},{224,192},{256... | collective-permute-start | bytes 9224 | tf_op jit(solution)/shard_map/ppermute | solution.py:29
  15.5 0.8 pad_maximum_fusion.5
  16.3 1.4 %broadcast_in_dim.24 = f32[32,1,1,7168]{3,2,1,0:T(1,128)} broadcast(f32[7168]{0:T(1024)S(1)} %bitcast.77), dimensions={3} | broadcast | bytes 946176 | tf_op jit(solution)/shard_map/broadcast_in_dim | solution.py:41
  17.7 21.7 %all-to-all-start = ((f32[32,1,1,7168]{3,2,1,0:T(1,128)}), f32[32,1,1,7168]{3,2,1,0:T(1,128)S(1)}, u32[]{:S(2)}, u32[]{:S(2)}) async-start(f32[32,1,1,7168]{3,2,1,0:T(1,128)} %broadcast_in_dim.24), calls=%async_computation | async-start | bytes 1835008 | tf_op jit(solution)/shard_map/all_to_all | solution.py:42
  40.1 0.7 fusion.10
  40.8 0.8 fusion.19
  41.6 0.8 compare_and_fusion
  43.4 5.1 %collective-permute-start.7 = (f32[2,10,1]{2,1,0:T(8,128)S(1)}, f32[2,10,1]{2,1,0:T(8,128)S(1)}, u32[]{:S(2)}, u32[]{:S(2)}) collective-permute-start(f32[2,10,1]{2,1,0:T(8,128)S(1)} %get-tuple-element.239), channel_id=1, source_target_pairs={{1,0},{2,1},{3,2},{4,3},{5,4},{6,5},{7,6},{8,7},{9,8},{10,9},{11,1... | collective-permute-start | bytes 248 | tf_op jit(solution)/shard_map/ppermute | solution.py:29
  48.5 1.4 %collective-permute-done.6 = f32[2,10,1]{2,1,0:T(8,128)S(1)} collective-permute-done((f32[2,10,1]{2,1,0:T(8,128)S(1)}, f32[2,10,1]{2,1,0:T(8,128)S(1)}, u32[]{:S(2)}, u32[]{:S(2)}) %collective-permute-start.6) | collective-permute-done | bytes 112 | tf_op jit(solution)/shard_map/ppermute | solution.py:28
  49.9 0.9 maximum_maximum_fusion.2
  50.8 0.8 pad_maximum_fusion.2
  51.6 2.9 %collective-permute-start.3 = (f32[3,2,10,1]{3,2,1,0:T(8,128)S(1)}, f32[3,2,10,1]{3,2,1,0:T(8,128)S(1)}, u32[]{:S(2)}, u32[]{:S(2)}) collective-permute-start(f32[3,2,10,1]{3,2,1,0:T(8,128)S(1)} %get-tuple-element.228), channel_id=1, source_target_pairs={{1,0},{2,1},{3,2},{4,3},{5,4},{6,5},{7,6},{8,7},{9,8},{10,9},{11,1... | collective-permute-start | bytes 728 | tf_op jit(solution)/shard_map/ppermute | solution.py:29
  54.6 1.7 %collective-permute-done.3 = f32[3,2,10,1]{3,2,1,0:T(8,128)S(1)} collective-permute-done((f32[3,2,10,1]{3,2,1,0:T(8,128)S(1)}, f32[3,2,10,1]{3,2,1,0:T(8,128)S(1)}, u32[]{:S(2)}, u32[]{:S(2)}) %collective-permute-start.3) | collective-permute-done | bytes 272 | tf_op jit(solution)/shard_map/ppermute | solution.py:29
  56.3 3.0 %collective-permute-done.2 = f32[3,2,10,1]{3,2,1,0:T(8,128)S(1)} collective-permute-done((f32[3,2,10,1]{3,2,1,0:T(8,128)S(1)}, f32[3,2,10,1]{3,2,1,0:T(8,128)S(1)}, u32[]{:S(2)}, u32[]{:S(2)}) %collective-permute-start.2) | collective-permute-done | bytes 272 | tf_op jit(solution)/shard_map/ppermute | solution.py:28
  59.3 0.9 pad_maximum_fusion
  61.7 2.0 %slice_reduce_fusion = f32[32,6144]{1,0:T(8,128)S(1)} fusion(f32[32,1,7168]{2,1,0:T(1,128)S(1)} %bitcast.74), kind=kLoop, calls=%fused_computation.6 | loop fusion | bytes 1572864 | tf_op jit(solution)/shard_map/split | solution.py:55
  63.7 6.2 %gather_fusion.3 = f32[1024]{0:T(1024)S(1)} fusion(f32[32768]{0:T(1024)S(1)} %bitcast.68, s32[1024]{0:T(1024)S(1)} %get-tuple-element.244), kind=kCustom, calls=%fused_computation.3.clone | custom fusion | bytes 12288 | tf_op jit(solution)/shard_map/jit(_take)/gather | solution.py:137
  69.9 6.2 %gather_fusion.1 = f32[1024]{0:T(1024)S(1)} fusion(f32[32768]{0:T(1024)S(1)} %bitcast.69, s32[1024]{0:T(1024)S(1)} %get-tuple-element.245), kind=kCustom, calls=%fused_computation.1.clone | custom fusion | bytes 12288 | tf_op jit(solution)/shard_map/jit(_take)/gather | solution.py:137
  76.5 8.3 %copy.29 = f32[6,32,1024]{0,2,1:T(8,128)} copy(f32[6,32,1024]{2,0,1:T(8,128)S(1)} %bitcast.72) | data formatting | bytes 1572864 | tf_op jit(solution)/shard_map/transpose | solution.py:127
  84.8 8.6 %gather_fusion.2 = f32[1024,6]{1,0:T(8,128)S(1)} fusion(f32[6,32768]{0,1:T(8,128)} %bitcast.70, s32[1024]{0:T(1024)S(1)} %get-tuple-element.244), kind=kCustom, calls=%fused_computation.2.clone | custom fusion | bytes 53248 | tf_op jit(solution)/shard_map/jit(_take)/gather | solution.py:136
  93.3 8.6 %gather_fusion = f32[1024,6]{1,0:T(8,128)S(1)} fusion(f32[6,32768]{0,1:T(8,128)} %bitcast.71, s32[1024]{0:T(1024)S(1)} %get-tuple-element.245), kind=kCustom, calls=%fused_computation.clone | custom fusion | bytes 53248 | tf_op jit(solution)/shard_map/jit(_take)/gather | solution.py:136
  103.3 3.7 %collective-permute-start.8 = (f32[3,2,1,128]{3,2,0,1:T(1,128)S(1)}, f32[3,2,1,128]{3,2,0,1:T(1,128)S(1)}, u32[]{:S(2)}, u32[]{:S(2)}) collective-permute-start(f32[3,2,1,128]{3,2,0,1:T(1,128)S(1)} %get-tuple-element.234), channel_id=1, source_target_pairs={{0,32},{32,64},{64,96},{96,128},{128,160},{160,192},{192,224},{224... | collective-permute-start | bytes 9224 | tf_op jit(solution)/shard_map/ppermute | solution.py:28
  106.9 2.2 %collective-permute-start.9 = (f32[3,2,1,128]{3,2,0,1:T(1,128)S(1)}, f32[3,2,1,128]{3,2,0,1:T(1,128)S(1)}, u32[]{:S(2)}, u32[]{:S(2)}) collective-permute-start(f32[3,2,1,128]{3,2,0,1:T(1,128)S(1)} %get-tuple-element.235), channel_id=1, source_target_pairs={{32,0},{64,32},{96,64},{128,96},{160,128},{192,160},{224,192},{256... | collective-permute-start | bytes 9224 | tf_op jit(solution)/shard_map/ppermute | solution.py:29
  109.7 4.8 %collective-permute-done.9 = f32[3,2,1,128]{3,2,0,1:T(1,128)S(1)} collective-permute-done((f32[3,2,1,128]{3,2,0,1:T(1,128)S(1)}, f32[3,2,1,128]{3,2,0,1:T(1,128)S(1)}, u32[]{:S(2)}, u32[]{:S(2)}) %collective-permute-start.9) | collective-permute-done | bytes 3104 | tf_op jit(solution)/shard_map/ppermute | solution.py:29
  114.6 3.1 %collective-permute-start.11 = (f32[3,2,10,1]{3,2,0,1:T(8,128)S(1)}, f32[3,2,10,1]{3,2,0,1:T(8,128)S(1)}, u32[]{:S(2)}, u32[]{:S(2)}) collective-permute-start(f32[3,2,10,1]{3,2,0,1:T(8,128)S(1)} %get-tuple-element.226), channel_id=1, source_target_pairs={{1,0},{2,1},{3,2},{4,3},{5,4},{6,5},{7,6},{8,7},{9,8},{10,9},{11,1... | collective-permute-start | bytes 728 | tf_op jit(solution)/shard_map/ppermute | solution.py:29
  118.3 1.2 collective-permute-done.11
  119.5 6.0 %collective-permute-done.10 = f32[3,2,10,1]{3,2,0,1:T(8,128)S(1)} collective-permute-done((f32[3,2,10,1]{3,2,0,1:T(8,128)S(1)}, f32[3,2,10,1]{3,2,0,1:T(8,128)S(1)}, u32[]{:S(2)}, u32[]{:S(2)}) %collective-permute-start.10) | collective-permute-done | bytes 272 | tf_op jit(solution)/shard_map/ppermute | solution.py:28
  (95 shorter events, 8.7 us)
Async XLA Ops:
  0.6 59.9 %copy-start = (f32[24,24]{1,0:T(8,128)S(1)}, f32[24,24]{1,0:T(8,128)}, u32[]{:S(2)}) copy-start(f32[24,24]{1,0:T(8,128)} %param.54) | copy-start | bytes 6916
  1.4 41.2 %collective-permute-start.4 = (f32[2,1,128]{2,1,0:T(1,128)S(1)}, f32[2,1,128]{2,1,0:T(1,128)S(1)}, u32[]{:S(2)}, u32[]{:S(2)}) collective-permute-start(f32[2,1,128]{2,1,0:T(1,128)S(1)} %get-tuple-element.246), channel_id=1, source_target_pairs={{0,32},{32,64},{64,96},{96,128},{128,160},{160,192},{192,224},{224... | collective-permute-start | bytes 3080 | tf_op jit(solution)/shard_map/ppermute | solution.py:28
  4.8 37.8 %collective-permute-start.5 = (f32[2,1,128]{2,1,0:T(1,128)S(1)}, f32[2,1,128]{2,1,0:T(1,128)S(1)}, u32[]{:S(2)}, u32[]{:S(2)}) collective-permute-start(f32[2,1,128]{2,1,0:T(1,128)S(1)} %get-tuple-element.247), channel_id=1, source_target_pairs={{32,0},{64,32},{96,64},{128,96},{160,128},{192,160},{224,192},{256... | collective-permute-start | bytes 3080 | tf_op jit(solution)/shard_map/ppermute | solution.py:29
  8.1 42.7 %collective-permute-start = (f32[3,2,1,128]{3,2,1,0:T(1,128)S(1)}, f32[3,2,1,128]{3,2,1,0:T(1,128)S(1)}, u32[]{:S(2)}, u32[]{:S(2)}) collective-permute-start(f32[3,2,1,128]{3,2,1,0:T(1,128)S(1)} %get-tuple-element.236), channel_id=1, source_target_pairs={{0,32},{32,64},{64,96},{96,128},{128,160},{160,192},{192,224},{224... | collective-permute-start | bytes 9224 | tf_op jit(solution)/shard_map/ppermute | solution.py:28
  13.6 37.2 %collective-permute-start.1 = (f32[3,2,1,128]{3,2,1,0:T(1,128)S(1)}, f32[3,2,1,128]{3,2,1,0:T(1,128)S(1)}, u32[]{:S(2)}, u32[]{:S(2)}) collective-permute-start(f32[3,2,1,128]{3,2,1,0:T(1,128)S(1)} %get-tuple-element.237), channel_id=1, source_target_pairs={{32,0},{64,32},{96,64},{128,96},{160,128},{192,160},{224,192},{256... | collective-permute-start | bytes 9224 | tf_op jit(solution)/shard_map/ppermute | solution.py:29
  17.7 43.9 %all-to-all-start = ((f32[32,1,1,7168]{3,2,1,0:T(1,128)}), f32[32,1,1,7168]{3,2,1,0:T(1,128)S(1)}, u32[]{:S(2)}, u32[]{:S(2)}) async-start(f32[32,1,1,7168]{3,2,1,0:T(1,128)} %broadcast_in_dim.24), calls=%async_computation | async-start | bytes 1835008 | tf_op jit(solution)/shard_map/all_to_all | solution.py:42
  43.4 6.5 %collective-permute-start.6 = (f32[2,10,1]{2,1,0:T(8,128)S(1)}, f32[2,10,1]{2,1,0:T(8,128)S(1)}, u32[]{:S(2)}, u32[]{:S(2)}) collective-permute-start(f32[2,10,1]{2,1,0:T(8,128)S(1)} %get-tuple-element.238), channel_id=1, source_target_pairs={{0,1},{1,2},{2,3},{3,4},{4,5},{5,6},{6,7},{7,8},{8,9},{9,10},{10,1... | collective-permute-start | bytes 248 | tf_op jit(solution)/shard_map/ppermute | solution.py:28
  43.4 6.5 %collective-permute-start.7 = (f32[2,10,1]{2,1,0:T(8,128)S(1)}, f32[2,10,1]{2,1,0:T(8,128)S(1)}, u32[]{:S(2)}, u32[]{:S(2)}) collective-permute-start(f32[2,10,1]{2,1,0:T(8,128)S(1)} %get-tuple-element.239), channel_id=1, source_target_pairs={{1,0},{2,1},{3,2},{4,3},{5,4},{6,5},{7,6},{8,7},{9,8},{10,9},{11,1... | collective-permute-start | bytes 248 | tf_op jit(solution)/shard_map/ppermute | solution.py:29
  51.6 4.7 %collective-permute-start.3 = (f32[3,2,10,1]{3,2,1,0:T(8,128)S(1)}, f32[3,2,10,1]{3,2,1,0:T(8,128)S(1)}, u32[]{:S(2)}, u32[]{:S(2)}) collective-permute-start(f32[3,2,10,1]{3,2,1,0:T(8,128)S(1)} %get-tuple-element.228), channel_id=1, source_target_pairs={{1,0},{2,1},{3,2},{4,3},{5,4},{6,5},{7,6},{8,7},{9,8},{10,9},{11,1... | collective-permute-start | bytes 728 | tf_op jit(solution)/shard_map/ppermute | solution.py:29
  54.6 4.7 %collective-permute-start.2 = (f32[3,2,10,1]{3,2,1,0:T(8,128)S(1)}, f32[3,2,10,1]{3,2,1,0:T(8,128)S(1)}, u32[]{:S(2)}, u32[]{:S(2)}) collective-permute-start(f32[3,2,10,1]{3,2,1,0:T(8,128)S(1)} %get-tuple-element.229), channel_id=1, source_target_pairs={{0,1},{1,2},{2,3},{3,4},{4,5},{5,6},{6,7},{7,8},{8,9},{9,10},{10,1... | collective-permute-start | bytes 728 | tf_op jit(solution)/shard_map/ppermute | solution.py:28
  63.7 39.5 %copy-start.1 = (f32[3,2,8,128]{3,2,1,0:T(8,128)S(1)}, f32[3,2,8,128]{3,2,1,0:T(8,128)}, u32[]{:S(2)}) copy-start(f32[3,2,8,128]{3,2,1,0:T(8,128)} %param.50) | copy-start | bytes 73732
  63.7 39.5 %copy-start.2 = (f32[3,2,8,128]{3,2,1,0:T(8,128)S(1)}, f32[3,2,8,128]{3,2,1,0:T(8,128)}, u32[]{:S(2)}) copy-start(f32[3,2,8,128]{3,2,1,0:T(8,128)} %param.51) | copy-start | bytes 73732
  63.7 39.5 %copy-start.4 = (f32[2,8,128]{2,1,0:T(8,128)S(1)}, f32[2,8,128]{2,1,0:T(8,128)}, u32[]{:S(2)}) copy-start(f32[2,8,128]{2,1,0:T(8,128)} %param.52) | copy-start | bytes 24580
  63.7 39.5 %copy-start.3 = (f32[3,8,128]{2,1,0:T(8,128)S(1)}, f32[3,8,128]{2,1,0:T(8,128)}, u32[]{:S(2)}) copy-start(f32[3,8,128]{2,1,0:T(8,128)} %param.55) | copy-start | bytes 36868
  103.3 6.5 %collective-permute-start.8 = (f32[3,2,1,128]{3,2,0,1:T(1,128)S(1)}, f32[3,2,1,128]{3,2,0,1:T(1,128)S(1)}, u32[]{:S(2)}, u32[]{:S(2)}) collective-permute-start(f32[3,2,1,128]{3,2,0,1:T(1,128)S(1)} %get-tuple-element.234), channel_id=1, source_target_pairs={{0,32},{32,64},{64,96},{96,128},{128,160},{160,192},{192,224},{224... | collective-permute-start | bytes 9224 | tf_op jit(solution)/shard_map/ppermute | solution.py:28
  106.9 7.6 %collective-permute-start.9 = (f32[3,2,1,128]{3,2,0,1:T(1,128)S(1)}, f32[3,2,1,128]{3,2,0,1:T(1,128)S(1)}, u32[]{:S(2)}, u32[]{:S(2)}) collective-permute-start(f32[3,2,1,128]{3,2,0,1:T(1,128)S(1)} %get-tuple-element.235), channel_id=1, source_target_pairs={{32,0},{64,32},{96,64},{128,96},{160,128},{192,160},{224,192},{256... | collective-permute-start | bytes 9224 | tf_op jit(solution)/shard_map/ppermute | solution.py:29
  114.6 4.9 %collective-permute-start.11 = (f32[3,2,10,1]{3,2,0,1:T(8,128)S(1)}, f32[3,2,10,1]{3,2,0,1:T(8,128)S(1)}, u32[]{:S(2)}, u32[]{:S(2)}) collective-permute-start(f32[3,2,10,1]{3,2,0,1:T(8,128)S(1)} %get-tuple-element.226), channel_id=1, source_target_pairs={{1,0},{2,1},{3,2},{4,3},{5,4},{6,5},{7,6},{8,7},{9,8},{10,9},{11,1... | collective-permute-start | bytes 728 | tf_op jit(solution)/shard_map/ppermute | solution.py:29
  117.8 7.8 %collective-permute-start.10 = (f32[3,2,10,1]{3,2,0,1:T(8,128)S(1)}, f32[3,2,10,1]{3,2,0,1:T(8,128)S(1)}, u32[]{:S(2)}, u32[]{:S(2)}) collective-permute-start(f32[3,2,10,1]{3,2,0,1:T(8,128)S(1)} %get-tuple-element.227), channel_id=1, source_target_pairs={{0,1},{1,2},{2,3},{3,4},{4,5},{5,6},{6,7},{7,8},{8,9},{9,10},{10,1... | collective-permute-start | bytes 728 | tf_op jit(solution)/shard_map/ppermute | solution.py:28
where the time goes:
time: 129 us; the launch traced here: 128 us
  starting transfers between devices  51.9 us (40%)
  local copies, waits for them, and re-layouts  46.6 us (36%)
  waiting for transfers between devices  18.2 us (14%)
  other arithmetic  9.94 us (8%)
    all_to_all x1, starting transfers between devices, sent_to_all(): return lax.all_to_all(copies, axis, split_axis=0, concat_axis=0, tiled=True)  21.7 us
    ppermute x6, starting transfers between devices, with_halo(): after = lax.ppermute(leading, axis, down)  17.7 us
    gather x2, local copies, waits for them, and re-layouts, shards(): facet_rows = jnp.take(wide_table, lookup, axis=1)  17.1 us
    ppermute x6, starting transfers between devices, with_halo(): before = lax.ppermute(last, axis, up)  12.6 us
    gather x2, local copies, waits for them, and re-layouts, shards(): jnp.take(wide_stiff, lookup)  12.3 us
    ppermute x6, waiting for transfers between devices, with_halo(): before = lax.ppermute(last, axis, up)  10.4 us
    transpose x1, local copies, waits for them, and re-layouts, shards(): wide_table = every_table[:, 0].transpose(1, 0, 2).reshape(6, -1)  8.27 us
    ppermute x6, waiting for transfers between devices, with_halo(): after = lax.ppermute(leading, axis, down)  7.77 us
  transfers between devices with their start and end apart: 13, of which 6 were waited for; matrix products, arithmetic and copies ran while one was open for 9% of the time, Pallas kernels for 0%

commit v1 on v0

v1 whole, which is shorter than its diff:
```python
import jax
import jax.numpy as jnp
from jax import lax
from jax.experimental import pallas as pl
from jax.experimental.pallas import tpu as pltpu
from jax.sharding import PartitionSpec as P

DT = 0.1
F32 = jnp.float32
VMEM = pl.BlockSpec(memory_space=pltpu.VMEM)
SMEM = pl.BlockSpec(memory_space=pltpu.SMEM)
ROWS = 8
COLS = 128
OWNERS = 32
AT_U, AT_E, AT_V, AT_M, AT_X, AT_P, AT_O = 0, 12, 16, 22, 24, 27, 28
MSG = 32


def struct(*shape, dtype=F32):
    return jax.ShapeDtypeStruct(shape, dtype)


def lanes(shape):
    return lax.broadcasted_iota(jnp.int32, shape, len(shape) - 1)


def pack_kernel(u, v, mass, mod, ref, fac, pen, own, pair, table, up, down):
    root = jnp.sqrt(pen[...])
    n = [fac[3 + m : 4 + m, :] for m in range(3)]
    c = [fac[m : m + 1, :] for m in range(3)]
    dist = n[0] * c[0] + n[1] * c[1] + n[2] * c[2]
    rows = [root * n[0], root * n[1], root * n[2], root * dist]
    half = fac.shape[1] // 2
    mine = jnp.concatenate([r[:, :half] for r in rows] + [r[:, half:] for r in rows], axis=0)
    for o in range(OWNERS):
        table[o] = mine
    for out, two, one in ((down, ROWS - 2, ROWS - 1), (up, 0, 0)):
        for m in range(3):
            for k in range(2):
                ch = 2 * m + k
                out[AT_U + 2 * ch : AT_U + 2 * ch + 2, :] = u[m, k, two : two + 2, :]
                out[AT_V + ch : AT_V + ch + 1, :] = v[m, k, one : one + 1, :]
            out[AT_X + m : AT_X + m + 1, :] = ref[m, one : one + 1, :]
        for k in range(2):
            out[AT_E + 2 * k : AT_E + 2 * k + 2, :] = mod[k, two : two + 2, :]
            out[AT_M + k : AT_M + k + 1, :] = mass[k, one : one + 1, :]
        out[AT_P : AT_P + 1, :] = pair[0, one : one + 1, :].astype(F32)
        out[AT_O : AT_O + 1, :] = jnp.full((1, COLS), own[0, 0, 0, one, 0]).astype(F32)
        out[AT_O + 1 :, :] = jnp.zeros((MSG - AT_O - 1, COLS), F32)


def extend_kernel(u, mod, above, below, ext, left, right):
    for ch in range(8):
        at = AT_U + 2 * ch if ch < 6 else AT_E + 2 * (ch - 6)
        own = u[ch // 2, ch % 2] if ch < 6 else mod[ch - 6]
        ext[16 * ch : 16 * ch + 2, :] = above[at : at + 2, :]
        ext[16 * ch + 2 : 16 * ch + 10, :] = own
        ext[16 * ch + 10 : 16 * ch + 12, :] = below[at : at + 2, :]
        ext[16 * ch + 12 : 16 * ch + 16, :] = jnp.zeros((4, COLS), F32)
    turned = jnp.transpose(ext[...])
    left[...] = turned[0:1, :]
    right[...] = turned[COLS - 1 : COLS, :]


def edge_columns(from_left, from_right):
    sub = lax.broadcasted_iota(jnp.int32, (128, COLS), 0)
    both = jnp.where(sub < 64, jnp.broadcast_to(from_left, (128, COLS)), jnp.broadcast_to(from_right, (128, COLS)))
    return jnp.transpose(both)


def with_columns(here, edges):
    lane = lanes(here.shape)
    return jnp.where(lane == COLS - 1, edges, pltpu.roll(here, COLS - 1, axis=1))


def internal_tile(stiff, at_left, at_right, at_edge, scale, at, scale_at):
    lane0 = lanes((ROWS, COLS)) == 0
    straight, moved, edge = {}, {}, {}
    for i in range(2):
        start = at + 1 - i
        rows = [pl.ds(start + x, ROWS) for x in range(2)]
        lefts = [at_left[ch, rows[x], :] for ch in range(6) for x in range(2)]
        rights = [at_right[ch, rows[x], :] for ch in range(6) for x in range(2)]
        edges = [at_edge[ch, rows[x], :] for ch in range(6) for x in range(2)]
        s_main = scale[0, pl.ds(start + scale_at, ROWS), :]
        s_edge = scale[1, pl.ds(start + scale_at, ROWS), :]
        for k in range(2):
            for m in range(3):
                for e in range(2):
                    row = 3 * (4 * k + 2 * i + e) + m
                    main = side = None
                    for kk in range(2):
                        for x in range(2):
                            for ee in range(2):
                                for mm in range(3):
                                    w = stiff[row, 3 * (4 * kk + 2 * x + ee) + mm]
                                    j = 2 * (2 * mm + kk) + x
                                    t = w * (rights if ee else lefts)[j]
                                    main = t if main is None else main + t
                                    if e:
                                        t = w * (lefts if ee else edges)[j]
                                        side = t if side is None else side + t
                    into = moved if e else straight
                    ch = 2 * m + k
                    main = main * s_main
                    into[ch] = main if i == 0 else into[ch] + main
                    if e:
                        side = side * s_edge
                        edge[ch] = side if i == 0 else edge[ch] + side
    return [straight[ch] + jnp.where(lane0, edge[ch], pltpu.roll(moved[ch], 1, axis=1)) for ch in range(6)]


def first_kernel(stiff, ext, from_left, from_right, above, below, v, mass, ref, pair, vel, dis, weight, point, index, scale, at_left, at_right, at_edge):
    edges = edge_columns(from_left[...], from_right[...])
    zero = jnp.zeros((8, COLS), F32)
    for ch in range(6):
        here, side = ext[16 * ch : 16 * ch + 16, :], edges[16 * ch : 16 * ch + 16, :]
        at_left[ch, 0:16, :] = here
        at_right[ch, 0:16, :] = with_columns(here, side)
        at_edge[ch, 0:16, :] = side
        for buf in (at_left, at_right, at_edge):
            buf[ch, 16:24, :] = zero
    here = ext[96:112, :] + ext[112:128, :]
    side = edges[96:112, :] + edges[112:128, :]
    right = with_columns(here, side)
    for n, both in enumerate((here + right, side + here)):
        scale[n, 0:16, :] = (both + pltpu.roll(both, 15, axis=0)) * 0.125
        scale[n, 16:24, :] = zero
    for k in range(2):
        weight[k, 0:1, :] = above[AT_M + k : AT_M + k + 1, :]
        weight[k, 1:9, :] = mass[k]
        weight[k, 9:10, :] = below[AT_M + k : AT_M + k + 1, :]
        weight[k, 10:16, :] = jnp.ones((6, COLS), F32)
        weight[k] = DT / weight[k]
    for ch in range(6):
        vel[ch, 0:1, :] = above[AT_V + ch : AT_V + ch + 1, :]
        vel[ch, 1:9, :] = v[ch // 2, ch % 2]
        vel[ch, 9:10, :] = below[AT_V + ch : AT_V + ch + 1, :]
        vel[ch, 10:16, :] = zero[:6]
    for m in range(3):
        point[m, 0:1, :] = above[AT_X + m : AT_X + m + 1, :]
        point[m, 1:9, :] = ref[m]
        point[m, 9:10, :] = below[AT_X + m : AT_X + m + 1, :]
        point[m, 10:16, :] = zero[:6]
        point[m] = point[m] + at_left[2 * m, 1:17, :]
    index[0:1, :] = above[AT_P : AT_P + 1, :].astype(jnp.int32)
    index[1:9, :] = pair[0]
    index[9:10, :] = below[AT_P : AT_P + 1, :].astype(jnp.int32)
    index[10:16, :] = jnp.zeros((6, COLS), jnp.int32)
    for at in (0, 8):
        forces = internal_tile(stiff, at_left, at_right, at_edge, scale, at, 0)
        for ch in range(6):
            new = vel[ch, at : at + 8, :] - weight[ch % 2, at : at + 8, :] * forces[ch]
            vel[ch, at : at + 8, :] = new
            dis[ch, at : at + 8, :] = at_left[ch, at + 1 : at + 9, :] + DT * new


def look_up(table, owner, index, row, out):
    which = jnp.broadcast_to(index, (8, COLS))
    place, part = which & 127, (which >> 7) & 3
    found = None
    for c in range(4):
        got = jnp.take_along_axis(table[owner, :, c * COLS : (c + 1) * COLS], place, axis=1)
        found = got if found is None else jnp.where(part == c, got, found)
    found = jnp.where(which[0:4] >= 512, found[4:8], found[0:4])
    for c in range(4):
        out[c, row : row + 1, :] = found[c : c + 1]


def contact(words, points):
    depth = jnp.maximum(words[3] - (words[0] * points[0] + words[1] * points[1] + words[2] * points[2]), 0.0)
    return [words[m] * depth for m in range(3)]


def contact_kernel(owner, table, index, pair, vel, dis, weight, point, ref, new_vel, new_dis, push, left, right, words, square):
    words[:, 8:16, :] = jnp.zeros((4, 8, COLS), F32)
    for b in range(ROWS + 2):
        look_up(table, owner[b], index[b : b + 1, :], b, words)
    pushes = contact([words[c] for c in range(4)], [point[m] for m in range(3)])
    for m in range(3):
        step = weight[0] * pushes[m]
        new_vel[2 * m] = (vel[2 * m] + step)[1:9]
        new_vel[2 * m + 1] = vel[2 * m + 1, 1:9, :]
        new_dis[2 * m] = dis[2 * m] + DT * step
        new_dis[2 * m + 1] = dis[2 * m + 1]
    for ch in range(6):
        square[16 * ch : 16 * ch + 16, :] = new_dis[ch]
    square[96:128, :] = jnp.zeros((32, COLS), F32)
    turned = jnp.transpose(square[...])
    left[...] = turned[0:1, :]
    right[...] = turned[COLS - 1 : COLS, :]
    for b in range(ROWS):
        look_up(table, owner[ROWS + 2 + b], pair[1, b : b + 1, :], b, words)
    pushes = contact([words[c, 0:8, :] for c in range(4)], [ref[m] + new_dis[2 * m, 1:9, :] for m in range(3)])
    for m in range(3):
        push[m] = pushes[m]


def second_kernel(stiff, dis, vel, push, mass, scale, from_left, from_right, out_dis, out_vel, at_left, at_right, at_edge):
    edges = edge_columns(from_left[...], from_right[...])
    for ch in range(6):
        here, side = dis[ch], edges[16 * ch : 16 * ch + 16, :]
        at_left[ch, 0:16, :] = here
        at_right[ch, 0:16, :] = with_columns(here, side)
        at_edge[ch, 0:16, :] = side
    forces = internal_tile(stiff, at_left, at_right, at_edge, scale, 0, 1)
    for m in range(3):
        for k in range(2):
            ch = 2 * m + k
            net = push[m] - forces[ch] if k == 0 else -forces[ch]
            new = vel[ch] + DT * net / mass[k]
            out_vel[m, k] = new
            out_dis[m, k] = at_left[ch, 1:9, :] + DT * new


def call(kernel, outs, specs, scratch=()):
    return pl.pallas_call(
        kernel,
        out_shape=outs,
        in_specs=specs,
        out_specs=jax.tree.map(lambda _: VMEM, outs),
        scratch_shapes=list(scratch),
        compiler_params=pltpu.CompilerParams(vmem_limit_bytes=16 * 1024 * 1024),
    )


def swapped(to_next, to_last, axis):
    size = lax.axis_size(axis)
    up = [(i, (i + 1) % size) for i in range(size)]
    down = [(j, i) for i, j in up]
    return lax.ppermute(to_next, axis, up), lax.ppermute(to_last, axis, down)


def shards(u, v, mass, mod, stiff, ref, facets, penalty, owners, pair):
    width = facets.shape[-1]
    buffers = [pltpu.VMEM((6, 24, COLS), F32)] * 3
    table, up, down = call(
        pack_kernel,
        (struct(OWNERS, 8, width // 2), struct(MSG, COLS), struct(MSG, COLS)),
        [VMEM] * 7 + [SMEM, VMEM],
    )(u, v, mass, mod, ref, facets.reshape(6, width), penalty.reshape(1, width), owners, pair)
    tables = lax.all_to_all(table, "mesh", split_axis=0, concat_axis=0, tiled=True)
    above, below = swapped(down, up, "mesh")
    ext, left, right = call(
        extend_kernel, (struct(128, COLS), struct(1, COLS), struct(1, COLS)), [VMEM] * 4
    )(u, mod, above, below)
    from_left, from_right = swapped(right, left, "sub")
    vel, dis, weight, point, index, scale = call(
        first_kernel,
        (
            struct(6, 16, COLS),
            struct(6, 16, COLS),
            struct(2, 16, COLS),
            struct(3, 16, COLS),
            struct(16, COLS, dtype=jnp.int32),
            struct(2, 24, COLS),
        ),
        [SMEM] + [VMEM] * 9,
        buffers,
    )(stiff, ext, from_left, from_right, above, below, v, mass, ref, pair)
    mine = owners.reshape(2, ROWS)
    outer = [side[AT_O, :1].astype(jnp.int32) for side in (above, below)]
    owner = jnp.concatenate([outer[0], mine[0], outer[1], mine[1]])
    new_vel, new_dis, push, left, right = call(
        contact_kernel,
        (
            struct(6, ROWS, COLS),
            struct(6, 16, COLS),
            struct(3, ROWS, COLS),
            struct(1, COLS),
            struct(1, COLS),
        ),
        [SMEM] + [VMEM] * 8,
        [pltpu.VMEM((4, 16, COLS), F32), pltpu.VMEM((128, COLS), F32)],
    )(owner, tables, index, pair, vel, dis, weight, point, ref)
    from_left, from_right = swapped(right, left, "sub")
    return call(
        second_kernel,
        (struct(3, 2, ROWS, COLS), struct(3, 2, ROWS, COLS)),
        [SMEM] + [VMEM] * 7,
        buffers,
    )(stiff, new_dis, new_vel, push, mass, scale, from_left, from_right)


def solution(mesh):
    in_specs = (
        P(None, None, "mesh", "sub"),
        P(None, None, "mesh", "sub"),
        P(None, "mesh", "sub"),
        P(None, "mesh", "sub"),
        P(),
        P(None, "mesh", "sub"),
        P("mesh", "sub", None, None),
        P("mesh", "sub", None),
        P(None, "mesh", "sub", None, None),
        P(None, "mesh", "sub"),
    )
    out_specs = (P(None, None, "mesh", "sub"), P(None, None, "mesh", "sub"))
    return jax.shard_map(shards, mesh=mesh, in_specs=in_specs, out_specs=out_specs, check_vma=False)
```

time: 129 us -> 57.8 us (0.45)
  the two profiles are of different devices: /device:TPU:14 before, /device:TPU:30 now
where the time goes in v1:
time: 57.8 us; the launch traced here: 57.2 us
  starting transfers between devices  41 us (71%)
  Pallas kernels  5.89 us (10%)
  local copies, waits for them, and re-layouts  4.68 us (8%)
  waiting for transfers between devices  3.46 us (6%)
  between operations  2.11 us (4%)
    ppermute x6, starting transfers between devices, swapped(): return (lax.ppermute(to_next, axis, up), lax.ppermute(to_last, axis, down))  24.5 us
    all_to_all x1, starting transfers between devices, shards(): lax.all_to_all(table, 'mesh', split_axis=0, concat_axis=0, tiled=True)  16.6 us
    unnamed x24, local copies, waits for them, and re-layouts  3.65 us
    ppermute x6, waiting for transfers between devices, swapped(): return (lax.ppermute(to_next, axis, up), lax.ppermute(to_last, axis, down))  3.45 us
    pallas_call x1, Pallas kernels, shards(): call(second_kernel, (struct(3, 2, ROWS, COLS), struct(3, 2, ROWS, COLS)),...  1.8 us
    pallas_call x1, Pallas kernels, shards(): call(first_kernel, (struct(6, 16, COLS), struct(6, 16, COLS), struct(2, 1...  1.62 us
    pallas_call x1, Pallas kernels, shards(): call(pack_kernel, (struct(OWNERS, 8, width // 2), struct(MSG, COLS), stru...  1.55 us
  transfers between devices with their start and end apart: 7, of which 5 were waited for; matrix products, arithmetic and copies ran while one was open for 2% of the time, Pallas kernels for 3%

profile of v1, /device:TPU:30, one launch (start us, length us, event | category | flops | bytes accessed | tf_op | source)
XLA Modules:
  0.0 57.2 jit_solution(14246978539810941479)
XLA Ops:
  0.7 0.8 %copy.15 = f32[1,1,6,1024]{3,2,1,0:T(8,128)S(1)} copy(f32[1,1,6,1024]{3,1,2,0:T(1,128)} %param.16) | data formatting | bytes 49152
  1.4 0.8 %copy.12.own = s32[2,1,1,8,1]{4,3,2,1,0:T(8,128)S(1)} copy(s32[2,1,1,8,1]{3,4,2,1,0:T(1,128)} %param.18) | data formatting | bytes 128 | tf_op args[8]
  2.2 0.0 copy-done.2
  2.2 0.0 copy-start.4
  2.2 0.7 %copy-done.4 = f32[2,8,128]{2,1,0:T(8,128)S(1)} copy-done((f32[2,8,128]{2,1,0:T(8,128)S(1)}, f32[2,8,128]{2,1,0:T(8,128)}, u32[]{:S(2)}) %copy-start.4) | copy-done | bytes 8216
  2.9 0.7 %copy-done.7 = f32[2,8,128]{2,1,0:T(8,128)S(1)} copy-done((f32[2,8,128]{2,1,0:T(8,128)S(1)}, f32[2,8,128]{2,1,0:T(8,128)}, u32[]{:S(2)}) %copy-start.7) | copy-done | bytes 8216
  3.6 0.7 %copy-done.9 = f32[1,1,1024]{2,1,0:T(1,128)S(1)} copy-done((f32[1,1,1024]{2,1,0:T(1,128)S(1)}, f32[1,1,1024]{2,1,0:T(1,128)}, u32[]{:S(2)}) %copy-start.9) | copy-done | bytes 4120
  4.3 1.6 %shard_map.113 = (f32[32,8,512]{2,1,0:T(8,128)}, f32[32,128]{1,0:T(8,128)S(1)}, f32[32,128]{1,0:T(8,128)S(1)}) custom-call(f32[3,2,8,128]{3,2,1,0:T(8,128)S(1)} %copy-done.2, f32[3,2,8,128]{3,2,1,0:T(8,128)S(1)} %copy-done.1, f32[2,8,128]{2,1,0:T(8,128)S(1)} %copy-done.4, f32[2,8,128]{2,1,0:T(8,128)S(1)} %copy-done.7, f32[3,8,128]{2,1,0:T(8,128)S(1)} %copy-done, ...), custom_call_target="tpu_custom_call" | custom-call | tf_op jit(solution)/shard_map/pallas_call | solution.py:237
  5.9 16.6 %all-to-all-start = ((f32[32,8,512]{2,1,0:T(8,128)}), f32[32,8,512]{2,1,0:T(8,128)S(1)}, u32[]{:S(2)}, u32[]{:S(2)}) async-start(f32[32,8,512]{2,1,0:T(8,128)} %get-tuple-element.21), calls=%async_computation | async-start | bytes 1048576 | tf_op jit(solution)/shard_map/all_to_all | solution.py:242
  22.4 0.0 copy-start.8
  22.4 2.8 %collective-permute-start.1 = (f32[32,128]{1,0:T(8,128)S(1)}, f32[32,128]{1,0:T(8,128)S(1)}, u32[]{:S(2)}, u32[]{:S(2)}) collective-permute-start(f32[32,128]{1,0:T(8,128)S(1)} %get-tuple-element.20), channel_id=1, source_target_pairs={{32,0},{64,32},{96,64},{128,96},{160,128},{192,160},{224,192},{256... | collective-permute-start | bytes 49160 | tf_op jit(solution)/shard_map/ppermute | solution.py:231
  25.2 6.4 %collective-permute-start = (f32[32,128]{1,0:T(8,128)S(1)}, f32[32,128]{1,0:T(8,128)S(1)}, u32[]{:S(2)}, u32[]{:S(2)}) collective-permute-start(f32[32,128]{1,0:T(8,128)S(1)} %get-tuple-element.19), channel_id=1, source_target_pairs={{0,32},{32,64},{64,96},{96,128},{128,160},{160,192},{192,224},{224... | collective-permute-start | bytes 49160 | tf_op jit(solution)/shard_map/ppermute | solution.py:231
  31.6 0.9 %collective-permute-done.1.below = f32[32,128]{1,0:T(8,128)S(1)} collective-permute-done((f32[32,128]{1,0:T(8,128)S(1)}, f32[32,128]{1,0:T(8,128)S(1)}, u32[]{:S(2)}, u32[]{:S(2)}) %collective-permute-start.1) | collective-permute-done | bytes 16416 | tf_op jit(solution)/shard_map/ppermute | solution.py:231
  32.6 0.5 slice.19
  33.7 0.0 collective-permute-done.above
  33.7 0.5 slice.18
  34.9 0.0 copy-start.6
  34.9 0.1 shard_map.114
  35.0 0.0 copy-start.5
  35.0 0.0 collective-permute-start.2
  35.1 12.3 %collective-permute-start.3 = (f32[1,128]{1,0:T(1,128)S(1)}, f32[1,128]{1,0:T(1,128)S(1)}, u32[]{:S(2)}, u32[]{:S(2)}) collective-permute-start(f32[1,128]{1,0:T(1,128)S(1)} %get-tuple-element.24), channel_id=1, source_target_pairs={{1,0},{2,1},{3,2},{4,3},{5,4},{6,5},{7,6},{8,7},{9,8},{10,9},{11,1... | collective-permute-start | bytes 1544 | tf_op jit(solution)/shard_map/ppermute | solution.py:231
  47.4 0.1 pad_add_fusion.owner
  47.5 1.1 %collective-permute-done.2.from_left = f32[1,128]{1,0:T(1,128)S(1)} collective-permute-done((f32[1,128]{1,0:T(1,128)S(1)}, f32[1,128]{1,0:T(1,128)S(1)}, u32[]{:S(2)}, u32[]{:S(2)}) %collective-permute-start.2) | collective-permute-done | bytes 544 | tf_op jit(solution)/shard_map/ppermute | solution.py:231
  48.6 0.1 collective-permute-done.3.from_right
  48.7 1.6 %shard_map.115 = (f32[6,16,128]{2,1,0:T(8,128)S(1)}, f32[6,16,128]{2,1,0:T(8,128)S(1)}, f32[2,16,128]{2,1,0:T(8,128)S(1)}, f32[3,16,128]{2,1,0:T(8,128)S(1)}, s3...) custom-call(f32[24,24]{1,0:T(8,128)S(1)} %copy-done.6, f32[128,128]{1,0:T(8,128)S(1)} %get-tuple-element.22.ext, ...), custom_call_target="tpu_custom_call" | custom-call | tf_op jit(solution)/shard_map/pallas_call | solution.py:248
  50.3 0.0 all-to-all-done.table
  50.3 0.8 %shard_map.116 = (f32[6,8,128]{2,1,0:T(8,128)S(1)}, f32[6,16,128]{2,1,0:T(8,128)S(1)}, f32[3,8,128]{2,1,0:T(8,128)S(1)}, f32[1,128]{1,0:T(1,128)S(1)}, f32[1,128]{1,0:T(1,128)S(1)}) custom-call(s32[18]{0:T(128)S(1)} %pad_add_fusion.owner, f32[32,8,512]{2,1,0:T(8,128)S(1)} %all-to-all-done.table, s32[16,128]{1,0:T(8,128)S(1)} %get-tuple-element.25.index, ...), custom_call_target="tpu_custom_call" | custom-call | tf_op jit(solution)/shard_map/pallas_call | solution.py:264
  51.2 0.0 collective-permute-start.4
  51.2 2.9 %collective-permute-start.5 = (f32[1,128]{1,0:T(1,128)S(1)}, f32[1,128]{1,0:T(1,128)S(1)}, u32[]{:S(2)}, u32[]{:S(2)}) collective-permute-start(f32[1,128]{1,0:T(1,128)S(1)} %get-tuple-element.35), channel_id=1, source_target_pairs={{1,0},{2,1},{3,2},{4,3},{5,4},{6,5},{7,6},{8,7},{9,8},{10,9},{11,1... | collective-permute-start | bytes 1544 | tf_op jit(solution)/shard_map/ppermute | solution.py:231
  54.1 1.2 %collective-permute-done.4.from_left = f32[1,128]{1,0:T(1,128)S(1)} collective-permute-done((f32[1,128]{1,0:T(1,128)S(1)}, f32[1,128]{1,0:T(1,128)S(1)}, u32[]{:S(2)}, u32[]{:S(2)}) %collective-permute-start.4) | collective-permute-done | bytes 544 | tf_op jit(solution)/shard_map/ppermute | solution.py:231
  55.4 0.1 collective-permute-done.5.from_right
  55.4 1.8 %shard_map.117 = (f32[3,2,8,128]{3,2,1,0:T(8,128)}, f32[3,2,8,128]{3,2,1,0:T(8,128)}) custom-call(f32[24,24]{1,0:T(8,128)S(1)} %copy-done.6, f32[6,16,128]{2,1,0:T(8,128)S(1)} %get-tuple-element.30.dis, f32[6,8,128]{2,1,0:T(8,128)S(1)} %get-tuple-element.31.vel, f32[3,8,128]{2,1,0:T(8,128)S(1)} %get-tuple-element.32.push, f32[2,8,128]{2,1,0:T(8,128)S(1)} %copy-done.5, ...), custom_call_target="tpu_custom_call" | custom-call | tf_op jit(solution)/shard_map/pallas_call | solution.py:277
  (15 shorter events, 0.0 us)
Async XLA Ops:
  0.6 1.6 %copy-start.2 = (f32[3,2,8,128]{3,2,1,0:T(8,128)S(1)}, f32[3,2,8,128]{3,2,1,0:T(8,128)}, u32[]{:S(2)}) copy-start(f32[3,2,8,128]{3,2,1,0:T(8,128)} %u.3) | copy-start | bytes 73732
  0.6 1.6 %copy-start.1 = (f32[3,2,8,128]{3,2,1,0:T(8,128)S(1)}, f32[3,2,8,128]{3,2,1,0:T(8,128)}, u32[]{:S(2)}) copy-start(f32[3,2,8,128]{3,2,1,0:T(8,128)} %v.3) | copy-start | bytes 73732
  0.7 1.6 %copy-start.3 = (s32[2,8,128]{2,1,0:T(8,128)S(1)}, s32[2,8,128]{2,1,0:T(8,128)}, u32[]{:S(2)}) copy-start(s32[2,8,128]{2,1,0:T(8,128)} %pair.5) | copy-start | bytes 24580
  1.4 0.8 %copy-start = (f32[3,8,128]{2,1,0:T(8,128)S(1)}, f32[3,8,128]{2,1,0:T(8,128)}, u32[]{:S(2)}) copy-start(f32[3,8,128]{2,1,0:T(8,128)} %ref.5) | copy-start | bytes 36868
  2.2 0.7 %copy-start.4 = (f32[2,8,128]{2,1,0:T(8,128)S(1)}, f32[2,8,128]{2,1,0:T(8,128)}, u32[]{:S(2)}) copy-start(f32[2,8,128]{2,1,0:T(8,128)} %mass.5) | copy-start | bytes 24580
  2.9 0.7 %copy-start.7 = (f32[2,8,128]{2,1,0:T(8,128)S(1)}, f32[2,8,128]{2,1,0:T(8,128)}, u32[]{:S(2)}) copy-start(f32[2,8,128]{2,1,0:T(8,128)} %mod.3) | copy-start | bytes 24580
  3.6 0.7 %copy-start.9 = (f32[1,1,1024]{2,1,0:T(1,128)S(1)}, f32[1,1,1024]{2,1,0:T(1,128)}, u32[]{:S(2)}) copy-start(f32[1,1,1024]{2,1,0:T(1,128)} %param.17) | copy-start | bytes 12292
  5.9 25.8 %copy-start.10 = (s32[2,1,1,8,1]{3,4,2,1,0:T(1,128)S(1)}, s32[2,1,1,8,1]{3,4,2,1,0:T(1,128)}, u32[]{:S(2)}) copy-start(s32[2,1,1,8,1]{3,4,2,1,0:T(1,128)} %param.18) | copy-start | bytes 196
  5.9 44.5 %all-to-all-start = ((f32[32,8,512]{2,1,0:T(8,128)}), f32[32,8,512]{2,1,0:T(8,128)S(1)}, u32[]{:S(2)}, u32[]{:S(2)}) async-start(f32[32,8,512]{2,1,0:T(8,128)} %get-tuple-element.21), calls=%async_computation | async-start | bytes 1048576 | tf_op jit(solution)/shard_map/all_to_all | solution.py:242
  22.4 12.5 %copy-start.8 = (f32[2,8,128]{2,1,0:T(8,128)S(1)}, f32[2,8,128]{2,1,0:T(8,128)}, u32[]{:S(2)}) copy-start(f32[2,8,128]{2,1,0:T(8,128)} %mod.3) | copy-start | bytes 24580
  22.4 10.1 %collective-permute-start.1 = (f32[32,128]{1,0:T(8,128)S(1)}, f32[32,128]{1,0:T(8,128)S(1)}, u32[]{:S(2)}, u32[]{:S(2)}) collective-permute-start(f32[32,128]{1,0:T(8,128)S(1)} %get-tuple-element.20), channel_id=1, source_target_pairs={{32,0},{64,32},{96,64},{128,96},{160,128},{192,160},{224,192},{256... | collective-permute-start | bytes 49160 | tf_op jit(solution)/shard_map/ppermute | solution.py:231
  25.2 8.5 %collective-permute-start = (f32[32,128]{1,0:T(8,128)S(1)}, f32[32,128]{1,0:T(8,128)S(1)}, u32[]{:S(2)}, u32[]{:S(2)}) collective-permute-start(f32[32,128]{1,0:T(8,128)S(1)} %get-tuple-element.19), channel_id=1, source_target_pairs={{0,32},{32,64},{64,96},{96,128},{128,160},{160,192},{192,224},{224... | collective-permute-start | bytes 49160 | tf_op jit(solution)/shard_map/ppermute | solution.py:231
  34.9 13.8 %copy-start.6 = (f32[24,24]{1,0:T(8,128)S(1)}, f32[24,24]{1,0:T(8,128)}, u32[]{:S(2)}) copy-start(f32[24,24]{1,0:T(8,128)} %stiff.3) | copy-start | bytes 6916
  35.0 13.7 %copy-start.5 = (f32[2,8,128]{2,1,0:T(8,128)S(1)}, f32[2,8,128]{2,1,0:T(8,128)}, u32[]{:S(2)}) copy-start(f32[2,8,128]{2,1,0:T(8,128)} %mass.5) | copy-start | bytes 24580
  35.0 13.6 %collective-permute-start.2 = (f32[1,128]{1,0:T(1,128)S(1)}, f32[1,128]{1,0:T(1,128)S(1)}, u32[]{:S(2)}, u32[]{:S(2)}) collective-permute-start(f32[1,128]{1,0:T(1,128)S(1)} %get-tuple-element.23), channel_id=1, source_target_pairs={{0,1},{1,2},{2,3},{3,4},{4,5},{5,6},{6,7},{7,8},{8,9},{9,10},{10,1... | collective-permute-start | bytes 1544 | tf_op jit(solution)/shard_map/ppermute | solution.py:231
  35.1 13.6 %collective-permute-start.3 = (f32[1,128]{1,0:T(1,128)S(1)}, f32[1,128]{1,0:T(1,128)S(1)}, u32[]{:S(2)}, u32[]{:S(2)}) collective-permute-start(f32[1,128]{1,0:T(1,128)S(1)} %get-tuple-element.24), channel_id=1, source_target_pairs={{1,0},{2,1},{3,2},{4,3},{5,4},{6,5},{7,6},{8,7},{9,8},{10,9},{11,1... | collective-permute-start | bytes 1544 | tf_op jit(solution)/shard_map/ppermute | solution.py:231
  51.2 4.2 %collective-permute-start.4 = (f32[1,128]{1,0:T(1,128)S(1)}, f32[1,128]{1,0:T(1,128)S(1)}, u32[]{:S(2)}, u32[]{:S(2)}) collective-permute-start(f32[1,128]{1,0:T(1,128)S(1)} %get-tuple-element.34), channel_id=1, source_target_pairs={{0,1},{1,2},{2,3},{3,4},{4,5},{5,6},{6,7},{7,8},{8,9},{9,10},{10,1... | collective-permute-start | bytes 1544 | tf_op jit(solution)/shard_map/ppermute | solution.py:231
  51.2 4.2 %collective-permute-start.5 = (f32[1,128]{1,0:T(1,128)S(1)}, f32[1,128]{1,0:T(1,128)S(1)}, u32[]{:S(2)}, u32[]{:S(2)}) collective-permute-start(f32[1,128]{1,0:T(1,128)S(1)} %get-tuple-element.35), channel_id=1, source_target_pairs={{1,0},{2,1},{3,2},{4,3},{5,4},{6,5},{7,6},{8,7},{9,8},{10,9},{11,1... | collective-permute-start | bytes 1544 | tf_op jit(solution)/shard_map/ppermute | solution.py:231

commit v2 on v1

v2 whole, which is shorter than its diff:
```python
import jax
import jax.numpy as jnp
from jax import lax
from jax.experimental import pallas as pl
from jax.experimental.pallas import tpu as pltpu
from jax.sharding import PartitionSpec as P

DT = 0.1
F32 = jnp.float32
VMEM = pl.BlockSpec(memory_space=pltpu.VMEM)
SMEM = pl.BlockSpec(memory_space=pltpu.SMEM)
ROWS = 8
COLS = 128
OWNERS = 32
AT_U, AT_E, AT_V, AT_M, AT_X, AT_P, AT_O = 0, 12, 16, 22, 24, 27, 28
MSG = 32


def struct(*shape, dtype=F32):
    return jax.ShapeDtypeStruct(shape, dtype)


def lanes(shape):
    return lax.broadcasted_iota(jnp.int32, shape, len(shape) - 1)


def pack_kernel(u, v, mass, mod, ref, fac, pen, pair, own, table, up, down, *held):
    arrays, sems = held[:-1], held[-1]
    copies = [pltpu.make_async_copy(a, b, sems.at[n]) for n, (a, b) in enumerate(zip((u, v, mass, mod, ref, fac, pen, pair), arrays))]
    for copy in copies:
        copy.start()
    for copy in copies:
        copy.wait()
    u, v, mass, mod, ref, fac, pen, pair = arrays
    root = jnp.sqrt(pen[...])
    c, n = [[fac[8 * (m + at) : 8 * (m + at) + 8, :] for m in range(3)] for at in (0, 3)]
    dist = n[0] * c[0] + n[1] * c[1] + n[2] * c[2]
    words = [root * n[0], root * n[1], root * n[2], root * dist]
    for q in range(4):
        mine = jnp.concatenate([w[4 * h + q : 4 * h + q + 1, :] for h in range(2) for w in words], axis=0)
        for o in range(OWNERS):
            table[o, 8 * q : 8 * q + 8, :] = mine
    for out, two, one in ((down, ROWS - 2, ROWS - 1), (up, 0, 0)):
        for m in range(3):
            for k in range(2):
                ch = 2 * m + k
                out[AT_U + 2 * ch : AT_U + 2 * ch + 2, :] = u[m, k, two : two + 2, :]
                out[AT_V + ch : AT_V + ch + 1, :] = v[m, k, one : one + 1, :]
            out[AT_X + m : AT_X + m + 1, :] = ref[m, one : one + 1, :]
        for k in range(2):
            out[AT_E + 2 * k : AT_E + 2 * k + 2, :] = mod[k, two : two + 2, :]
            out[AT_M + k : AT_M + k + 1, :] = mass[k, one : one + 1, :]
        out[AT_P : AT_P + 1, :] = pair[0, one : one + 1, :].astype(F32)
        out[AT_O : AT_O + 1, :] = jnp.full((1, COLS), own[0, 0, one]).astype(F32)
        out[AT_O + 1 :, :] = jnp.zeros((MSG - AT_O - 1, COLS), F32)


def extend_kernel(u, mod, above, below, ext, left, right):
    for ch in range(8):
        at = AT_U + 2 * ch if ch < 6 else AT_E + 2 * (ch - 6)
        own = u[ch // 2, ch % 2] if ch < 6 else mod[ch - 6]
        ext[16 * ch : 16 * ch + 2, :] = above[at : at + 2, :]
        ext[16 * ch + 2 : 16 * ch + 10, :] = own
        ext[16 * ch + 10 : 16 * ch + 12, :] = below[at : at + 2, :]
        ext[16 * ch + 12 : 16 * ch + 16, :] = jnp.zeros((4, COLS), F32)
    turned = jnp.transpose(ext[...])
    left[...] = turned[0:1, :]
    right[...] = turned[COLS - 1 : COLS, :]


def edge_columns(from_left, from_right):
    sub = lax.broadcasted_iota(jnp.int32, (128, COLS), 0)
    both = jnp.where(sub < 64, jnp.broadcast_to(from_left, (128, COLS)), jnp.broadcast_to(from_right, (128, COLS)))
    return jnp.transpose(both)


def with_columns(here, edges):
    lane = lanes(here.shape)
    return jnp.where(lane == COLS - 1, edges, pltpu.roll(here, COLS - 1, axis=1))


def corners():
    return [(3 * (4 * k + 2 * x + e) + m, 2 * m + k, x, e) for k in range(2) for x in range(2) for e in range(2) for m in range(3)]


def element_sums(weight, rows_of, sides, scales, at):
    total = {}
    for i in range(2):
        start = at + 1 - i
        values = {c: rows_of[e][ch, pl.ds(start + x, ROWS), :] for c, ch, x, e in corners()}
        for k in range(2):
            for m in range(3):
                force = None
                for c in range(24):
                    t = weight(k, i, m, c) * values[c]
                    force = t if force is None else force + t
                force = force * scales[pl.ds(start + sides, ROWS), :]
                total[2 * m + k] = force if i == 0 else total[2 * m + k] + force
    return [total[ch] for ch in range(6)]


def by_corner(stiff, e):
    return lambda k, i, m, c: stiff[3 * (4 * k + 2 * i + e) + m, c]


def first_kernel(stiff, owner, ext, from_left, from_right, above, below, v, mass, ref, pair, vel, dis, weight, point, index, who, scale, spread, at_left, at_right, at_edge):
    edges = edge_columns(from_left[...], from_right[...])
    zero = jnp.zeros((8, COLS), F32)
    lane = lanes((ROWS, COLS))
    for ch in range(6):
        here, side = ext[16 * ch : 16 * ch + 16, :], edges[16 * ch : 16 * ch + 16, :]
        at_left[ch, 0:16, :] = here
        at_right[ch, 0:16, :] = with_columns(here, side)
        at_edge[ch, 0:16, :] = side
        for buf in (at_left, at_right, at_edge):
            buf[ch, 16:24, :] = zero
    here = ext[96:112, :] + ext[112:128, :]
    side = edges[96:112, :] + edges[112:128, :]
    right = with_columns(here, side)
    for n, both in enumerate((here + right, side + here)):
        scale[n, 0:16, :] = (both + pltpu.roll(both, 15, axis=0)) * 0.125
        scale[n, 16:24, :] = zero
    for k in range(2):
        weight[k, 0:1, :] = above[AT_M + k : AT_M + k + 1, :]
        weight[k, 1:9, :] = mass[k]
        weight[k, 9:10, :] = below[AT_M + k : AT_M + k + 1, :]
        weight[k, 10:16, :] = jnp.ones((6, COLS), F32)
        weight[k] = DT / weight[k]
    for ch in range(6):
        vel[ch, 0:1, :] = above[AT_V + ch : AT_V + ch + 1, :]
        vel[ch, 1:9, :] = v[ch // 2, ch % 2]
        vel[ch, 9:10, :] = below[AT_V + ch : AT_V + ch + 1, :]
        vel[ch, 10:16, :] = zero[:6]
    for m in range(3):
        point[m, 0:1, :] = above[AT_X + m : AT_X + m + 1, :]
        point[m, 1:9, :] = ref[m]
        point[m, 9:10, :] = below[AT_X + m : AT_X + m + 1, :]
        point[m, 10:16, :] = zero[:6]
        point[m] = point[m] + at_left[2 * m, 1:17, :]
    index[0:1, :] = above[AT_P : AT_P + 1, :].astype(jnp.int32)
    index[1:9, :] = pair[0]
    index[9:10, :] = below[AT_P : AT_P + 1, :].astype(jnp.int32)
    index[10:16, :] = jnp.zeros((6, COLS), jnp.int32)
    who[0:1, :] = above[AT_O : AT_O + 1, :].astype(jnp.int32)
    who[9:10, :] = below[AT_O : AT_O + 1, :].astype(jnp.int32)
    for b in range(ROWS):
        who[1 + b : 2 + b, :] = jnp.full((1, COLS), owner[0, 0, b])
        who[16 + b : 17 + b, :] = jnp.full((1, COLS), owner[1, 0, b])
    who[10:16, :] = jnp.zeros((6, COLS), jnp.int32)
    for at in (0, 8):
        straight = element_sums(by_corner(stiff, 0), (at_left, at_right), 0, scale.at[0], at)
        moved = element_sums(by_corner(stiff, 1), (at_left, at_right), 0, scale.at[0], at)
        edge = element_sums(by_corner(stiff, 1), (at_edge, at_left), 0, scale.at[1], at)
        for ch in range(6):
            force = straight[ch] + jnp.where(lane == 0, edge[ch], pltpu.roll(moved[ch], 1, axis=1))
            new = vel[ch, at : at + 8, :] - weight[ch % 2, at : at + 8, :] * force
            vel[ch, at : at + 8, :] = new
            dis[ch, at : at + 8, :] = at_left[ch, at + 1 : at + 9, :] + DT * new
    row = lanes((1, COLS))
    for k in range(2):
        for i in range(2):
            for m in range(3):
                for c in range(24):
                    one, other = [stiff[3 * (4 * k + 2 * i + e) + m, c] for e in (1, 0)]
                    at = 24 * (6 * k + 3 * i + m) + c
                    spread[at : at + 1, :] = jnp.where(row < 64, one, other)
    scale[2] = jnp.where(lanes((24, COLS)) < 64, scale[1], scale[0])


def look_up(table, owner, index, row, out):
    which = jnp.broadcast_to(index, (8, COLS))
    place, part = which & 127, (which >> 7) & 3
    found = None
    for c in range(4):
        got = jnp.take_along_axis(table[owner, 8 * c : 8 * c + 8, :], place, axis=1)
        found = got if found is None else jnp.where(part == c, got, found)
    found = jnp.where(which[0:4] >= 512, found[4:8], found[0:4])
    for c in range(4):
        out[c, row : row + 1, :] = found[c : c + 1]


def contact(words, points):
    depth = jnp.maximum(words[3] - (words[0] * points[0] + words[1] * points[1] + words[2] * points[2]), 0.0)
    return [words[m] * depth for m in range(3)]


def contact_kernel(who, table, index, vel, dis, weight, point, new_vel, new_dis, left, right, words, square):
    words[:, 8:16, :] = jnp.zeros((4, 8, COLS), F32)
    for b in range(ROWS + 2):
        look_up(table, who[b, 0], index[b : b + 1, :], b, words)
    pushes = contact([words[c] for c in range(4)], [point[m] for m in range(3)])
    for m in range(3):
        step = weight[0] * pushes[m]
        new_vel[2 * m] = (vel[2 * m] + step)[1:9]
        new_vel[2 * m + 1] = vel[2 * m + 1, 1:9, :]
        new_dis[2 * m] = dis[2 * m] + DT * step
        new_dis[2 * m + 1] = dis[2 * m + 1]
    for ch in range(6):
        square[16 * ch : 16 * ch + 16, :] = new_dis[ch]
    square[96:128, :] = jnp.zeros((32, COLS), F32)
    turned = jnp.transpose(square[...])
    left[...] = turned[0:1, :]
    right[...] = turned[COLS - 1 : COLS, :]


def inner_kernel(who, stiff, table, pair, dis, vel, mass, ref, scale, base_dis, base_vel, weight, at_right, words):
    lane = lanes((ROWS, COLS))
    for b in range(ROWS):
        look_up(table, who[16 + b, 0], pair[1, b : b + 1, :], b, words)
    push = contact([words[c] for c in range(4)], [ref[m] + dis[2 * m, 1:9, :] for m in range(3)])
    for ch in range(6):
        at_right[ch] = pltpu.roll(dis[ch], COLS - 1, axis=1)
    straight = element_sums(by_corner(stiff, 0), (dis, at_right), 1, scale.at[0], 0)
    moved = element_sums(by_corner(stiff, 1), (dis, at_right), 1, scale.at[0], 0)
    for k in range(2):
        weight[k] = DT / mass[k]
        for m in range(3):
            ch = 2 * m + k
            force = jnp.where(lane == COLS - 1, 0.0, straight[ch]) + jnp.where(lane == 0, 0.0, pltpu.roll(moved[ch], 1, axis=1))
            net = push[m] - force if k == 0 else -force
            new = vel[ch] + weight[k] * net
            base_vel[ch] = new
            base_dis[ch] = dis[ch, 1:9, :] + DT * new


def outer_kernel(dis, base_dis, base_vel, weight, scale, spread, from_left, from_right, out_dis, out_vel, at_left, at_right):
    edges = edge_columns(from_left[...], from_right[...])
    lane = lanes((16, COLS))
    for ch in range(6):
        here, side = dis[ch], edges[16 * ch : 16 * ch + 16, :]
        at_left[ch] = jnp.where(lane < 64, side, here)
        at_right[ch] = jnp.where(lane < 64, here, side)

    def spread_row(k, i, m, c):
        at = 24 * (6 * k + 3 * i + m) + c
        return spread[at : at + 1, :]

    forces = element_sums(spread_row, (at_left, at_right), 1, scale.at[2], 0)
    lane = lanes((ROWS, COLS))
    for m in range(3):
        for k in range(2):
            ch = 2 * m + k
            change = weight[k] * jnp.where((lane == 0) | (lane == COLS - 1), forces[ch], 0.0)
            out_vel[m, k] = base_vel[ch] - change
            out_dis[m, k] = base_dis[ch] - DT * change


def call(kernel, outs, specs, scratch=(), flops=1_000_000, moved=1_000_000, room=16):
    return pl.pallas_call(
        kernel,
        out_shape=outs,
        in_specs=specs,
        out_specs=jax.tree.map(lambda _: VMEM, outs),
        scratch_shapes=list(scratch),
        compiler_params=pltpu.CompilerParams(vmem_limit_bytes=room << 20),
        cost_estimate=pl.CostEstimate(flops=flops, bytes_accessed=moved, transcendentals=0),
    )


def swapped(to_next, to_last, axis):
    size = lax.axis_size(axis)
    up = [(i, (i + 1) % size) for i in range(size)]
    down = [(j, i) for i, j in up]
    return lax.ppermute(to_next, axis, up), lax.ppermute(to_last, axis, down)


def shards(u, v, mass, mod, stiff, ref, facets, penalty, owners, pair):
    width = facets.shape[-1]
    buffers = [pltpu.VMEM((6, 24, COLS), F32)] * 3
    owner = owners.reshape(2, 1, ROWS)
    sources = (u, v, mass, mod, ref, facets.reshape(6 * width // COLS, COLS), penalty.reshape(width // COLS, COLS), pair)
    table, up, down = call(
        pack_kernel,
        (struct(OWNERS, 32, COLS), struct(MSG, COLS), struct(MSG, COLS)),
        [pl.BlockSpec(memory_space=pltpu.HBM)] * len(sources) + [SMEM],
        [pltpu.VMEM(x.shape, x.dtype) for x in sources] + [pltpu.SemaphoreType.DMA((len(sources),))],
        room=60,
    )(*sources, owner)
    tables = lax.all_to_all(table, "mesh", split_axis=0, concat_axis=0, tiled=True)
    above, below = swapped(down, up, "mesh")
    ext, left, right = call(
        extend_kernel, (struct(128, COLS), struct(1, COLS), struct(1, COLS)), [VMEM] * 4
    )(u, mod, above, below)
    from_left, from_right = swapped(right, left, "sub")
    vel, dis, weight, point, index, who, scale, spread = call(
        first_kernel,
        (
            struct(6, 16, COLS),
            struct(6, 16, COLS),
            struct(2, 16, COLS),
            struct(3, 16, COLS),
            struct(16, COLS, dtype=jnp.int32),
            struct(24, COLS, dtype=jnp.int32),
            struct(3, 24, COLS),
            struct(288, COLS),
        ),
        [SMEM] * 2 + [VMEM] * 9,
        buffers,
    )(stiff, owner, ext, from_left, from_right, above, below, v, mass, ref, pair)
    new_vel, new_dis, left, right = call(
        contact_kernel,
        (struct(6, ROWS, COLS), struct(6, 16, COLS), struct(1, COLS), struct(1, COLS)),
        [VMEM] * 7,
        [pltpu.VMEM((4, 16, COLS), F32), pltpu.VMEM((128, COLS), F32)],
    )(who, tables, index, vel, dis, weight, point)
    from_left, from_right = swapped(right, left, "sub")
    base_dis, base_vel, weight = call(
        inner_kernel,
        (struct(6, ROWS, COLS), struct(6, ROWS, COLS), struct(2, ROWS, COLS)),
        [VMEM, SMEM] + [VMEM] * 7,
        [pltpu.VMEM((6, 16, COLS), F32), pltpu.VMEM((4, 8, COLS), F32)],
    )(who, stiff, tables, pair, new_dis, new_vel, mass, ref, scale)
    return call(
        outer_kernel,
        (struct(3, 2, ROWS, COLS), struct(3, 2, ROWS, COLS)),
        [VMEM] * 8,
        [pltpu.VMEM((6, 16, COLS), F32)] * 2,
    )(new_dis, base_dis, base_vel, weight, scale, spread, from_left, from_right)


def solution(mesh):
    in_specs = (
        P(None, None, "mesh", "sub"),
        P(None, None, "mesh", "sub"),
        P(None, "mesh", "sub"),
        P(None, "mesh", "sub"),
        P(),
        P(None, "mesh", "sub"),
        P("mesh", "sub", None, None),
        P("mesh", "sub", None),
        P(None, "mesh", "sub", None, None),
        P(None, "mesh", "sub"),
    )
    out_specs = (P(None, None, "mesh", "sub"), P(None, None, "mesh", "sub"))
    return jax.shard_map(shards, mesh=mesh, in_specs=in_specs, out_specs=out_specs, check_vma=False)
```

time: 57.8 us -> 52.7 us (0.912)
  the two profiles are of different devices: /device:TPU:30 before, /device:TPU:24 now
where the time goes in v2:
time: 52.7 us; the launch traced here: 52.2 us
  starting transfers between devices  41 us (78%)
  Pallas kernels  6.7 us (13%)
  waiting for transfers between devices  3.6 us (7%)
  between operations  0.85 us (2%)
    ppermute x6, starting transfers between devices, swapped(): return (lax.ppermute(to_next, axis, up), lax.ppermute(to_last, axis, down))  24.4 us
    all_to_all x1, starting transfers between devices, shards(): lax.all_to_all(table, 'mesh', split_axis=0, concat_axis=0, tiled=True)  16.6 us
    ppermute x6, waiting for transfers between devices, swapped(): return (lax.ppermute(to_next, axis, up), lax.ppermute(to_last, axis, down))  3.6 us
    pallas_call x1, Pallas kernels, shards(): call(pack_kernel, (struct(OWNERS, 32, COLS), struct(MSG, COLS), struct(MS...  2.48 us
    pallas_call x1, Pallas kernels, shards(): call(first_kernel, (struct(6, 16, COLS), struct(6, 16, COLS), struct(2, 1...  1.98 us
    pallas_call x1, Pallas kernels, shards(): call(inner_kernel, (struct(6, ROWS, COLS), struct(6, ROWS, COLS), struct(...  1.09 us
  transfers between devices with their start and end apart: 7, of which 5 were waited for; matrix products, arithmetic and copies ran while one was open for 0% of the time, Pallas kernels for 6%

profile of v2, /device:TPU:24, one launch (start us, length us, event | category | flops | bytes accessed | tf_op | source)
XLA Modules:
  0.0 52.2 jit_solution(603411913334848641)
XLA Ops:
  0.6 2.5 %shard_map.113 = (f32[32,32,128]{2,1,0:T(8,128)}, f32[32,128]{1,0:T(8,128)}, f32[32,128]{1,0:T(8,128)}) custom-call(f32[3,2,8,128]{3,2,1,0:T(8,128)} %u.3, f32[3,2,8,128]{3,2,1,0:T(8,128)} %v.3, f32[2,8,128]{2,1,0:T(8,128)} %mass.5, f32[2,8,128]{2,1,0:T(8,128)} %mod.3, f32[3,8,128]{2,1,0:T(8,128)} %ref.5, f32[48,128]{1,0:T(8,128)} %bitcast.7, ...), custom_call_target="tpu_custom_call" | custom-call | flops 1000000 | bytes 1000000 | tf_op jit(solution)/shard_map/pallas_call | solution.py:272
  3.1 0.0 copy-start.9
  3.1 0.0 copy-start.8
  3.1 0.0 copy-start.1
  3.1 0.0 copy-start.6
  3.2 16.6 %all-to-all-start = ((f32[32,32,128]{2,1,0:T(8,128)}), f32[32,32,128]{2,1,0:T(8,128)S(1)}, u32[]{:S(2)}, u32[]{:S(2)}) async-start(f32[32,32,128]{2,1,0:T(8,128)} %get-tuple-element.29), calls=%async_computation | async-start | bytes 1048576 | tf_op jit(solution)/shard_map/all_to_all | solution.py:279
  19.8 3.4 %collective-permute-start = (f32[32,128]{1,0:T(8,128)S(1)}, f32[32,128]{1,0:T(8,128)S(1)}, u32[]{:S(2)}, u32[]{:S(2)}) collective-permute-start(f32[32,128]{1,0:T(8,128)S(1)} %copy-done.9), channel_id=1, source_target_pairs={{0,32},{32,64},{64,96},{96,128},{128,160},{160,192},{192,224},{224... | collective-permute-start | bytes 49160 | tf_op jit(solution)/shard_map/ppermute | solution.py:264
  23.2 0.0 copy-done.8
  23.2 0.0 copy-start.2
  23.2 4.6 %collective-permute-start.1 = (f32[32,128]{1,0:T(8,128)S(1)}, f32[32,128]{1,0:T(8,128)S(1)}, u32[]{:S(2)}, u32[]{:S(2)}) collective-permute-start(f32[32,128]{1,0:T(8,128)S(1)} %copy-done.8), channel_id=1, source_target_pairs={{32,0},{64,32},{96,64},{128,96},{160,128},{192,160},{224,192},{256... | collective-permute-start | bytes 49160 | tf_op jit(solution)/shard_map/ppermute | solution.py:264
  27.8 2.1 %collective-permute-done.above = f32[32,128]{1,0:T(8,128)S(1)} collective-permute-done((f32[32,128]{1,0:T(8,128)S(1)}, f32[32,128]{1,0:T(8,128)S(1)}, u32[]{:S(2)}, u32[]{:S(2)}) %collective-permute-start) | collective-permute-done | bytes 16416 | tf_op jit(solution)/shard_map/ppermute | solution.py:264
  29.9 0.0 collective-permute-done.1.below
  29.9 0.0 copy-start
  29.9 0.0 copy-start.3
  29.9 0.0 copy-start.4
  29.9 0.0 copy-start.5
  30.0 0.1 shard_map.114
  30.0 0.0 collective-permute-start.2
  30.1 0.0 copy-start.7
  30.1 13.5 %collective-permute-start.3 = (f32[1,128]{1,0:T(1,128)S(1)}, f32[1,128]{1,0:T(1,128)S(1)}, u32[]{:S(2)}, u32[]{:S(2)}) collective-permute-start(f32[1,128]{1,0:T(1,128)S(1)} %get-tuple-element.27), channel_id=1, source_target_pairs={{1,0},{2,1},{3,2},{4,3},{5,4},{6,5},{7,6},{8,7},{9,8},{10,9},{11,1... | collective-permute-start | bytes 1544 | tf_op jit(solution)/shard_map/ppermute | solution.py:264
  43.5 1.2 %collective-permute-done.2.from_left = f32[1,128]{1,0:T(1,128)S(1)} collective-permute-done((f32[1,128]{1,0:T(1,128)S(1)}, f32[1,128]{1,0:T(1,128)S(1)}, u32[]{:S(2)}, u32[]{:S(2)}) %collective-permute-start.2) | collective-permute-done | bytes 544 | tf_op jit(solution)/shard_map/ppermute | solution.py:264
  44.7 0.1 collective-permute-done.3.from_right
  44.8 0.0 copy-done
  44.9 2.0 %shard_map.115 = (f32[6,16,128]{2,1,0:T(8,128)S(1)}, f32[6,16,128]{2,1,0:T(8,128)S(1)}, f32[2,16,128]{2,1,0:T(8,128)S(1)}, f32[3,16,128]{2,1,0:T(8,128)S(1)}, s3...) custom-call(f32[24,24]{1,0:T(8,128)S(1)} %copy-done.5, ...), custom_call_target="tpu_custom_call" | custom-call | flops 1000000 | bytes 1000000 | tf_op jit(solution)/shard_map/pallas_call | solution.py:285
  46.9 0.0 all-to-all-done.table
  46.9 0.3 shard_map.116
  47.2 0.0 collective-permute-start.4
  47.2 3.0 %collective-permute-start.5 = (f32[1,128]{1,0:T(1,128)S(1)}, f32[1,128]{1,0:T(1,128)S(1)}, u32[]{:S(2)}, u32[]{:S(2)}) collective-permute-start(f32[1,128]{1,0:T(1,128)S(1)} %get-tuple-element.43), channel_id=1, source_target_pairs={{1,0},{2,1},{3,2},{4,3},{5,4},{6,5},{7,6},{8,7},{9,8},{10,9},{11,1... | collective-permute-start | bytes 1544 | tf_op jit(solution)/shard_map/ppermute | solution.py:264
  50.1 1.1 %shard_map.117 = (f32[6,8,128]{2,1,0:T(8,128)S(1)}, f32[6,8,128]{2,1,0:T(8,128)S(1)}, f32[2,8,128]{2,1,0:T(8,128)S(1)}) custom-call(s32[24,128]{1,0:T(8,128)S(1)} %get-tuple-element.28.who, f32[24,24]{1,0:T(8,128)S(1)} %copy-done.5, f32[32,32,128]{2,1,0:T(8,128)S(1)} %all-to-all-done.table, s32[2,8,128]{2,1,0:T(8,128)S(1)} %copy-done.4, ...), custom_call_target="tpu_custom_call" | custom-call | flops 1000000 | bytes 1000000 | tf_op jit(solution)/shard_map/pallas_call | solution.py:307
  51.2 0.1 collective-permute-done.4.from_left
  51.4 0.1 collective-permute-done.5.from_right
  51.4 0.8 %shard_map.118 = (f32[3,2,8,128]{3,2,1,0:T(8,128)}, f32[3,2,8,128]{3,2,1,0:T(8,128)}) custom-call(f32[6,16,128]{2,1,0:T(8,128)S(1)} %get-tuple-element.35.dis, f32[6,8,128]{2,1,0:T(8,128)S(1)} %get-tuple-element.38.base_dis, f32[6,8,128]{2,1,0:T(8,128)S(1)} %get-tuple-element.39.base_vel, f32[2,8,128]{2,1,0:T(8,128)S(1)} %get-tuple-element.40.weight, ...), custom_call_target="tpu_custom_call" | custom-call | flops 1000000 | bytes 1000000 | tf_op jit(solution)/shard_map/pallas_call | solution.py:313
  (8 shorter events, 0.0 us)
Async XLA Ops:
  3.1 16.7 %copy-start.9 = (f32[32,128]{1,0:T(8,128)S(1)}, f32[32,128]{1,0:T(8,128)}, u32[]{:S(2)}) copy-start(f32[32,128]{1,0:T(8,128)} %get-tuple-element.23) | copy-start | bytes 49156
  3.1 20.1 %copy-start.8 = (f32[32,128]{1,0:T(8,128)S(1)}, f32[32,128]{1,0:T(8,128)}, u32[]{:S(2)}) copy-start(f32[32,128]{1,0:T(8,128)} %get-tuple-element.24) | copy-start | bytes 49156
  3.1 26.8 %copy-start.1 = (f32[3,2,8,128]{3,2,1,0:T(8,128)S(1)}, f32[3,2,8,128]{3,2,1,0:T(8,128)}, u32[]{:S(2)}) copy-start(f32[3,2,8,128]{3,2,1,0:T(8,128)} %u.3) | copy-start | bytes 73732
  3.1 26.8 %copy-start.6 = (f32[2,8,128]{2,1,0:T(8,128)S(1)}, f32[2,8,128]{2,1,0:T(8,128)}, u32[]{:S(2)}) copy-start(f32[2,8,128]{2,1,0:T(8,128)} %mod.3) | copy-start | bytes 24580
  3.2 43.7 %all-to-all-start = ((f32[32,32,128]{2,1,0:T(8,128)}), f32[32,32,128]{2,1,0:T(8,128)S(1)}, u32[]{:S(2)}, u32[]{:S(2)}) async-start(f32[32,32,128]{2,1,0:T(8,128)} %get-tuple-element.29), calls=%async_computation | async-start | bytes 1048576 | tf_op jit(solution)/shard_map/all_to_all | solution.py:279
  19.8 10.1 %collective-permute-start = (f32[32,128]{1,0:T(8,128)S(1)}, f32[32,128]{1,0:T(8,128)S(1)}, u32[]{:S(2)}, u32[]{:S(2)}) collective-permute-start(f32[32,128]{1,0:T(8,128)S(1)} %copy-done.9), channel_id=1, source_target_pairs={{0,32},{32,64},{64,96},{96,128},{128,160},{160,192},{192,224},{224... | collective-permute-start | bytes 49160 | tf_op jit(solution)/shard_map/ppermute | solution.py:264
  23.2 21.6 %copy-start.2 = (f32[3,2,8,128]{3,2,1,0:T(8,128)S(1)}, f32[3,2,8,128]{3,2,1,0:T(8,128)}, u32[]{:S(2)}) copy-start(f32[3,2,8,128]{3,2,1,0:T(8,128)} %v.3) | copy-start | bytes 73732
  23.2 6.7 %collective-permute-start.1 = (f32[32,128]{1,0:T(8,128)S(1)}, f32[32,128]{1,0:T(8,128)S(1)}, u32[]{:S(2)}, u32[]{:S(2)}) collective-permute-start(f32[32,128]{1,0:T(8,128)S(1)} %copy-done.8), channel_id=1, source_target_pairs={{32,0},{64,32},{96,64},{128,96},{160,128},{192,160},{224,192},{256... | collective-permute-start | bytes 49160 | tf_op jit(solution)/shard_map/ppermute | solution.py:264
  29.9 14.9 %copy-start = (f32[3,8,128]{2,1,0:T(8,128)S(1)}, f32[3,8,128]{2,1,0:T(8,128)}, u32[]{:S(2)}) copy-start(f32[3,8,128]{2,1,0:T(8,128)} %ref.5) | copy-start | bytes 36868
  29.9 14.9 %copy-start.3 = (f32[2,8,128]{2,1,0:T(8,128)S(1)}, f32[2,8,128]{2,1,0:T(8,128)}, u32[]{:S(2)}) copy-start(f32[2,8,128]{2,1,0:T(8,128)} %mass.5) | copy-start | bytes 24580
  29.9 14.9 %copy-start.4 = (s32[2,8,128]{2,1,0:T(8,128)S(1)}, s32[2,8,128]{2,1,0:T(8,128)}, u32[]{:S(2)}) copy-start(s32[2,8,128]{2,1,0:T(8,128)} %pair.5) | copy-start | bytes 24580
  29.9 14.9 %copy-start.5 = (f32[24,24]{1,0:T(8,128)S(1)}, f32[24,24]{1,0:T(8,128)}, u32[]{:S(2)}) copy-start(f32[24,24]{1,0:T(8,128)} %stiff.3) | copy-start | bytes 6916
  30.0 14.7 %collective-permute-start.2 = (f32[1,128]{1,0:T(1,128)S(1)}, f32[1,128]{1,0:T(1,128)S(1)}, u32[]{:S(2)}, u32[]{:S(2)}) collective-permute-start(f32[1,128]{1,0:T(1,128)S(1)} %get-tuple-element.26), channel_id=1, source_target_pairs={{0,1},{1,2},{2,3},{3,4},{4,5},{5,6},{6,7},{7,8},{8,9},{9,10},{10,1... | collective-permute-start | bytes 1544 | tf_op jit(solution)/shard_map/ppermute | solution.py:264
  30.1 14.8 %copy-start.7 = (s32[2,1,1,8,1]{3,4,2,1,0:T(1,128)S(1)}, s32[2,1,1,8,1]{3,4,2,1,0:T(1,128)}, u32[]{:S(2)}) copy-start(s32[2,1,1,8,1]{3,4,2,1,0:T(1,128)} %param.18) | copy-start | bytes 196
  30.1 14.8 %collective-permute-start.3 = (f32[1,128]{1,0:T(1,128)S(1)}, f32[1,128]{1,0:T(1,128)S(1)}, u32[]{:S(2)}, u32[]{:S(2)}) collective-permute-start(f32[1,128]{1,0:T(1,128)S(1)} %get-tuple-element.27), channel_id=1, source_target_pairs={{1,0},{2,1},{3,2},{4,3},{5,4},{6,5},{7,6},{8,7},{9,8},{10,9},{11,1... | collective-permute-start | bytes 1544 | tf_op jit(solution)/shard_map/ppermute | solution.py:264
  47.2 4.2 %collective-permute-start.4 = (f32[1,128]{1,0:T(1,128)S(1)}, f32[1,128]{1,0:T(1,128)S(1)}, u32[]{:S(2)}, u32[]{:S(2)}) collective-permute-start(f32[1,128]{1,0:T(1,128)S(1)} %get-tuple-element.42), channel_id=1, source_target_pairs={{0,1},{1,2},{2,3},{3,4},{4,5},{5,6},{6,7},{7,8},{8,9},{9,10},{10,1... | collective-permute-start | bytes 1544 | tf_op jit(solution)/shard_map/ppermute | solution.py:264
  47.2 4.3 %collective-permute-start.5 = (f32[1,128]{1,0:T(1,128)S(1)}, f32[1,128]{1,0:T(1,128)S(1)}, u32[]{:S(2)}, u32[]{:S(2)}) collective-permute-start(f32[1,128]{1,0:T(1,128)S(1)} %get-tuple-element.43), channel_id=1, source_target_pairs={{1,0},{2,1},{3,2},{4,3},{5,4},{6,5},{7,6},{8,7},{9,8},{10,9},{11,1... | collective-permute-start | bytes 1544 | tf_op jit(solution)/shard_map/ppermute | solution.py:264

commit v3 on v2

--- a/solution.py
+++ b/solution.py
@@ -8,6 +8,8 @@
 DT = 0.1
 F32 = jnp.float32
 VMEM = pl.BlockSpec(memory_space=pltpu.VMEM)
+HBM = pl.BlockSpec(memory_space=pltpu.HBM)
+ANY = pl.BlockSpec(memory_space=pl.ANY)
 SMEM = pl.BlockSpec(memory_space=pltpu.SMEM)
 ROWS = 8
 COLS = 128
@@ -24,22 +26,23 @@
     return lax.broadcasted_iota(jnp.int32, shape, len(shape) - 1)
 
 
-def pack_kernel(u, v, mass, mod, ref, fac, pen, pair, own, table, up, down, *held):
-    arrays, sems = held[:-1], held[-1]
-    copies = [pltpu.make_async_copy(a, b, sems.at[n]) for n, (a, b) in enumerate(zip((u, v, mass, mod, ref, fac, pen, pair), arrays))]
+def fetched(sources, held, sems):
+    copies = [pltpu.make_async_copy(a, b, sems.at[n]) for n, (a, b) in enumerate(zip(sources, held))]
     for copy in copies:
         copy.start()
     for copy in copies:
         copy.wait()
-    u, v, mass, mod, ref, fac, pen, pair = arrays
+    return held
+
+
+def pack_kernel(fac, pen, u, v, mass, mod, ref, pair, own, mine, up, down, *held):
+    fac, pen, u, v, mass, mod, ref, pair, own = fetched((fac, pen, u, v, mass, mod, ref, pair, own), held[:-1], held[-1])
     root = jnp.sqrt(pen[...])
     c, n = [[fac[8 * (m + at) : 8 * (m + at) + 8, :] for m in range(3)] for at in (0, 3)]
     dist = n[0] * c[0] + n[1] * c[1] + n[2] * c[2]
     words = [root * n[0], root * n[1], root * n[2], root * dist]
     for q in range(4):
-        mine = jnp.concatenate([w[4 * h + q : 4 * h + q + 1, :] for h in range(2) for w in words], axis=0)
-        for o in range(OWNERS):
-            table[o, 8 * q : 8 * q + 8, :] = mine
+        mine[8 * q : 8 * q + 8, :] = jnp.concatenate([w[4 * h + q : 4 * h + q + 1, :] for h in range(2) for w in words], axis=0)
     for out, two, one in ((down, ROWS - 2, ROWS - 1), (up, 0, 0)):
         for m in range(3):
             for k in range(2):
@@ -51,8 +54,16 @@
             out[AT_E + 2 * k : AT_E + 2 * k + 2, :] = mod[k, two : two + 2, :]
             out[AT_M + k : AT_M + k + 1, :] = mass[k, one : one + 1, :]
         out[AT_P : AT_P + 1, :] = pair[0, one : one + 1, :].astype(F32)
-        out[AT_O : AT_O + 1, :] = jnp.full((1, COLS), own[0, 0, one]).astype(F32)
-        out[AT_O + 1 :, :] = jnp.zeros((MSG - AT_O - 1, COLS), F32)
+        out[AT_O :, :] = jnp.zeros((MSG - AT_O, COLS), F32)
+        out[AT_O : AT_O + 1, 0:ROWS] = own[0].astype(F32)
+
+
+def spread_kernel(mine, above, below, table, sems):
+    copies = [pltpu.make_async_copy(mine, table.at[o], sems.at[o]) for o in range(OWNERS)]
+    for copy in copies:
+        copy.start()
+    for copy in copies:
+        copy.wait()
 
 
 def extend_kernel(u, mod, above, below, ext, left, right):
@@ -141,12 +152,11 @@
     index[1:9, :] = pair[0]
     index[9:10, :] = below[AT_P : AT_P + 1, :].astype(jnp.int32)
     index[10:16, :] = jnp.zeros((6, COLS), jnp.int32)
+    who[...] = jnp.zeros((8, COLS), jnp.int32)
     who[0:1, :] = above[AT_O : AT_O + 1, :].astype(jnp.int32)
-    who[9:10, :] = below[AT_O : AT_O + 1, :].astype(jnp.int32)
-    for b in range(ROWS):
-        who[1 + b : 2 + b, :] = jnp.full((1, COLS), owner[0, 0, b])
-        who[16 + b : 17 + b, :] = jnp.full((1, COLS), owner[1, 0, b])
-    who[10:16, :] = jnp.zeros((6, COLS), jnp.int32)
+    who[1:2, :] = below[AT_O : AT_O + 1, :].astype(jnp.int32)
+    for step in range(2):
+        who[2 + step : 3 + step, 0:ROWS] = owner[step]
     for at in (0, 8):
         straight = element_sums(by_corner(stiff, 0), (at_left, at_right), 0, scale.at[0], at)
         moved = element_sums(by_corner(stiff, 1), (at_left, at_right), 0, scale.at[0], at)
@@ -187,7 +197,7 @@
 def contact_kernel(who, table, index, vel, dis, weight, point, new_vel, new_dis, left, right, words, square):
     words[:, 8:16, :] = jnp.zeros((4, 8, COLS), F32)
     for b in range(ROWS + 2):
-        look_up(table, who[b, 0], index[b : b + 1, :], b, words)
+        look_up(table, who[0, ROWS - 1] if b == 0 else who[1, 0] if b == ROWS + 1 else who[2, b - 1], index[b : b + 1, :], b, words)
     pushes = contact([words[c] for c in range(4)], [point[m] for m in range(3)])
     for m in range(3):
         step = weight[0] * pushes[m]
@@ -206,7 +216,7 @@
 def inner_kernel(who, stiff, table, pair, dis, vel, mass, ref, scale, base_dis, base_vel, weight, at_right, words):
     lane = lanes((ROWS, COLS))
     for b in range(ROWS):
-        look_up(table, who[16 + b, 0], pair[1, b : b + 1, :], b, words)
+        look_up(table, who[3, b], pair[1, b : b + 1, :], b, words)
     push = contact([words[c] for c in range(4)], [ref[m] + dis[2 * m, 1:9, :] for m in range(3)])
     for ch in range(6):
         at_right[ch] = pltpu.roll(dis[ch], COLS - 1, axis=1)
@@ -245,12 +255,12 @@
             out_dis[m, k] = base_dis[ch] - DT * change
 
 
-def call(kernel, outs, specs, scratch=(), flops=1_000_000, moved=1_000_000, room=16):
+def call(kernel, outs, specs, scratch=(), room=16, out_specs=None, flops=1_000_000, moved=1_000_000):
     return pl.pallas_call(
         kernel,
         out_shape=outs,
         in_specs=specs,
-        out_specs=jax.tree.map(lambda _: VMEM, outs),
+        out_specs=out_specs or jax.tree.map(lambda _: VMEM, outs),
         scratch_shapes=list(scratch),
         compiler_params=pltpu.CompilerParams(vmem_limit_bytes=room << 20),
         cost_estimate=pl.CostEstimate(flops=flops, bytes_accessed=moved, transcendentals=0),
@@ -268,16 +278,29 @@
     width = facets.shape[-1]
     buffers = [pltpu.VMEM((6, 24, COLS), F32)] * 3
     owner = owners.reshape(2, 1, ROWS)
-    sources = (u, v, mass, mod, ref, facets.reshape(6 * width // COLS, COLS), penalty.reshape(width // COLS, COLS), pair)
-    table, up, down = call(
+    sources = (
+        facets.reshape(6 * width // COLS, COLS),
+        penalty.reshape(width // COLS, COLS),
+        *(u, v, mass, mod, ref, pair, owner),
+    )
+    mine, up, down = call(
         pack_kernel,
-        (struct(OWNERS, 32, COLS), struct(MSG, COLS), struct(MSG, COLS)),
-        [pl.BlockSpec(memory_space=pltpu.HBM)] * len(sources) + [SMEM],
+        (struct(32, COLS), struct(MSG, COLS), struct(MSG, COLS)),
+        [HBM] * len(sources),
         [pltpu.VMEM(x.shape, x.dtype) for x in sources] + [pltpu.SemaphoreType.DMA((len(sources),))],
         room=60,
-    )(*sources, owner)
+    )(*sources)
+    above, below = swapped(down, up, "mesh")
+    table = call(
+        spread_kernel,
+        struct(OWNERS, 32, COLS),
+        [HBM, ANY, ANY],
+        [pltpu.SemaphoreType.DMA((OWNERS,))],
+        out_specs=HBM,
+        flops=0,
+        moved=0,
+    )(mine, above, below)
     tables = lax.all_to_all(table, "mesh", split_axis=0, concat_axis=0, tiled=True)
-    above, below = swapped(down, up, "mesh")
     ext, left, right = call(
         extend_kernel, (struct(128, COLS), struct(1, COLS), struct(1, COLS)), [VMEM] * 4
     )(u, mod, above, below)
@@ -290,11 +313,11 @@
             struct(2, 16, COLS),
             struct(3, 16, COLS),
             struct(16, COLS, dtype=jnp.int32),
-            struct(24, COLS, dtype=jnp.int32),
+            struct(8, COLS, dtype=jnp.int32),
             struct(3, 24, COLS),
             struct(288, COLS),
         ),
-        [SMEM] * 2 + [VMEM] * 9,
+        [SMEM] + [VMEM] * 10,
         buffers,
     )(stiff, owner, ext, from_left, from_right, above, below, v, mass, ref, pair)
     new_vel, new_dis, left, right = call(

time: 52.7 us -> 56.8 us (1.078)
  the two profiles are of different devices: /device:TPU:24 before, /device:TPU:6 now
where the time goes in v3:
time: 56.8 us; the launch traced here: 56.4 us
  starting transfers between devices  34.9 us (61%)
  waiting for transfers between devices  13 us (23%)
  Pallas kernels  6.87 us (12%)
  between operations  0.83 us (1%)
  local copies, waits for them, and re-layouts  0.77 us (1%)
    all_to_all x1, starting transfers between devices, shards(): lax.all_to_all(table, 'mesh', split_axis=0, concat_axis=0, tiled=True)  20.8 us
    ppermute x6, starting transfers between devices, swapped(): return (lax.ppermute(to_next, axis, up), lax.ppermute(to_last, axis, down))  14.2 us
    ppermute x6, waiting for transfers between devices, swapped(): return (lax.ppermute(to_next, axis, up), lax.ppermute(to_last, axis, down))  7.01 us
    all_to_all x1, waiting for transfers between devices, shards(): lax.all_to_all(table, 'mesh', split_axis=0, concat_axis=0, tiled=True)  5.96 us
    pallas_call x1, Pallas kernels, shards(): call(first_kernel, (struct(6, 16, COLS), struct(6, 16, COLS), struct(2, 1...  1.97 us
    pallas_call x1, Pallas kernels, shards(): call(pack_kernel, (struct(32, COLS), struct(MSG, COLS), struct(MSG, COLS)...  1.53 us
  transfers between devices with their start and end apart: 7, of which 6 were waited for; matrix products, arithmetic and copies ran while one was open for 0% of the time, Pallas kernels for 6%

profile of v3, /device:TPU:6, one launch (start us, length us, event | category | flops | bytes accessed | tf_op | source)
XLA Modules:
  0.0 56.4 jit_solution(13144891632538199982)
XLA Ops:
  0.6 1.5 %shard_map.113 = (f32[32,128]{1,0:T(8,128)}, f32[32,128]{1,0:T(8,128)}, f32[32,128]{1,0:T(8,128)}) custom-call(f32[48,128]{1,0:T(8,128)} %bitcast.7, f32[8,128]{1,0:T(8,128)} %bitcast.8, f32[3,2,8,128]{3,2,1,0:T(8,128)} %u.3, f32[3,2,8,128]{3,2,1,0:T(8,128)} %v.3, f32[2,8,128]{2,1,0:T(8,128)} %mass.5, f32[2,8,128]{2,1,0:T(8,128)} %mod.3, f32[3,8,128]{2,1,0:T(8,128)} %ref.5, ...), custom_call_target="tpu_custom_call" | custom-call | flops 1000000 | bytes 1000000 | tf_op jit(solution)/shard_map/pallas_call | solution.py:286
  2.2 3.4 %collective-permute-start = (f32[32,128]{1,0:T(8,128)}, f32[32,128]{1,0:T(8,128)S(1)}, u32[]{:S(2)}, u32[]{:S(2)}) collective-permute-start(f32[32,128]{1,0:T(8,128)} %get-tuple-element.23), channel_id=1, source_target_pairs={{0,32},{32,64},{64,96},{96,128},{128,160},{160,192},{192,224},{224... | collective-permute-start | bytes 49160 | tf_op jit(solution)/shard_map/ppermute | solution.py:274
  5.6 2.4 %collective-permute-start.1 = (f32[32,128]{1,0:T(8,128)}, f32[32,128]{1,0:T(8,128)S(1)}, u32[]{:S(2)}, u32[]{:S(2)}) collective-permute-start(f32[32,128]{1,0:T(8,128)} %get-tuple-element.24), channel_id=1, source_target_pairs={{32,0},{64,32},{96,64},{128,96},{160,128},{192,160},{224,192},{256... | collective-permute-start | bytes 49160 | tf_op jit(solution)/shard_map/ppermute | solution.py:274
  8.0 0.0 collective-permute-done.above
  8.0 5.5 %collective-permute-done.1.below = f32[32,128]{1,0:T(8,128)S(1)} collective-permute-done((f32[32,128]{1,0:T(8,128)}, f32[32,128]{1,0:T(8,128)S(1)}, u32[]{:S(2)}, u32[]{:S(2)}) %collective-permute-start.1) | collective-permute-done | bytes 16416 | tf_op jit(solution)/shard_map/ppermute | solution.py:274
  13.5 0.7 %copy-done.7 = f32[32,128]{1,0:T(8,128)S(1)} copy-done((f32[32,128]{1,0:T(8,128)S(1)}, f32[32,128]{1,0:T(8,128)}, u32[]{:S(2)}) %copy-start.7) | copy-done | bytes 16408
  14.2 1.1 %shard_map.116 = f32[32,32,128]{2,1,0:T(8,128)} custom-call(f32[32,128]{1,0:T(8,128)S(1)} %copy-done.7, f32[32,128]{1,0:T(8,128)S(1)} %collective-permute-done.above, f32[32,128]{1,0:T(8,128)S(1)} %collective-permute-done.1.below), custom_call_target="tpu_custom_call" | custom-call | tf_op jit(solution)/shard_map/pallas_call | solution.py:294
  15.3 0.0 copy-start.1
  15.4 0.0 copy-start.6
  15.4 20.8 %all-to-all-start = ((f32[32,32,128]{2,1,0:T(8,128)}), f32[32,32,128]{2,1,0:T(8,128)S(1)}, u32[]{:S(2)}, u32[]{:S(2)}) async-start(f32[32,32,128]{2,1,0:T(8,128)} %shard_map.116), calls=%async_computation | async-start | bytes 1048576 | tf_op jit(solution)/shard_map/all_to_all | solution.py:303
  36.2 0.0 copy-start
  36.2 0.0 copy-start.2
  36.2 0.0 copy-start.3
  36.2 0.0 copy-start.4
  36.2 0.0 copy-start.5
  36.2 0.1 shard_map.114
  36.3 0.0 collective-permute-start.2
  36.3 0.0 copy-start.8
  36.4 3.1 %collective-permute-start.3 = (f32[1,128]{1,0:T(1,128)S(1)}, f32[1,128]{1,0:T(1,128)S(1)}, u32[]{:S(2)}, u32[]{:S(2)}) collective-permute-start(f32[1,128]{1,0:T(1,128)S(1)} %get-tuple-element.27), channel_id=1, source_target_pairs={{1,0},{2,1},{3,2},{4,3},{5,4},{6,5},{7,6},{8,7},{9,8},{10,9},{11,1... | collective-permute-start | bytes 1544 | tf_op jit(solution)/shard_map/ppermute | solution.py:274
  39.5 1.2 %collective-permute-done.2.from_left = f32[1,128]{1,0:T(1,128)S(1)} collective-permute-done((f32[1,128]{1,0:T(1,128)S(1)}, f32[1,128]{1,0:T(1,128)S(1)}, u32[]{:S(2)}, u32[]{:S(2)}) %collective-permute-start.2) | collective-permute-done | bytes 544 | tf_op jit(solution)/shard_map/ppermute | solution.py:274
  40.7 0.1 collective-permute-done.3.from_right
  40.8 0.0 copy-done.2
  40.8 0.0 copy-done.4
  40.8 2.0 %shard_map.115 = (f32[6,16,128]{2,1,0:T(8,128)S(1)}, f32[6,16,128]{2,1,0:T(8,128)S(1)}, f32[2,16,128]{2,1,0:T(8,128)S(1)}, f32[3,16,128]{2,1,0:T(8,128)S(1)}, s3...) custom-call(f32[24,24]{1,0:T(8,128)S(1)} %copy-done.5, ...), custom_call_target="tpu_custom_call" | custom-call | flops 1000000 | bytes 1000000 | tf_op jit(solution)/shard_map/pallas_call | solution.py:308
  42.8 6.0 %all-to-all-done.table = f32[32,32,128]{2,1,0:T(8,128)S(1)} async-done(((f32[32,32,128]{2,1,0:T(8,128)}), f32[32,32,128]{2,1,0:T(8,128)S(1)}, u32[]{:S(2)}, u32[]{:S(2)}) %all-to-all-start) | async-done | bytes 524320 | tf_op jit(solution)/shard_map/all_to_all | solution.py:303
  48.8 0.3 shard_map.117
  49.1 0.0 collective-permute-start.4
  49.2 5.1 %collective-permute-start.5 = (f32[1,128]{1,0:T(1,128)S(1)}, f32[1,128]{1,0:T(1,128)S(1)}, u32[]{:S(2)}, u32[]{:S(2)}) collective-permute-start(f32[1,128]{1,0:T(1,128)S(1)} %get-tuple-element.43), channel_id=1, source_target_pairs={{1,0},{2,1},{3,2},{4,3},{5,4},{6,5},{7,6},{8,7},{9,8},{10,9},{11,1... | collective-permute-start | bytes 1544 | tf_op jit(solution)/shard_map/ppermute | solution.py:274
  54.3 1.1 %shard_map.118 = (f32[6,8,128]{2,1,0:T(8,128)S(1)}, f32[6,8,128]{2,1,0:T(8,128)S(1)}, f32[2,8,128]{2,1,0:T(8,128)S(1)}) custom-call(s32[8,128]{1,0:T(8,128)S(1)} %get-tuple-element.28.who, f32[24,24]{1,0:T(8,128)S(1)} %copy-done.5, f32[32,32,128]{2,1,0:T(8,128)S(1)} %all-to-all-done.table, s32[2,8,128]{2,1,0:T(8,128)S(1)} %copy-done.4, ...), custom_call_target="tpu_custom_call" | custom-call | flops 1000000 | bytes 1000000 | tf_op jit(solution)/shard_map/pallas_call | solution.py:330
  55.4 0.1 collective-permute-done.4.from_left
  55.5 0.1 collective-permute-done.5.from_right
  55.6 0.8 %shard_map.119 = (f32[3,2,8,128]{3,2,1,0:T(8,128)}, f32[3,2,8,128]{3,2,1,0:T(8,128)}) custom-call(f32[6,16,128]{2,1,0:T(8,128)S(1)} %get-tuple-element.35.dis, f32[6,8,128]{2,1,0:T(8,128)S(1)} %get-tuple-element.38.base_dis, f32[6,8,128]{2,1,0:T(8,128)S(1)} %get-tuple-element.39.base_vel, f32[2,8,128]{2,1,0:T(8,128)S(1)} %get-tuple-element.40.weight, ...), custom_call_target="tpu_custom_call" | custom-call | flops 1000000 | bytes 1000000 | tf_op jit(solution)/shard_map/pallas_call | solution.py:336
  (7 shorter events, 0.0 us)
Async XLA Ops:
  2.2 5.9 %collective-permute-start = (f32[32,128]{1,0:T(8,128)}, f32[32,128]{1,0:T(8,128)S(1)}, u32[]{:S(2)}, u32[]{:S(2)}) collective-permute-start(f32[32,128]{1,0:T(8,128)} %get-tuple-element.23), channel_id=1, source_target_pairs={{0,32},{32,64},{64,96},{96,128},{128,160},{160,192},{192,224},{224... | collective-permute-start | bytes 49160 | tf_op jit(solution)/shard_map/ppermute | solution.py:274
  5.6 8.0 %collective-permute-start.1 = (f32[32,128]{1,0:T(8,128)}, f32[32,128]{1,0:T(8,128)S(1)}, u32[]{:S(2)}, u32[]{:S(2)}) collective-permute-start(f32[32,128]{1,0:T(8,128)} %get-tuple-element.24), channel_id=1, source_target_pairs={{32,0},{64,32},{96,64},{128,96},{160,128},{192,160},{224,192},{256... | collective-permute-start | bytes 49160 | tf_op jit(solution)/shard_map/ppermute | solution.py:274
  13.5 0.7 %copy-start.7 = (f32[32,128]{1,0:T(8,128)S(1)}, f32[32,128]{1,0:T(8,128)}, u32[]{:S(2)}) copy-start(f32[32,128]{1,0:T(8,128)} %get-tuple-element.29.mine) | copy-start | bytes 49156
  15.3 20.8 %copy-start.1 = (f32[3,2,8,128]{3,2,1,0:T(8,128)S(1)}, f32[3,2,8,128]{3,2,1,0:T(8,128)}, u32[]{:S(2)}) copy-start(f32[3,2,8,128]{3,2,1,0:T(8,128)} %u.3) | copy-start | bytes 73732
  15.4 20.8 %copy-start.6 = (f32[2,8,128]{2,1,0:T(8,128)S(1)}, f32[2,8,128]{2,1,0:T(8,128)}, u32[]{:S(2)}) copy-start(f32[2,8,128]{2,1,0:T(8,128)} %mod.3) | copy-start | bytes 24580
  15.4 33.4 %all-to-all-start = ((f32[32,32,128]{2,1,0:T(8,128)}), f32[32,32,128]{2,1,0:T(8,128)S(1)}, u32[]{:S(2)}, u32[]{:S(2)}) async-start(f32[32,32,128]{2,1,0:T(8,128)} %shard_map.116), calls=%async_computation | async-start | bytes 1048576 | tf_op jit(solution)/shard_map/all_to_all | solution.py:303
  36.2 4.6 %copy-start = (f32[3,8,128]{2,1,0:T(8,128)S(1)}, f32[3,8,128]{2,1,0:T(8,128)}, u32[]{:S(2)}) copy-start(f32[3,8,128]{2,1,0:T(8,128)} %ref.5) | copy-start | bytes 36868
  36.2 4.6 %copy-start.2 = (f32[3,2,8,128]{3,2,1,0:T(8,128)S(1)}, f32[3,2,8,128]{3,2,1,0:T(8,128)}, u32[]{:S(2)}) copy-start(f32[3,2,8,128]{3,2,1,0:T(8,128)} %v.3) | copy-start | bytes 73732
  36.2 4.6 %copy-start.3 = (f32[2,8,128]{2,1,0:T(8,128)S(1)}, f32[2,8,128]{2,1,0:T(8,128)}, u32[]{:S(2)}) copy-start(f32[2,8,128]{2,1,0:T(8,128)} %mass.5) | copy-start | bytes 24580
  36.2 4.6 %copy-start.4 = (s32[2,8,128]{2,1,0:T(8,128)S(1)}, s32[2,8,128]{2,1,0:T(8,128)}, u32[]{:S(2)}) copy-start(s32[2,8,128]{2,1,0:T(8,128)} %pair.5) | copy-start | bytes 24580
  36.2 4.6 %copy-start.5 = (f32[24,24]{1,0:T(8,128)S(1)}, f32[24,24]{1,0:T(8,128)}, u32[]{:S(2)}) copy-start(f32[24,24]{1,0:T(8,128)} %stiff.3) | copy-start | bytes 6916
  36.3 4.4 %collective-permute-start.2 = (f32[1,128]{1,0:T(1,128)S(1)}, f32[1,128]{1,0:T(1,128)S(1)}, u32[]{:S(2)}, u32[]{:S(2)}) collective-permute-start(f32[1,128]{1,0:T(1,128)S(1)} %get-tuple-element.26), channel_id=1, source_target_pairs={{0,1},{1,2},{2,3},{3,4},{4,5},{5,6},{6,7},{7,8},{8,9},{9,10},{10,1... | collective-permute-start | bytes 1544 | tf_op jit(solution)/shard_map/ppermute | solution.py:274
  36.3 4.5 %copy-start.8 = (s32[2,1,1,8,1]{3,4,2,1,0:T(1,128)S(1)}, s32[2,1,1,8,1]{3,4,2,1,0:T(1,128)}, u32[]{:S(2)}) copy-start(s32[2,1,1,8,1]{3,4,2,1,0:T(1,128)} %param.18) | copy-start | bytes 196
  36.4 4.4 %collective-permute-start.3 = (f32[1,128]{1,0:T(1,128)S(1)}, f32[1,128]{1,0:T(1,128)S(1)}, u32[]{:S(2)}, u32[]{:S(2)}) collective-permute-start(f32[1,128]{1,0:T(1,128)S(1)} %get-tuple-element.27), channel_id=1, source_target_pairs={{1,0},{2,1},{3,2},{4,3},{5,4},{6,5},{7,6},{8,7},{9,8},{10,9},{11,1... | collective-permute-start | bytes 1544 | tf_op jit(solution)/shard_map/ppermute | solution.py:274
  49.1 6.4 %collective-permute-start.4 = (f32[1,128]{1,0:T(1,128)S(1)}, f32[1,128]{1,0:T(1,128)S(1)}, u32[]{:S(2)}, u32[]{:S(2)}) collective-permute-start(f32[1,128]{1,0:T(1,128)S(1)} %get-tuple-element.42), channel_id=1, source_target_pairs={{0,1},{1,2},{2,3},{3,4},{4,5},{5,6},{6,7},{7,8},{8,9},{9,10},{10,1... | collective-permute-start | bytes 1544 | tf_op jit(solution)/shard_map/ppermute | solution.py:274
  49.2 6.4 %collective-permute-start.5 = (f32[1,128]{1,0:T(1,128)S(1)}, f32[1,128]{1,0:T(1,128)S(1)}, u32[]{:S(2)}, u32[]{:S(2)}) collective-permute-start(f32[1,128]{1,0:T(1,128)S(1)} %get-tuple-element.43), channel_id=1, source_target_pairs={{1,0},{2,1},{3,2},{4,3},{5,4},{6,5},{7,6},{8,7},{9,8},{10,9},{11,1... | collective-permute-start | bytes 1544 | tf_op jit(solution)/shard_map/ppermute | solution.py:274

commit v4 on v3

--- a/solution.py
+++ b/solution.py
@@ -9,12 +9,11 @@
 F32 = jnp.float32
 VMEM = pl.BlockSpec(memory_space=pltpu.VMEM)
 HBM = pl.BlockSpec(memory_space=pltpu.HBM)
-ANY = pl.BlockSpec(memory_space=pl.ANY)
 SMEM = pl.BlockSpec(memory_space=pltpu.SMEM)
 ROWS = 8
 COLS = 128
 OWNERS = 32
-AT_U, AT_E, AT_V, AT_M, AT_X, AT_P, AT_O = 0, 12, 16, 22, 24, 27, 28
+AT_U, AT_E, AT_V, AT_M, AT_X, AT_P, AT_O, AT_L, AT_R = 0, 12, 16, 22, 24, 27, 28, 29, 30
 MSG = 32
 
 
@@ -26,23 +25,32 @@
     return lax.broadcasted_iota(jnp.int32, shape, len(shape) - 1)
 
 
-def fetched(sources, held, sems):
-    copies = [pltpu.make_async_copy(a, b, sems.at[n]) for n, (a, b) in enumerate(zip(sources, held))]
+def table_kernel(fac, pen, u, mod, table, left, right, fac_, pen_, u_, mod_, mine, square, sems, out_sems):
+    copies = [pltpu.make_async_copy(a, b, sems.at[n]) for n, (a, b) in enumerate(zip((fac, pen, u, mod), (fac_, pen_, u_, mod_)))]
     for copy in copies:
         copy.start()
     for copy in copies:
         copy.wait()
-    return held
-
-
-def pack_kernel(fac, pen, u, v, mass, mod, ref, pair, own, mine, up, down, *held):
-    fac, pen, u, v, mass, mod, ref, pair, own = fetched((fac, pen, u, v, mass, mod, ref, pair, own), held[:-1], held[-1])
-    root = jnp.sqrt(pen[...])
-    c, n = [[fac[8 * (m + at) : 8 * (m + at) + 8, :] for m in range(3)] for at in (0, 3)]
+    root = jnp.sqrt(pen_[...])
+    c, n = [[fac_[8 * (m + at) : 8 * (m + at) + 8, :] for m in range(3)] for at in (0, 3)]
     dist = n[0] * c[0] + n[1] * c[1] + n[2] * c[2]
     words = [root * n[0], root * n[1], root * n[2], root * dist]
     for q in range(4):
         mine[8 * q : 8 * q + 8, :] = jnp.concatenate([w[4 * h + q : 4 * h + q + 1, :] for h in range(2) for w in words], axis=0)
+    outs = [pltpu.make_async_copy(mine, table.at[o], out_sems.at[o]) for o in range(OWNERS)]
+    for copy in outs:
+        copy.start()
+    for ch in range(8):
+        square[16 * ch : 16 * ch + 8, :] = u_[ch // 2, ch % 2] if ch < 6 else mod_[ch - 6]
+        square[16 * ch + 8 : 16 * ch + 16, :] = jnp.zeros((8, COLS), F32)
+    turned = jnp.transpose(square[...])
+    left[...] = turned[0:1, :]
+    right[...] = turned[COLS - 1 : COLS, :]
+    for copy in outs:
+        copy.wait()
+
+
+def pack_kernel(u, v, mass, mod, ref, pair, own, from_left, from_right, up, down):
     for out, two, one in ((down, ROWS - 2, ROWS - 1), (up, 0, 0)):
         for m in range(3):
             for k in range(2):
@@ -56,27 +64,16 @@
         out[AT_P : AT_P + 1, :] = pair[0, one : one + 1, :].astype(F32)
         out[AT_O :, :] = jnp.zeros((MSG - AT_O, COLS), F32)
         out[AT_O : AT_O + 1, 0:ROWS] = own[0].astype(F32)
-
-
-def spread_kernel(mine, above, below, table, sems):
-    copies = [pltpu.make_async_copy(mine, table.at[o], sems.at[o]) for o in range(OWNERS)]
-    for copy in copies:
-        copy.start()
-    for copy in copies:
-        copy.wait()
-
-
-def extend_kernel(u, mod, above, below, ext, left, right):
-    for ch in range(8):
-        at = AT_U + 2 * ch if ch < 6 else AT_E + 2 * (ch - 6)
-        own = u[ch // 2, ch % 2] if ch < 6 else mod[ch - 6]
-        ext[16 * ch : 16 * ch + 2, :] = above[at : at + 2, :]
-        ext[16 * ch + 2 : 16 * ch + 10, :] = own
-        ext[16 * ch + 10 : 16 * ch + 12, :] = below[at : at + 2, :]
-        ext[16 * ch + 12 : 16 * ch + 16, :] = jnp.zeros((4, COLS), F32)
-    turned = jnp.transpose(ext[...])
-    left[...] = turned[0:1, :]
-    right[...] = turned[COLS - 1 : COLS, :]
+        out[AT_L : AT_L + 1, :] = from_left[...]
+        out[AT_R : AT_R + 1, :] = from_right[...]
+
+
+def extended(here, above, below):
+    here, above, below = [jnp.broadcast_to(x, (8, COLS)) for x in (here, above, below)]
+    at = lanes((8, COLS)) & 15
+    out = jnp.where(at < 12, pltpu.roll(below, 10, axis=1), 0.0)
+    out = jnp.where(at < 10, pltpu.roll(here, 2, axis=1), out)
+    return jnp.where(at < 2, pltpu.roll(above, COLS - 6, axis=1), out)[0:1]
 
 
 def edge_columns(from_left, from_right):
@@ -114,23 +111,29 @@
     return lambda k, i, m, c: stiff[3 * (4 * k + 2 * i + e) + m, c]
 
 
-def first_kernel(stiff, owner, ext, from_left, from_right, above, below, v, mass, ref, pair, vel, dis, weight, point, index, who, scale, spread, at_left, at_right, at_edge):
-    edges = edge_columns(from_left[...], from_right[...])
+def first_kernel(stiff, owner, spread, from_left, from_right, above, below, u, v, mass, mod, ref, pair, vel, dis, weight, point, index, who, scale, at_left, at_right, at_edge):
+    edges = edge_columns(
+        extended(from_left[...], above[AT_L : AT_L + 1, :], below[AT_L : AT_L + 1, :]),
+        extended(from_right[...], above[AT_R : AT_R + 1, :], below[AT_R : AT_R + 1, :]),
+    )
     zero = jnp.zeros((8, COLS), F32)
-    lane = lanes((ROWS, COLS))
-    for ch in range(6):
-        here, side = ext[16 * ch : 16 * ch + 16, :], edges[16 * ch : 16 * ch + 16, :]
-        at_left[ch, 0:16, :] = here
-        at_right[ch, 0:16, :] = with_columns(here, side)
+    lane = lanes((16, COLS))
+    for ch in range(8):
+        at = AT_U + 2 * ch if ch < 6 else AT_E + 2 * (ch - 6)
+        at_left[ch, 0:2, :] = above[at : at + 2, :]
+        at_left[ch, 2:10, :] = u[ch // 2, ch % 2] if ch < 6 else mod[ch - 6]
+        at_left[ch, 10:12, :] = below[at : at + 2, :]
+        at_left[ch, 12:16, :] = zero[:4]
+        side = edges[16 * ch : 16 * ch + 16, :]
+        at_right[ch, 0:16, :] = with_columns(at_left[ch, 0:16, :], side)
         at_edge[ch, 0:16, :] = side
         for buf in (at_left, at_right, at_edge):
             buf[ch, 16:24, :] = zero
-    here = ext[96:112, :] + ext[112:128, :]
-    side = edges[96:112, :] + edges[112:128, :]
-    right = with_columns(here, side)
+    here, right, side = [buf[6, 0:16, :] + buf[7, 0:16, :] for buf in (at_left, at_right, at_edge)]
     for n, both in enumerate((here + right, side + here)):
         scale[n, 0:16, :] = (both + pltpu.roll(both, 15, axis=0)) * 0.125
         scale[n, 16:24, :] = zero
+    scale[2] = jnp.where(lanes((24, COLS)) < 64, scale[1], scale[0])
     for k in range(2):
         weight[k, 0:1, :] = above[AT_M + k : AT_M + k + 1, :]
         weight[k, 1:9, :] = mass[k]
@@ -157,24 +160,39 @@
     who[1:2, :] = below[AT_O : AT_O + 1, :].astype(jnp.int32)
     for step in range(2):
         who[2 + step : 3 + step, 0:ROWS] = owner[step]
-    for at in (0, 8):
-        straight = element_sums(by_corner(stiff, 0), (at_left, at_right), 0, scale.at[0], at)
-        moved = element_sums(by_corner(stiff, 1), (at_left, at_right), 0, scale.at[0], at)
-        edge = element_sums(by_corner(stiff, 1), (at_edge, at_left), 0, scale.at[1], at)
-        for ch in range(6):
-            force = straight[ch] + jnp.where(lane == 0, edge[ch], pltpu.roll(moved[ch], 1, axis=1))
-            new = vel[ch, at : at + 8, :] - weight[ch % 2, at : at + 8, :] * force
-            vel[ch, at : at + 8, :] = new
-            dis[ch, at : at + 8, :] = at_left[ch, at + 1 : at + 9, :] + DT * new
-    row = lanes((1, COLS))
+    del spread
+    straight, moved, edge = {}, {}, {}
+    for i in range(2):
+        start = 1 - i
+        s_main, s_edge = [scale[n, start : start + 16, :] for n in range(2)]
+        for k in range(2):
+            for m in range(3):
+                sums = [None, None, None]
+                for c, ch, x, e in corners():
+                    rows = slice(start + x, start + x + 16)
+                    near = at_left[ch, rows, :]
+                    main, side = (at_right[ch, rows, :], near) if e else (near, at_edge[ch, rows, :])
+                    w0, w1 = [stiff[3 * (4 * k + 2 * i + end) + m, c] for end in range(2)]
+                    terms = (w0 * main, w1 * main, w1 * side)
+                    sums = [t if s is None else s + t for s, t in zip(sums, terms)]
+                for into, s, by in zip((straight, moved, edge), sums, (s_main, s_main, s_edge)):
+                    into[2 * m + k] = s * by if i == 0 else into[2 * m + k] + s * by
+    for ch in range(6):
+        force = straight[ch] + jnp.where(lane == 0, edge[ch], pltpu.roll(moved[ch], 1, axis=1))
+        new = vel[ch] - weight[ch % 2] * force
+        vel[ch] = new
+        dis[ch] = at_left[ch, 1:17, :] + DT * new
+
+
+def spread_kernel(stiff, spread):
+    lane = lanes((1, COLS))
     for k in range(2):
         for i in range(2):
             for m in range(3):
                 for c in range(24):
                     one, other = [stiff[3 * (4 * k + 2 * i + e) + m, c] for e in (1, 0)]
                     at = 24 * (6 * k + 3 * i + m) + c
-                    spread[at : at + 1, :] = jnp.where(row < 64, one, other)
-    scale[2] = jnp.where(lanes((24, COLS)) < 64, scale[1], scale[0])
+                    spread[at : at + 1, :] = jnp.where(lane < 64, one, other)
 
 
 def look_up(table, owner, index, row, out):
@@ -276,36 +294,26 @@
 
 def shards(u, v, mass, mod, stiff, ref, facets, penalty, owners, pair):
     width = facets.shape[-1]
-    buffers = [pltpu.VMEM((6, 24, COLS), F32)] * 3
     owner = owners.reshape(2, 1, ROWS)
-    sources = (
-        facets.reshape(6 * width // COLS, COLS),
-        penalty.reshape(width // COLS, COLS),
-        *(u, v, mass, mod, ref, pair, owner),
+    sources = (facets.reshape(6 * width // COLS, COLS), penalty.reshape(width // COLS, COLS), u, mod)
+    table, left, right = call(
+        table_kernel,
+        (struct(OWNERS, 32, COLS), struct(1, COLS), struct(1, COLS)),
+        [HBM] * 4,
+        [pltpu.VMEM(x.shape, x.dtype) for x in sources]
+        + [pltpu.VMEM((32, COLS), F32), pltpu.VMEM((128, COLS), F32)]
+        + [pltpu.SemaphoreType.DMA((n,)) for n in (4, OWNERS)],
+        room=60,
+        out_specs=(HBM, VMEM, VMEM),
+    )(*sources)
+    tables = lax.all_to_all(table, "mesh", split_axis=0, concat_axis=0, tiled=True)
+    from_left, from_right = swapped(right, left, "sub")
+    up, down = call(pack_kernel, (struct(MSG, COLS), struct(MSG, COLS)), [VMEM] * 9)(
+        u, v, mass, mod, ref, pair, owner, from_left, from_right
     )
-    mine, up, down = call(
-        pack_kernel,
-        (struct(32, COLS), struct(MSG, COLS), struct(MSG, COLS)),
-        [HBM] * len(sources),
-        [pltpu.VMEM(x.shape, x.dtype) for x in sources] + [pltpu.SemaphoreType.DMA((len(sources),))],
-        room=60,
-    )(*sources)
     above, below = swapped(down, up, "mesh")
-    table = call(
-        spread_kernel,
-        struct(OWNERS, 32, COLS),
-        [HBM, ANY, ANY],
-        [pltpu.SemaphoreType.DMA((OWNERS,))],
-        out_specs=HBM,
-        flops=0,
-        moved=0,
-    )(mine, above, below)
-    tables = lax.all_to_all(table, "mesh", split_axis=0, concat_axis=0, tiled=True)
-    ext, left, right = call(
-        extend_kernel, (struct(128, COLS), struct(1, COLS), struct(1, COLS)), [VMEM] * 4
-    )(u, mod, above, below)
-    from_left, from_right = swapped(right, left, "sub")
-    vel, dis, weight, point, index, who, scale, spread = call(
+    spread = call(spread_kernel, struct(288, COLS), [SMEM])(stiff)
+    vel, dis, weight, point, index, who, scale = call(
         first_kernel,
         (
             struct(6, 16, COLS),
@@ -315,11 +323,10 @@
             struct(16, COLS, dtype=jnp.int32),
             struct(8, COLS, dtype=jnp.int32),
             struct(3, 24, COLS),
-            struct(288, COLS),
         ),
-        [SMEM] + [VMEM] * 10,
-        buffers,
-    )(stiff, owner, ext, from_left, from_right, above, below, v, mass, ref, pair)
+        [SMEM] + [VMEM] * 12,
+        [pltpu.VMEM((8, 24, COLS), F32)] * 3,
+    )(stiff, owner, spread, from_left, from_right, above, below, u, v, mass, mod, ref, pair)
     new_vel, new_dis, left, right = call(
         contact_kernel,
         (struct(6, ROWS, COLS), struct(6, 16, COLS), struct(1, COLS), struct(1, COLS)),

time: 56.8 us -> 52 us (0.915)
  the two profiles are of different devices: /device:TPU:6 before, /device:TPU:30 now
where the time goes in v4:
time: 52 us; the launch traced here: 51.5 us
  starting transfers between devices  34.7 us (67%)
  waiting for transfers between devices  7.63 us (15%)
  Pallas kernels  7.06 us (14%)
  local copies, waits for them, and re-layouts  1.35 us (3%)
  between operations  0.82 us (2%)
    ppermute x6, starting transfers between devices, swapped(): return (lax.ppermute(to_next, axis, up), lax.ppermute(to_last, axis, down))  18.1 us
    all_to_all x1, starting transfers between devices, shards(): lax.all_to_all(table, 'mesh', split_axis=0, concat_axis=0, tiled=True)  16.6 us
    ppermute x6, waiting for transfers between devices, swapped(): return (lax.ppermute(to_next, axis, up), lax.ppermute(to_last, axis, down))  7.63 us
    pallas_call x1, Pallas kernels, shards(): call(table_kernel, (struct(OWNERS, 32, COLS), struct(1, COLS), struct(1,...  2.43 us
    pallas_call x1, Pallas kernels, shards(): call(first_kernel, (struct(6, 16, COLS), struct(6, 16, COLS), struct(2, 1...  1.5 us
    unnamed x20, local copies, waits for them, and re-layouts  1.35 us
    pallas_call x1, Pallas kernels, shards(): call(inner_kernel, (struct(6, ROWS, COLS), struct(6, ROWS, COLS), struct(...  1.07 us
  transfers between devices with their start and end apart: 7, of which 5 were waited for; matrix products, arithmetic and copies ran while one was open for 0% of the time, Pallas kernels for 7%

profile of v4, /device:TPU:30, one launch (start us, length us, event | category | flops | bytes accessed | tf_op | source)
XLA Modules:
  0.0 51.5 jit_solution(3336794499563074086)
XLA Ops:
  0.6 2.4 %shard_map.114 = (f32[32,32,128]{2,1,0:T(8,128)}, f32[1,128]{1,0:T(1,128)}, f32[1,128]{1,0:T(1,128)}) custom-call(f32[48,128]{1,0:T(8,128)} %bitcast.7, f32[8,128]{1,0:T(8,128)} %bitcast.8, f32[3,2,8,128]{3,2,1,0:T(8,128)} %u.5, f32[2,8,128]{2,1,0:T(8,128)} %mod.5), custom_call_target="tpu_custom_call" | custom-call | flops 1000000 | bytes 1000000 | tf_op jit(solution)/shard_map/pallas_call | solution.py:299
  3.1 0.0 copy-start
  3.1 0.0 copy-start.2
  3.1 0.0 copy-start.3
  3.1 0.0 copy-start.4
  3.1 0.0 copy-start.5
  3.1 0.0 copy-start.6
  3.1 16.6 %all-to-all-start = ((f32[32,32,128]{2,1,0:T(8,128)}), f32[32,32,128]{2,1,0:T(8,128)S(1)}, u32[]{:S(2)}, u32[]{:S(2)}) async-start(f32[32,32,128]{2,1,0:T(8,128)} %get-tuple-element.26), calls=%async_computation | async-start | bytes 1048576 | tf_op jit(solution)/shard_map/all_to_all | solution.py:309
  19.7 0.0 copy-start.9
  19.7 0.6 %copy-done.9 = f32[1,128]{1,0:T(1,128)S(1)} copy-done((f32[1,128]{1,0:T(1,128)S(1)}, f32[1,128]{1,0:T(1,128)}, u32[]{:S(2)}) %copy-start.9) | copy-done | bytes 536
  20.4 0.0 collective-permute-start
  20.4 0.7 %copy-done.8 = f32[1,128]{1,0:T(1,128)S(1)} copy-done((f32[1,128]{1,0:T(1,128)S(1)}, f32[1,128]{1,0:T(1,128)}, u32[]{:S(2)}) %copy-start.8) | copy-done | bytes 536
  21.0 8.6 %collective-permute-start.1 = (f32[1,128]{1,0:T(1,128)S(1)}, f32[1,128]{1,0:T(1,128)S(1)}, u32[]{:S(2)}, u32[]{:S(2)}) collective-permute-start(f32[1,128]{1,0:T(1,128)S(1)} %copy-done.8), channel_id=1, source_target_pairs={{1,0},{2,1},{3,2},{4,3},{5,4},{6,5},{7,6},{8,7},{9,8},{10,9},{11,1... | collective-permute-start | bytes 1544 | tf_op jit(solution)/shard_map/ppermute | solution.py:292
  29.7 0.6 %collective-permute-done.from_left = f32[1,128]{1,0:T(1,128)S(1)} collective-permute-done((f32[1,128]{1,0:T(1,128)S(1)}, f32[1,128]{1,0:T(1,128)S(1)}, u32[]{:S(2)}, u32[]{:S(2)}) %collective-permute-start) | collective-permute-done | bytes 544 | tf_op jit(solution)/shard_map/ppermute | solution.py:292
  30.2 0.7 %collective-permute-done.1.from_right = f32[1,128]{1,0:T(1,128)S(1)} collective-permute-done((f32[1,128]{1,0:T(1,128)S(1)}, f32[1,128]{1,0:T(1,128)S(1)}, u32[]{:S(2)}, u32[]{:S(2)}) %collective-permute-start.1) | collective-permute-done | bytes 544 | tf_op jit(solution)/shard_map/ppermute | solution.py:292
  31.0 0.0 copy-done.4
  31.0 0.0 copy-done.5
  31.0 0.0 copy-start.1
  31.0 4.6 %collective-permute-start.2 = (f32[32,128]{1,0:T(8,128)S(1)}, f32[32,128]{1,0:T(8,128)S(1)}, u32[]{:S(2)}, u32[]{:S(2)}) collective-permute-start(f32[32,128]{1,0:T(8,128)S(1)} %get-tuple-element.23), channel_id=1, source_target_pairs={{0,32},{32,64},{64,96},{96,128},{128,160},{160,192},{192,224},{224... | collective-permute-start | bytes 49160 | tf_op jit(solution)/shard_map/ppermute | solution.py:292
  35.6 1.9 %collective-permute-start.3 = (f32[32,128]{1,0:T(8,128)S(1)}, f32[32,128]{1,0:T(8,128)S(1)}, u32[]{:S(2)}, u32[]{:S(2)}) collective-permute-start(f32[32,128]{1,0:T(8,128)S(1)} %get-tuple-element.24), channel_id=1, source_target_pairs={{32,0},{64,32},{96,64},{128,96},{160,128},{192,160},{224,192},{256... | collective-permute-start | bytes 49160 | tf_op jit(solution)/shard_map/ppermute | solution.py:292
  37.6 0.9 %shard_map.113.spread = f32[288,128]{1,0:T(8,128)S(1)} custom-call(f32[24,24]{1,0:T(8,128)S(1)} %copy-done.1), custom_call_target="tpu_custom_call" | custom-call | flops 1000000 | bytes 1000000 | tf_op jit(solution)/shard_map/pallas_call | solution.py:315
  38.5 0.0 collective-permute-done.2.above
  38.5 6.1 %collective-permute-done.3.below = f32[32,128]{1,0:T(8,128)S(1)} collective-permute-done((f32[32,128]{1,0:T(8,128)S(1)}, f32[32,128]{1,0:T(8,128)S(1)}, u32[]{:S(2)}, u32[]{:S(2)}) %collective-permute-start.3) | collective-permute-done | bytes 16416 | tf_op jit(solution)/shard_map/ppermute | solution.py:292
  44.6 1.5 %shard_map.116 = (f32[6,16,128]{2,1,0:T(8,128)S(1)}, f32[6,16,128]{2,1,0:T(8,128)S(1)}, f32[2,16,128]{2,1,0:T(8,128)S(1)}, f32[3,16,128]{2,1,0:T(8,128)S(1)}, s3...) custom-call(f32[24,24]{1,0:T(8,128)S(1)} %copy-done.1, s32[2,1,8]{2,1,0:T(1,128)S(1)} %bitcast.6, ...), custom_call_target="tpu_custom_call" | custom-call | flops 1000000 | bytes 1000000 | tf_op jit(solution)/shard_map/pallas_call | solution.py:316
  46.1 0.0 all-to-all-done.table
  46.1 0.3 shard_map.117
  46.5 0.0 collective-permute-start.4
  46.5 3.0 %collective-permute-start.5 = (f32[1,128]{1,0:T(1,128)S(1)}, f32[1,128]{1,0:T(1,128)S(1)}, u32[]{:S(2)}, u32[]{:S(2)}) collective-permute-start(f32[1,128]{1,0:T(1,128)S(1)} %get-tuple-element.39), channel_id=1, source_target_pairs={{1,0},{2,1},{3,2},{4,3},{5,4},{6,5},{7,6},{8,7},{9,8},{10,9},{11,1... | collective-permute-start | bytes 1544 | tf_op jit(solution)/shard_map/ppermute | solution.py:292
  49.4 1.1 %shard_map.118 = (f32[6,8,128]{2,1,0:T(8,128)S(1)}, f32[6,8,128]{2,1,0:T(8,128)S(1)}, f32[2,8,128]{2,1,0:T(8,128)S(1)}) custom-call(s32[8,128]{1,0:T(8,128)S(1)} %get-tuple-element.25.who, f32[24,24]{1,0:T(8,128)S(1)} %copy-done.1, f32[32,32,128]{2,1,0:T(8,128)S(1)} %all-to-all-done.table, s32[2,8,128]{2,1,0:T(8,128)S(1)} %copy-done.5, ...), custom_call_target="tpu_custom_call" | custom-call | flops 1000000 | bytes 1000000 | tf_op jit(solution)/shard_map/pallas_call | solution.py:337
  50.5 0.1 collective-permute-done.4.from_left
  50.7 0.1 collective-permute-done.5.from_right
  50.7 0.8 %shard_map.119 = (f32[3,2,8,128]{3,2,1,0:T(8,128)}, f32[3,2,8,128]{3,2,1,0:T(8,128)}) custom-call(f32[6,16,128]{2,1,0:T(8,128)S(1)} %get-tuple-element.32.dis, f32[6,8,128]{2,1,0:T(8,128)S(1)} %get-tuple-element.35.base_dis, f32[6,8,128]{2,1,0:T(8,128)S(1)} %get-tuple-element.36.base_vel, f32[2,8,128]{2,1,0:T(8,128)S(1)} %get-tuple-element.37.weight, ...), custom_call_target="tpu_custom_call" | custom-call | flops 1000000 | bytes 1000000 | tf_op jit(solution)/shard_map/pallas_call | solution.py:343
  (9 shorter events, 0.0 us)
Async XLA Ops:
  3.1 27.9 %copy-start = (f32[3,2,8,128]{3,2,1,0:T(8,128)S(1)}, f32[3,2,8,128]{3,2,1,0:T(8,128)}, u32[]{:S(2)}) copy-start(f32[3,2,8,128]{3,2,1,0:T(8,128)} %u.5) | copy-start | bytes 73732
  3.1 27.9 %copy-start.2 = (f32[3,8,128]{2,1,0:T(8,128)S(1)}, f32[3,8,128]{2,1,0:T(8,128)}, u32[]{:S(2)}) copy-start(f32[3,8,128]{2,1,0:T(8,128)} %ref.5) | copy-start | bytes 36868
  3.1 27.9 %copy-start.3 = (f32[3,2,8,128]{3,2,1,0:T(8,128)S(1)}, f32[3,2,8,128]{3,2,1,0:T(8,128)}, u32[]{:S(2)}) copy-start(f32[3,2,8,128]{3,2,1,0:T(8,128)} %v.3) | copy-start | bytes 73732
  3.1 27.9 %copy-start.4 = (f32[2,8,128]{2,1,0:T(8,128)S(1)}, f32[2,8,128]{2,1,0:T(8,128)}, u32[]{:S(2)}) copy-start(f32[2,8,128]{2,1,0:T(8,128)} %mass.5) | copy-start | bytes 24580
  3.1 27.9 %copy-start.5 = (s32[2,8,128]{2,1,0:T(8,128)S(1)}, s32[2,8,128]{2,1,0:T(8,128)}, u32[]{:S(2)}) copy-start(s32[2,8,128]{2,1,0:T(8,128)} %pair.5) | copy-start | bytes 24580
  3.1 27.9 %copy-start.6 = (f32[2,8,128]{2,1,0:T(8,128)S(1)}, f32[2,8,128]{2,1,0:T(8,128)}, u32[]{:S(2)}) copy-start(f32[2,8,128]{2,1,0:T(8,128)} %mod.5) | copy-start | bytes 24580
  3.1 42.9 %all-to-all-start = ((f32[32,32,128]{2,1,0:T(8,128)}), f32[32,32,128]{2,1,0:T(8,128)S(1)}, u32[]{:S(2)}, u32[]{:S(2)}) async-start(f32[32,32,128]{2,1,0:T(8,128)} %get-tuple-element.26), calls=%async_computation | async-start | bytes 1048576 | tf_op jit(solution)/shard_map/all_to_all | solution.py:309
  19.7 0.7 %copy-start.9 = (f32[1,128]{1,0:T(1,128)S(1)}, f32[1,128]{1,0:T(1,128)}, u32[]{:S(2)}) copy-start(f32[1,128]{1,0:T(1,128)} %get-tuple-element.21) | copy-start | bytes 1540
  20.4 0.7 %copy-start.8 = (f32[1,128]{1,0:T(1,128)S(1)}, f32[1,128]{1,0:T(1,128)}, u32[]{:S(2)}) copy-start(f32[1,128]{1,0:T(1,128)} %get-tuple-element.22) | copy-start | bytes 1540
  20.4 9.9 %collective-permute-start = (f32[1,128]{1,0:T(1,128)S(1)}, f32[1,128]{1,0:T(1,128)S(1)}, u32[]{:S(2)}, u32[]{:S(2)}) collective-permute-start(f32[1,128]{1,0:T(1,128)S(1)} %copy-done.9), channel_id=1, source_target_pairs={{0,1},{1,2},{2,3},{3,4},{4,5},{5,6},{6,7},{7,8},{8,9},{9,10},{10,1... | collective-permute-start | bytes 1544 | tf_op jit(solution)/shard_map/ppermute | solution.py:292
  21.0 10.0 %copy-start.7 = (s32[2,1,1,8,1]{3,4,2,1,0:T(1,128)S(1)}, s32[2,1,1,8,1]{3,4,2,1,0:T(1,128)}, u32[]{:S(2)}) copy-start(s32[2,1,1,8,1]{3,4,2,1,0:T(1,128)} %param.18) | copy-start | bytes 196
  21.0 9.9 %collective-permute-start.1 = (f32[1,128]{1,0:T(1,128)S(1)}, f32[1,128]{1,0:T(1,128)S(1)}, u32[]{:S(2)}, u32[]{:S(2)}) collective-permute-start(f32[1,128]{1,0:T(1,128)S(1)} %copy-done.8), channel_id=1, source_target_pairs={{1,0},{2,1},{3,2},{4,3},{5,4},{6,5},{7,6},{8,7},{9,8},{10,9},{11,1... | collective-permute-start | bytes 1544 | tf_op jit(solution)/shard_map/ppermute | solution.py:292
  31.0 6.6 %copy-start.1 = (f32[24,24]{1,0:T(8,128)S(1)}, f32[24,24]{1,0:T(8,128)}, u32[]{:S(2)}) copy-start(f32[24,24]{1,0:T(8,128)} %stiff.5) | copy-start | bytes 6916
  31.0 7.4 %collective-permute-start.2 = (f32[32,128]{1,0:T(8,128)S(1)}, f32[32,128]{1,0:T(8,128)S(1)}, u32[]{:S(2)}, u32[]{:S(2)}) collective-permute-start(f32[32,128]{1,0:T(8,128)S(1)} %get-tuple-element.23), channel_id=1, source_target_pairs={{0,32},{32,64},{64,96},{96,128},{128,160},{160,192},{192,224},{224... | collective-permute-start | bytes 49160 | tf_op jit(solution)/shard_map/ppermute | solution.py:292
  35.6 9.0 %collective-permute-start.3 = (f32[32,128]{1,0:T(8,128)S(1)}, f32[32,128]{1,0:T(8,128)S(1)}, u32[]{:S(2)}, u32[]{:S(2)}) collective-permute-start(f32[32,128]{1,0:T(8,128)S(1)} %get-tuple-element.24), channel_id=1, source_target_pairs={{32,0},{64,32},{96,64},{128,96},{160,128},{192,160},{224,192},{256... | collective-permute-start | bytes 49160 | tf_op jit(solution)/shard_map/ppermute | solution.py:292
  46.5 4.2 %collective-permute-start.4 = (f32[1,128]{1,0:T(1,128)S(1)}, f32[1,128]{1,0:T(1,128)S(1)}, u32[]{:S(2)}, u32[]{:S(2)}) collective-permute-start(f32[1,128]{1,0:T(1,128)S(1)} %get-tuple-element.38), channel_id=1, source_target_pairs={{0,1},{1,2},{2,3},{3,4},{4,5},{5,6},{6,7},{7,8},{8,9},{9,10},{10,1... | collective-permute-start | bytes 1544 | tf_op jit(solution)/shard_map/ppermute | solution.py:292
  46.5 4.3 %collective-permute-start.5 = (f32[1,128]{1,0:T(1,128)S(1)}, f32[1,128]{1,0:T(1,128)S(1)}, u32[]{:S(2)}, u32[]{:S(2)}) collective-permute-start(f32[1,128]{1,0:T(1,128)S(1)} %get-tuple-element.39), channel_id=1, source_target_pairs={{1,0},{2,1},{3,2},{4,3},{5,4},{6,5},{7,6},{8,7},{9,8},{10,9},{11,1... | collective-permute-start | bytes 1544 | tf_op jit(solution)/shard_map/ppermute | solution.py:292

commit v5 on v4

--- a/solution.py
+++ b/solution.py
@@ -13,6 +13,7 @@
 ROWS = 8
 COLS = 128
 OWNERS = 32
+REPLICAS = 8
 AT_U, AT_E, AT_V, AT_M, AT_X, AT_P, AT_O, AT_L, AT_R = 0, 12, 16, 22, 24, 27, 28, 29, 30
 MSG = 32
 
@@ -25,8 +26,8 @@
     return lax.broadcasted_iota(jnp.int32, shape, len(shape) - 1)
 
 
-def table_kernel(fac, pen, u, mod, table, left, right, fac_, pen_, u_, mod_, mine, square, sems, out_sems):
-    copies = [pltpu.make_async_copy(a, b, sems.at[n]) for n, (a, b) in enumerate(zip((fac, pen, u, mod), (fac_, pen_, u_, mod_)))]
+def table_kernel(fac, pen, table, fac_, pen_, mine, sems, out_sems):
+    copies = [pltpu.make_async_copy(a, b, sems.at[n]) for n, (a, b) in enumerate(((fac, fac_), (pen, pen_)))]
     for copy in copies:
         copy.start()
     for copy in copies:
@@ -36,18 +37,23 @@
     dist = n[0] * c[0] + n[1] * c[1] + n[2] * c[2]
     words = [root * n[0], root * n[1], root * n[2], root * dist]
     for q in range(4):
-        mine[8 * q : 8 * q + 8, :] = jnp.concatenate([w[4 * h + q : 4 * h + q + 1, :] for h in range(2) for w in words], axis=0)
-    outs = [pltpu.make_async_copy(mine, table.at[o], out_sems.at[o]) for o in range(OWNERS)]
+        tile = jnp.concatenate([w[4 * h + q : 4 * h + q + 1, :] for h in range(2) for w in words], axis=0)
+        for r in range(REPLICAS):
+            mine[r, 8 * q : 8 * q + 8, :] = tile
+    outs = [pltpu.make_async_copy(mine, table.at[pl.ds(o * REPLICAS, REPLICAS)], out_sems.at[o]) for o in range(OWNERS // REPLICAS)]
     for copy in outs:
         copy.start()
+    for copy in outs:
+        copy.wait()
+
+
+def columns_kernel(u, mod, left, right, square):
     for ch in range(8):
-        square[16 * ch : 16 * ch + 8, :] = u_[ch // 2, ch % 2] if ch < 6 else mod_[ch - 6]
+        square[16 * ch : 16 * ch + 8, :] = u[ch // 2, ch % 2] if ch < 6 else mod[ch - 6]
         square[16 * ch + 8 : 16 * ch + 16, :] = jnp.zeros((8, COLS), F32)
     turned = jnp.transpose(square[...])
     left[...] = turned[0:1, :]
     right[...] = turned[COLS - 1 : COLS, :]
-    for copy in outs:
-        copy.wait()
 
 
 def pack_kernel(u, v, mass, mod, ref, pair, own, from_left, from_right, up, down):
@@ -295,17 +301,20 @@
 def shards(u, v, mass, mod, stiff, ref, facets, penalty, owners, pair):
     width = facets.shape[-1]
     owner = owners.reshape(2, 1, ROWS)
-    sources = (facets.reshape(6 * width // COLS, COLS), penalty.reshape(width // COLS, COLS), u, mod)
-    table, left, right = call(
+    sources = (facets.reshape(6 * width // COLS, COLS), penalty.reshape(width // COLS, COLS))
+    table = call(
         table_kernel,
-        (struct(OWNERS, 32, COLS), struct(1, COLS), struct(1, COLS)),
-        [HBM] * 4,
+        struct(OWNERS, 32, COLS),
+        [HBM] * 2,
         [pltpu.VMEM(x.shape, x.dtype) for x in sources]
-        + [pltpu.VMEM((32, COLS), F32), pltpu.VMEM((128, COLS), F32)]
-        + [pltpu.SemaphoreType.DMA((n,)) for n in (4, OWNERS)],
+        + [pltpu.VMEM((REPLICAS, 32, COLS), F32)]
+        + [pltpu.SemaphoreType.DMA((n,)) for n in (2, OWNERS // REPLICAS)],
         room=60,
-        out_specs=(HBM, VMEM, VMEM),
+        out_specs=HBM,
     )(*sources)
+    left, right = call(
+        columns_kernel, (struct(1, COLS), struct(1, COLS)), [VMEM] * 2, [pltpu.VMEM((128, COLS), F32)]
+    )(u, mod)
     tables = lax.all_to_all(table, "mesh", split_axis=0, concat_axis=0, tiled=True)
     from_left, from_right = swapped(right, left, "sub")
     up, down = call(pack_kernel, (struct(MSG, COLS), struct(MSG, COLS)), [VMEM] * 9)(

time: 52 us -> 49.9 us (0.960)
  local copies, waits for them, and re-layouts: 1.35 us -> 0.05 us
  Pallas kernels: 7.06 us -> 6.29 us
    unnamed x20 -> x16, local copies, waits for them, and re-layouts: 1.35 us -> 0.05 us
    pallas_call x1 -> x2, Pallas kernels: 2.43 us -> 1.66 us  [the longest x1 1.6 us: shards(): call(table_kernel, struct(OWNERS, 32, COLS), [HBM] * 2, [pltpu.VMEM(x.sha...]
where the time goes in v5:
time: 49.9 us; the launch traced here: 49.5 us
  starting transfers between devices  34.7 us (70%)
  waiting for transfers between devices  7.63 us (15%)
  Pallas kernels  6.29 us (13%)
  between operations  0.84 us (2%)
    ppermute x6, starting transfers between devices, swapped(): return (lax.ppermute(to_next, axis, up), lax.ppermute(to_last, axis, down))  18.1 us
    all_to_all x1, starting transfers between devices, shards(): lax.all_to_all(table, 'mesh', split_axis=0, concat_axis=0, tiled=True)  16.6 us
    ppermute x6, waiting for transfers between devices, swapped(): return (lax.ppermute(to_next, axis, up), lax.ppermute(to_last, axis, down))  7.63 us
    pallas_call x1, Pallas kernels, shards(): call(table_kernel, struct(OWNERS, 32, COLS), [HBM] * 2, [pltpu.VMEM(x.sha...  1.6 us
    pallas_call x1, Pallas kernels, shards(): call(first_kernel, (struct(6, 16, COLS), struct(6, 16, COLS), struct(2, 1...  1.5 us
    pallas_call x1, Pallas kernels, shards(): call(inner_kernel, (struct(6, ROWS, COLS), struct(6, ROWS, COLS), struct(...  1.07 us
  transfers between devices with their start and end apart: 7, of which 5 were waited for; matrix products, arithmetic and copies ran while one was open for 0% of the time, Pallas kernels for 7%

profile of v5, /device:TPU:30, one launch (start us, length us, event | category | flops | bytes accessed | tf_op | source)
XLA Modules:
  0.0 49.5 jit_solution(11327341153251647951)
XLA Ops:
  0.6 1.6 %shard_map.117 = f32[32,32,128]{2,1,0:T(8,128)} custom-call(f32[48,128]{1,0:T(8,128)} %bitcast.7, f32[8,128]{1,0:T(8,128)} %bitcast.8), custom_call_target="tpu_custom_call" | custom-call | flops 1000000 | bytes 1000000 | tf_op jit(solution)/shard_map/pallas_call | solution.py:305
  2.2 0.0 copy-start
  2.3 0.0 copy-start.6
  2.3 0.0 copy-start.4
  2.3 0.0 copy-start.5
  2.3 16.6 %all-to-all-start = ((f32[32,32,128]{2,1,0:T(8,128)}), f32[32,32,128]{2,1,0:T(8,128)S(1)}, u32[]{:S(2)}, u32[]{:S(2)}) async-start(f32[32,32,128]{2,1,0:T(8,128)} %shard_map.117), calls=%async_computation | async-start | bytes 1048576 | tf_op jit(solution)/shard_map/all_to_all | solution.py:318
  18.9 0.0 copy-done
  18.9 0.0 copy-start.2
  18.9 0.0 copy-start.3
  18.9 0.1 shard_map.114
  19.0 0.0 collective-permute-start
  19.0 0.0 copy-start.7
  19.0 8.6 %collective-permute-start.1 = (f32[1,128]{1,0:T(1,128)S(1)}, f32[1,128]{1,0:T(1,128)S(1)}, u32[]{:S(2)}, u32[]{:S(2)}) collective-permute-start(f32[1,128]{1,0:T(1,128)S(1)} %get-tuple-element.21), channel_id=1, source_target_pairs={{1,0},{2,1},{3,2},{4,3},{5,4},{6,5},{7,6},{8,7},{9,8},{10,9},{11,1... | collective-permute-start | bytes 1544 | tf_op jit(solution)/shard_map/ppermute | solution.py:298
  27.7 1.2 %collective-permute-done.from_left = f32[1,128]{1,0:T(1,128)S(1)} collective-permute-done((f32[1,128]{1,0:T(1,128)S(1)}, f32[1,128]{1,0:T(1,128)S(1)}, u32[]{:S(2)}, u32[]{:S(2)}) %collective-permute-start) | collective-permute-done | bytes 544 | tf_op jit(solution)/shard_map/ppermute | solution.py:298
  28.9 0.1 collective-permute-done.1.from_right
  29.0 0.0 copy-done.5
  29.0 0.0 copy-start.1
  29.0 4.6 %collective-permute-start.2 = (f32[32,128]{1,0:T(8,128)S(1)}, f32[32,128]{1,0:T(8,128)S(1)}, u32[]{:S(2)}, u32[]{:S(2)}) collective-permute-start(f32[32,128]{1,0:T(8,128)S(1)} %get-tuple-element.22), channel_id=1, source_target_pairs={{0,32},{32,64},{64,96},{96,128},{128,160},{160,192},{192,224},{224... | collective-permute-start | bytes 49160 | tf_op jit(solution)/shard_map/ppermute | solution.py:298
  33.6 1.9 %collective-permute-start.3 = (f32[32,128]{1,0:T(8,128)S(1)}, f32[32,128]{1,0:T(8,128)S(1)}, u32[]{:S(2)}, u32[]{:S(2)}) collective-permute-start(f32[32,128]{1,0:T(8,128)S(1)} %get-tuple-element.23), channel_id=1, source_target_pairs={{32,0},{64,32},{96,64},{128,96},{160,128},{192,160},{224,192},{256... | collective-permute-start | bytes 49160 | tf_op jit(solution)/shard_map/ppermute | solution.py:298
  35.5 0.0 copy-done.1
  35.6 0.9 %shard_map.113.spread = f32[288,128]{1,0:T(8,128)S(1)} custom-call(f32[24,24]{1,0:T(8,128)S(1)} %copy-done.1), custom_call_target="tpu_custom_call" | custom-call | flops 1000000 | bytes 1000000 | tf_op jit(solution)/shard_map/pallas_call | solution.py:324
  36.5 0.0 collective-permute-done.2.above
  36.5 6.1 %collective-permute-done.3.below = f32[32,128]{1,0:T(8,128)S(1)} collective-permute-done((f32[32,128]{1,0:T(8,128)S(1)}, f32[32,128]{1,0:T(8,128)S(1)}, u32[]{:S(2)}, u32[]{:S(2)}) %collective-permute-start.3) | collective-permute-done | bytes 16416 | tf_op jit(solution)/shard_map/ppermute | solution.py:298
  42.6 1.5 %shard_map.116 = (f32[6,16,128]{2,1,0:T(8,128)S(1)}, f32[6,16,128]{2,1,0:T(8,128)S(1)}, f32[2,16,128]{2,1,0:T(8,128)S(1)}, f32[3,16,128]{2,1,0:T(8,128)S(1)}, s3...) custom-call(f32[24,24]{1,0:T(8,128)S(1)} %copy-done.1, s32[2,1,8]{2,1,0:T(1,128)S(1)} %bitcast.6, ...), custom_call_target="tpu_custom_call" | custom-call | flops 1000000 | bytes 1000000 | tf_op jit(solution)/shard_map/pallas_call | solution.py:325
  44.1 0.0 all-to-all-done.table
  44.1 0.3 shard_map.118
  44.4 0.0 collective-permute-start.4
  44.5 3.0 %collective-permute-start.5 = (f32[1,128]{1,0:T(1,128)S(1)}, f32[1,128]{1,0:T(1,128)S(1)}, u32[]{:S(2)}, u32[]{:S(2)}) collective-permute-start(f32[1,128]{1,0:T(1,128)S(1)} %get-tuple-element.37), channel_id=1, source_target_pairs={{1,0},{2,1},{3,2},{4,3},{5,4},{6,5},{7,6},{8,7},{9,8},{10,9},{11,1... | collective-permute-start | bytes 1544 | tf_op jit(solution)/shard_map/ppermute | solution.py:298
  47.4 1.1 %shard_map.119 = (f32[6,8,128]{2,1,0:T(8,128)S(1)}, f32[6,8,128]{2,1,0:T(8,128)S(1)}, f32[2,8,128]{2,1,0:T(8,128)S(1)}) custom-call(s32[8,128]{1,0:T(8,128)S(1)} %get-tuple-element.24.who, f32[24,24]{1,0:T(8,128)S(1)} %copy-done.1, f32[32,32,128]{2,1,0:T(8,128)S(1)} %all-to-all-done.table, s32[2,8,128]{2,1,0:T(8,128)S(1)} %copy-done.5, ...), custom_call_target="tpu_custom_call" | custom-call | flops 1000000 | bytes 1000000 | tf_op jit(solution)/shard_map/pallas_call | solution.py:346
  48.5 0.2 collective-permute-done.4.from_left
  48.6 0.1 collective-permute-done.5.from_right
  48.7 0.8 %shard_map.120 = (f32[3,2,8,128]{3,2,1,0:T(8,128)}, f32[3,2,8,128]{3,2,1,0:T(8,128)}) custom-call(f32[6,16,128]{2,1,0:T(8,128)S(1)} %get-tuple-element.30.dis, f32[6,8,128]{2,1,0:T(8,128)S(1)} %get-tuple-element.33.base_dis, f32[6,8,128]{2,1,0:T(8,128)S(1)} %get-tuple-element.34.base_vel, f32[2,8,128]{2,1,0:T(8,128)S(1)} %get-tuple-element.35.weight, ...), custom_call_target="tpu_custom_call" | custom-call | flops 1000000 | bytes 1000000 | tf_op jit(solution)/shard_map/pallas_call | solution.py:352
  (6 shorter events, 0.0 us)
Async XLA Ops:
  2.2 16.6 %copy-start = (f32[3,2,8,128]{3,2,1,0:T(8,128)S(1)}, f32[3,2,8,128]{3,2,1,0:T(8,128)}, u32[]{:S(2)}) copy-start(f32[3,2,8,128]{3,2,1,0:T(8,128)} %u.5) | copy-start | bytes 73732
  2.3 16.6 %copy-start.6 = (f32[2,8,128]{2,1,0:T(8,128)S(1)}, f32[2,8,128]{2,1,0:T(8,128)}, u32[]{:S(2)}) copy-start(f32[2,8,128]{2,1,0:T(8,128)} %mod.5) | copy-start | bytes 24580
  2.3 26.7 %copy-start.4 = (f32[2,8,128]{2,1,0:T(8,128)S(1)}, f32[2,8,128]{2,1,0:T(8,128)}, u32[]{:S(2)}) copy-start(f32[2,8,128]{2,1,0:T(8,128)} %mass.5) | copy-start | bytes 24580
  2.3 26.7 %copy-start.5 = (s32[2,8,128]{2,1,0:T(8,128)S(1)}, s32[2,8,128]{2,1,0:T(8,128)}, u32[]{:S(2)}) copy-start(s32[2,8,128]{2,1,0:T(8,128)} %pair.5) | copy-start | bytes 24580
  2.3 41.8 %all-to-all-start = ((f32[32,32,128]{2,1,0:T(8,128)}), f32[32,32,128]{2,1,0:T(8,128)S(1)}, u32[]{:S(2)}, u32[]{:S(2)}) async-start(f32[32,32,128]{2,1,0:T(8,128)} %shard_map.117), calls=%async_computation | async-start | bytes 1048576 | tf_op jit(solution)/shard_map/all_to_all | solution.py:318
  18.9 10.1 %copy-start.2 = (f32[3,8,128]{2,1,0:T(8,128)S(1)}, f32[3,8,128]{2,1,0:T(8,128)}, u32[]{:S(2)}) copy-start(f32[3,8,128]{2,1,0:T(8,128)} %ref.5) | copy-start | bytes 36868
  18.9 10.1 %copy-start.3 = (f32[3,2,8,128]{3,2,1,0:T(8,128)S(1)}, f32[3,2,8,128]{3,2,1,0:T(8,128)}, u32[]{:S(2)}) copy-start(f32[3,2,8,128]{3,2,1,0:T(8,128)} %v.3) | copy-start | bytes 73732
  19.0 9.9 %collective-permute-start = (f32[1,128]{1,0:T(1,128)S(1)}, f32[1,128]{1,0:T(1,128)S(1)}, u32[]{:S(2)}, u32[]{:S(2)}) collective-permute-start(f32[1,128]{1,0:T(1,128)S(1)} %get-tuple-element.20), channel_id=1, source_target_pairs={{0,1},{1,2},{2,3},{3,4},{4,5},{5,6},{6,7},{7,8},{8,9},{9,10},{10,1... | collective-permute-start | bytes 1544 | tf_op jit(solution)/shard_map/ppermute | solution.py:298
  19.0 10.0 %copy-start.7 = (s32[2,1,1,8,1]{3,4,2,1,0:T(1,128)S(1)}, s32[2,1,1,8,1]{3,4,2,1,0:T(1,128)}, u32[]{:S(2)}) copy-start(s32[2,1,1,8,1]{3,4,2,1,0:T(1,128)} %param.18) | copy-start | bytes 196
  19.0 9.9 %collective-permute-start.1 = (f32[1,128]{1,0:T(1,128)S(1)}, f32[1,128]{1,0:T(1,128)S(1)}, u32[]{:S(2)}, u32[]{:S(2)}) collective-permute-start(f32[1,128]{1,0:T(1,128)S(1)} %get-tuple-element.21), channel_id=1, source_target_pairs={{1,0},{2,1},{3,2},{4,3},{5,4},{6,5},{7,6},{8,7},{9,8},{10,9},{11,1... | collective-permute-start | bytes 1544 | tf_op jit(solution)/shard_map/ppermute | solution.py:298
  29.0 6.6 %copy-start.1 = (f32[24,24]{1,0:T(8,128)S(1)}, f32[24,24]{1,0:T(8,128)}, u32[]{:S(2)}) copy-start(f32[24,24]{1,0:T(8,128)} %stiff.5) | copy-start | bytes 6916
  29.0 7.4 %collective-permute-start.2 = (f32[32,128]{1,0:T(8,128)S(1)}, f32[32,128]{1,0:T(8,128)S(1)}, u32[]{:S(2)}, u32[]{:S(2)}) collective-permute-start(f32[32,128]{1,0:T(8,128)S(1)} %get-tuple-element.22), channel_id=1, source_target_pairs={{0,32},{32,64},{64,96},{96,128},{128,160},{160,192},{192,224},{224... | collective-permute-start | bytes 49160 | tf_op jit(solution)/shard_map/ppermute | solution.py:298
  33.6 9.0 %collective-permute-start.3 = (f32[32,128]{1,0:T(8,128)S(1)}, f32[32,128]{1,0:T(8,128)S(1)}, u32[]{:S(2)}, u32[]{:S(2)}) collective-permute-start(f32[32,128]{1,0:T(8,128)S(1)} %get-tuple-element.23), channel_id=1, source_target_pairs={{32,0},{64,32},{96,64},{128,96},{160,128},{192,160},{224,192},{256... | collective-permute-start | bytes 49160 | tf_op jit(solution)/shard_map/ppermute | solution.py:298
  44.4 4.2 %collective-permute-start.4 = (f32[1,128]{1,0:T(1,128)S(1)}, f32[1,128]{1,0:T(1,128)S(1)}, u32[]{:S(2)}, u32[]{:S(2)}) collective-permute-start(f32[1,128]{1,0:T(1,128)S(1)} %get-tuple-element.36), channel_id=1, source_target_pairs={{0,1},{1,2},{2,3},{3,4},{4,5},{5,6},{6,7},{7,8},{8,9},{9,10},{10,1... | collective-permute-start | bytes 1544 | tf_op jit(solution)/shard_map/ppermute | solution.py:298
  44.5 4.3 %collective-permute-start.5 = (f32[1,128]{1,0:T(1,128)S(1)}, f32[1,128]{1,0:T(1,128)S(1)}, u32[]{:S(2)}, u32[]{:S(2)}) collective-permute-start(f32[1,128]{1,0:T(1,128)S(1)} %get-tuple-element.37), channel_id=1, source_target_pairs={{1,0},{2,1},{3,2},{4,3},{5,4},{6,5},{7,6},{8,7},{9,8},{10,9},{11,1... | collective-permute-start | bytes 1544 | tf_op jit(solution)/shard_map/ppermute | solution.py:298

commit v6 on v5

--- a/solution.py
+++ b/solution.py
@@ -9,7 +9,6 @@
 F32 = jnp.float32
 VMEM = pl.BlockSpec(memory_space=pltpu.VMEM)
 HBM = pl.BlockSpec(memory_space=pltpu.HBM)
-SMEM = pl.BlockSpec(memory_space=pltpu.SMEM)
 ROWS = 8
 COLS = 128
 OWNERS = 32
@@ -113,11 +112,16 @@
     return [total[ch] for ch in range(6)]
 
 
-def by_corner(stiff, e):
-    return lambda k, i, m, c: stiff[3 * (4 * k + 2 * i + e) + m, c]
-
-
-def first_kernel(stiff, owner, spread, from_left, from_right, above, below, u, v, mass, mod, ref, pair, vel, dis, weight, point, index, who, scale, at_left, at_right, at_edge):
+def by_corner(entries, e):
+    return lambda k, i, m, c: entries[entry(k, i, e, m, c), :]
+
+
+def entry(k, i, e, m, c):
+    at = 24 * c + 3 * (4 * k + 2 * i + e) + m
+    return slice(at, at + 1)
+
+
+def first_kernel(entries, owner, from_left, from_right, above, below, u, v, mass, mod, ref, pair, vel, dis, weight, point, index, who, scale, at_left, at_right, at_edge):
     edges = edge_columns(
         extended(from_left[...], above[AT_L : AT_L + 1, :], below[AT_L : AT_L + 1, :]),
         extended(from_right[...], above[AT_R : AT_R + 1, :], below[AT_R : AT_R + 1, :]),
@@ -166,7 +170,6 @@
     who[1:2, :] = below[AT_O : AT_O + 1, :].astype(jnp.int32)
     for step in range(2):
         who[2 + step : 3 + step, 0:ROWS] = owner[step]
-    del spread
     straight, moved, edge = {}, {}, {}
     for i in range(2):
         start = 1 - i
@@ -178,7 +181,7 @@
                     rows = slice(start + x, start + x + 16)
                     near = at_left[ch, rows, :]
                     main, side = (at_right[ch, rows, :], near) if e else (near, at_edge[ch, rows, :])
-                    w0, w1 = [stiff[3 * (4 * k + 2 * i + end) + m, c] for end in range(2)]
+                    w0, w1 = [entries[entry(k, i, end, m, c), :] for end in range(2)]
                     terms = (w0 * main, w1 * main, w1 * side)
                     sums = [t if s is None else s + t for s, t in zip(sums, terms)]
                 for into, s, by in zip((straight, moved, edge), sums, (s_main, s_main, s_edge)):
@@ -190,15 +193,12 @@
         dis[ch] = at_left[ch, 1:17, :] + DT * new
 
 
-def spread_kernel(stiff, spread):
-    lane = lanes((1, COLS))
-    for k in range(2):
-        for i in range(2):
-            for m in range(3):
-                for c in range(24):
-                    one, other = [stiff[3 * (4 * k + 2 * i + e) + m, c] for e in (1, 0)]
-                    at = 24 * (6 * k + 3 * i + m) + c
-                    spread[at : at + 1, :] = jnp.where(lane < 64, one, other)
+def spread_kernel(stiff, entries, sided):
+    lane = lanes((24, COLS))
+    for c in range(24):
+        column = jnp.broadcast_to(stiff[:, c : c + 1], (24, COLS))
+        entries[24 * c : 24 * c + 24, :] = column
+        sided[24 * c : 24 * c + 24, :] = jnp.where(lane < 64, pltpu.roll(column, 21, axis=0), column)
 
 
 def look_up(table, owner, index, row, out):
@@ -237,15 +237,15 @@
     right[...] = turned[COLS - 1 : COLS, :]
 
 
-def inner_kernel(who, stiff, table, pair, dis, vel, mass, ref, scale, base_dis, base_vel, weight, at_right, words):
+def inner_kernel(who, entries, table, pair, dis, vel, mass, ref, scale, base_dis, base_vel, weight, at_right, words):
     lane = lanes((ROWS, COLS))
     for b in range(ROWS):
         look_up(table, who[3, b], pair[1, b : b + 1, :], b, words)
     push = contact([words[c] for c in range(4)], [ref[m] + dis[2 * m, 1:9, :] for m in range(3)])
     for ch in range(6):
         at_right[ch] = pltpu.roll(dis[ch], COLS - 1, axis=1)
-    straight = element_sums(by_corner(stiff, 0), (dis, at_right), 1, scale.at[0], 0)
-    moved = element_sums(by_corner(stiff, 1), (dis, at_right), 1, scale.at[0], 0)
+    straight = element_sums(by_corner(entries, 0), (dis, at_right), 1, scale.at[0], 0)
+    moved = element_sums(by_corner(entries, 1), (dis, at_right), 1, scale.at[0], 0)
     for k in range(2):
         weight[k] = DT / mass[k]
         for m in range(3):
@@ -257,7 +257,7 @@
             base_dis[ch] = dis[ch, 1:9, :] + DT * new
 
 
-def outer_kernel(dis, base_dis, base_vel, weight, scale, spread, from_left, from_right, out_dis, out_vel, at_left, at_right):
+def outer_kernel(dis, base_dis, base_vel, weight, scale, sided, from_left, from_right, out_dis, out_vel, at_left, at_right):
     edges = edge_columns(from_left[...], from_right[...])
     lane = lanes((16, COLS))
     for ch in range(6):
@@ -265,11 +265,7 @@
         at_left[ch] = jnp.where(lane < 64, side, here)
         at_right[ch] = jnp.where(lane < 64, here, side)
 
-    def spread_row(k, i, m, c):
-        at = 24 * (6 * k + 3 * i + m) + c
-        return spread[at : at + 1, :]
-
-    forces = element_sums(spread_row, (at_left, at_right), 1, scale.at[2], 0)
+    forces = element_sums(by_corner(sided, 0), (at_left, at_right), 1, scale.at[2], 0)
     lane = lanes((ROWS, COLS))
     for m in range(3):
         for k in range(2):
@@ -321,7 +317,7 @@
         u, v, mass, mod, ref, pair, owner, from_left, from_right
     )
     above, below = swapped(down, up, "mesh")
-    spread = call(spread_kernel, struct(288, COLS), [SMEM])(stiff)
+    entries, sided = call(spread_kernel, (struct(576, COLS), struct(576, COLS)), [VMEM])(stiff)
     vel, dis, weight, point, index, who, scale = call(
         first_kernel,
         (
@@ -333,9 +329,9 @@
             struct(8, COLS, dtype=jnp.int32),
             struct(3, 24, COLS),
         ),
-        [SMEM] + [VMEM] * 12,
+        [VMEM] * 12,
         [pltpu.VMEM((8, 24, COLS), F32)] * 3,
-    )(stiff, owner, spread, from_left, from_right, above, below, u, v, mass, mod, ref, pair)
+    )(entries, owner, from_left, from_right, above, below, u, v, mass, mod, ref, pair)
     new_vel, new_dis, left, right = call(
         contact_kernel,
         (struct(6, ROWS, COLS), struct(6, 16, COLS), struct(1, COLS), struct(1, COLS)),
@@ -346,15 +342,15 @@
     base_dis, base_vel, weight = call(
         inner_kernel,
         (struct(6, ROWS, COLS), struct(6, ROWS, COLS), struct(2, ROWS, COLS)),
-        [VMEM, SMEM] + [VMEM] * 7,
+        [VMEM] * 9,
         [pltpu.VMEM((6, 16, COLS), F32), pltpu.VMEM((4, 8, COLS), F32)],
-    )(who, stiff, tables, pair, new_dis, new_vel, mass, ref, scale)
+    )(who, entries, tables, pair, new_dis, new_vel, mass, ref, scale)
     return call(
         outer_kernel,
         (struct(3, 2, ROWS, COLS), struct(3, 2, ROWS, COLS)),
         [VMEM] * 8,
         [pltpu.VMEM((6, 16, COLS), F32)] * 2,
-    )(new_dis, base_dis, base_vel, weight, scale, spread, from_left, from_right)
+    )(new_dis, base_dis, base_vel, weight, scale, sided, from_left, from_right)
 
 
 def solution(mesh):

time: 49.9 us -> 49.2 us (0.986)
  Pallas kernels: 6.29 us -> 4.1 us
  waiting for transfers between devices: 7.63 us -> 9.09 us
    ppermute x6, waiting for transfers between devices: 7.63 us -> 9.09 us  [swapped(): return (lax.ppermute(to_next, axis, up), lax.ppermute(to_last, axis, down))]
    pallas_call x1, Pallas kernels: 1.07 us -> 0.32 us  [shards(): call(inner_kernel, (struct(6, ROWS, COLS), struct(6, ROWS, COLS), struct(...]
    pallas_call x1, Pallas kernels: 1.5 us -> 0.76 us  [shards(): call(first_kernel, (struct(6, 16, COLS), struct(6, 16, COLS), struct(2, 1...]
    pallas_call x1, Pallas kernels: 0.89 us -> 0.18 us  [shards(): call(spread_kernel, (struct(576, COLS), struct(576, COLS)), [VMEM])(stiff)]
  transfers between devices with their start and end apart: 7 -> 7, of which waited for: 5 -> 5; matrix products, arithmetic and copies ran while one was open for 0% -> 0% of each run, Pallas kernels for 7% -> 3%
where the time goes in v6:
time: 49.2 us; the launch traced here: 48.8 us
  starting transfers between devices  34.7 us (71%)
  waiting for transfers between devices  9.09 us (18%)
  Pallas kernels  4.1 us (8%)
  between operations  0.84 us (2%)
    ppermute x6, starting transfers between devices, swapped(): return (lax.ppermute(to_next, axis, up), lax.ppermute(to_last, axis, down))  18.1 us
    all_to_all x1, starting transfers between devices, shards(): lax.all_to_all(table, 'mesh', split_axis=0, concat_axis=0, tiled=True)  16.6 us
    ppermute x6, waiting for transfers between devices, swapped(): return (lax.ppermute(to_next, axis, up), lax.ppermute(to_last, axis, down))  9.09 us
    pallas_call x1, Pallas kernels, shards(): call(table_kernel, struct(OWNERS, 32, COLS), [HBM] * 2, [pltpu.VMEM(x.sha...  1.62 us
  transfers between devices with their start and end apart: 7, of which 5 were waited for; matrix products, arithmetic and copies ran while one was open for 0% of the time, Pallas kernels for 3%

profile of v6, /device:TPU:30, one launch (start us, length us, event | category | flops | bytes accessed | tf_op | source)
XLA Modules:
  0.0 48.8 jit_solution(8315755867564386875)
XLA Ops:
  0.6 1.6 %shard_map.117 = f32[32,32,128]{2,1,0:T(8,128)} custom-call(f32[48,128]{1,0:T(8,128)} %bitcast.7, f32[8,128]{1,0:T(8,128)} %bitcast.8), custom_call_target="tpu_custom_call" | custom-call | flops 1000000 | bytes 1000000 | tf_op jit(solution)/shard_map/pallas_call | solution.py:301
  2.3 0.0 copy-start
  2.3 0.0 copy-start.5
  2.3 0.0 copy-start.3
  2.3 0.0 copy-start.4
  2.3 16.6 %all-to-all-start = ((f32[32,32,128]{2,1,0:T(8,128)}), f32[32,32,128]{2,1,0:T(8,128)S(1)}, u32[]{:S(2)}, u32[]{:S(2)}) async-start(f32[32,32,128]{2,1,0:T(8,128)} %shard_map.117), calls=%async_computation | async-start | bytes 1048576 | tf_op jit(solution)/shard_map/all_to_all | solution.py:314
  18.9 0.0 copy-done
  18.9 0.0 copy-done.5
  18.9 0.0 copy-start.1
  18.9 0.0 copy-start.2
  18.9 0.1 shard_map.114
  19.0 0.0 collective-permute-start
  19.0 0.0 copy-start.7
  19.0 8.6 %collective-permute-start.1 = (f32[1,128]{1,0:T(1,128)S(1)}, f32[1,128]{1,0:T(1,128)S(1)}, u32[]{:S(2)}, u32[]{:S(2)}) collective-permute-start(f32[1,128]{1,0:T(1,128)S(1)} %get-tuple-element.24), channel_id=1, source_target_pairs={{1,0},{2,1},{3,2},{4,3},{5,4},{6,5},{7,6},{8,7},{9,8},{10,9},{11,1... | collective-permute-start | bytes 1544 | tf_op jit(solution)/shard_map/ppermute | solution.py:294
  27.7 1.2 %collective-permute-done.from_left = f32[1,128]{1,0:T(1,128)S(1)} collective-permute-done((f32[1,128]{1,0:T(1,128)S(1)}, f32[1,128]{1,0:T(1,128)S(1)}, u32[]{:S(2)}, u32[]{:S(2)}) %collective-permute-start) | collective-permute-done | bytes 544 | tf_op jit(solution)/shard_map/ppermute | solution.py:294
  28.9 0.1 collective-permute-done.1.from_right
  29.0 0.0 copy-done.3
  29.0 0.0 copy-start.6
  29.0 4.6 %collective-permute-start.2 = (f32[32,128]{1,0:T(8,128)S(1)}, f32[32,128]{1,0:T(8,128)S(1)}, u32[]{:S(2)}, u32[]{:S(2)}) collective-permute-start(f32[32,128]{1,0:T(8,128)S(1)} %get-tuple-element.25), channel_id=1, source_target_pairs={{0,32},{32,64},{64,96},{96,128},{128,160},{160,192},{192,224},{224... | collective-permute-start | bytes 49160 | tf_op jit(solution)/shard_map/ppermute | solution.py:294
  33.6 1.9 %collective-permute-start.3 = (f32[32,128]{1,0:T(8,128)S(1)}, f32[32,128]{1,0:T(8,128)S(1)}, u32[]{:S(2)}, u32[]{:S(2)}) collective-permute-start(f32[32,128]{1,0:T(8,128)S(1)} %get-tuple-element.26), channel_id=1, source_target_pairs={{32,0},{64,32},{96,64},{128,96},{160,128},{192,160},{224,192},{256... | collective-permute-start | bytes 49160 | tf_op jit(solution)/shard_map/ppermute | solution.py:294
  35.6 0.2 shard_map.113
  35.8 0.0 collective-permute-done.2.above
  35.8 6.8 %collective-permute-done.3.below = f32[32,128]{1,0:T(8,128)S(1)} collective-permute-done((f32[32,128]{1,0:T(8,128)S(1)}, f32[32,128]{1,0:T(8,128)S(1)}, u32[]{:S(2)}, u32[]{:S(2)}) %collective-permute-start.3) | collective-permute-done | bytes 16416 | tf_op jit(solution)/shard_map/ppermute | solution.py:294
  42.6 0.8 %shard_map.116 = (f32[6,16,128]{2,1,0:T(8,128)S(1)}, f32[6,16,128]{2,1,0:T(8,128)S(1)}, f32[2,16,128]{2,1,0:T(8,128)S(1)}, f32[3,16,128]{2,1,0:T(8,128)S(1)}, s3...) custom-call(f32[576,128]{1,0:T(8,128)S(1)} %get-tuple-element.22.entries, ...), custom_call_target="tpu_custom_call" | custom-call | flops 1000000 | bytes 1000000 | tf_op jit(solution)/shard_map/pallas_call | solution.py:321
  43.3 0.0 all-to-all-done.table
  43.4 0.3 shard_map.118
  43.7 0.0 collective-permute-start.4
  43.7 3.0 %collective-permute-start.5 = (f32[1,128]{1,0:T(1,128)S(1)}, f32[1,128]{1,0:T(1,128)S(1)}, u32[]{:S(2)}, u32[]{:S(2)}) collective-permute-start(f32[1,128]{1,0:T(1,128)S(1)} %get-tuple-element.41), channel_id=1, source_target_pairs={{1,0},{2,1},{3,2},{4,3},{5,4},{6,5},{7,6},{8,7},{9,8},{10,9},{11,1... | collective-permute-start | bytes 1544 | tf_op jit(solution)/shard_map/ppermute | solution.py:294
  46.7 0.3 shard_map.119
  47.0 0.9 %collective-permute-done.4.from_left = f32[1,128]{1,0:T(1,128)S(1)} collective-permute-done((f32[1,128]{1,0:T(1,128)S(1)}, f32[1,128]{1,0:T(1,128)S(1)}, u32[]{:S(2)}, u32[]{:S(2)}) %collective-permute-start.4) | collective-permute-done | bytes 544 | tf_op jit(solution)/shard_map/ppermute | solution.py:294
  47.9 0.1 collective-permute-done.5.from_right
  48.0 0.8 %shard_map.120 = (f32[3,2,8,128]{3,2,1,0:T(8,128)}, f32[3,2,8,128]{3,2,1,0:T(8,128)}) custom-call(f32[6,16,128]{2,1,0:T(8,128)S(1)} %get-tuple-element.33.dis, f32[6,8,128]{2,1,0:T(8,128)S(1)} %get-tuple-element.36.base_dis, f32[6,8,128]{2,1,0:T(8,128)S(1)} %get-tuple-element.37.base_vel, f32[2,8,128]{2,1,0:T(8,128)S(1)} %get-tuple-element.38.weight, ...), custom_call_target="tpu_custom_call" | custom-call | flops 1000000 | bytes 1000000 | tf_op jit(solution)/shard_map/pallas_call | solution.py:348
  (6 shorter events, 0.0 us)
Async XLA Ops:
  2.3 16.6 %copy-start = (f32[3,2,8,128]{3,2,1,0:T(8,128)S(1)}, f32[3,2,8,128]{3,2,1,0:T(8,128)}, u32[]{:S(2)}) copy-start(f32[3,2,8,128]{3,2,1,0:T(8,128)} %u.5) | copy-start | bytes 73732
  2.3 16.6 %copy-start.5 = (f32[2,8,128]{2,1,0:T(8,128)S(1)}, f32[2,8,128]{2,1,0:T(8,128)}, u32[]{:S(2)}) copy-start(f32[2,8,128]{2,1,0:T(8,128)} %mod.5) | copy-start | bytes 24580
  2.3 26.7 %copy-start.3 = (f32[2,8,128]{2,1,0:T(8,128)S(1)}, f32[2,8,128]{2,1,0:T(8,128)}, u32[]{:S(2)}) copy-start(f32[2,8,128]{2,1,0:T(8,128)} %mass.5) | copy-start | bytes 24580
  2.3 26.7 %copy-start.4 = (s32[2,8,128]{2,1,0:T(8,128)S(1)}, s32[2,8,128]{2,1,0:T(8,128)}, u32[]{:S(2)}) copy-start(s32[2,8,128]{2,1,0:T(8,128)} %pair.5) | copy-start | bytes 24580
  2.3 41.0 %all-to-all-start = ((f32[32,32,128]{2,1,0:T(8,128)}), f32[32,32,128]{2,1,0:T(8,128)S(1)}, u32[]{:S(2)}, u32[]{:S(2)}) async-start(f32[32,32,128]{2,1,0:T(8,128)} %shard_map.117), calls=%async_computation | async-start | bytes 1048576 | tf_op jit(solution)/shard_map/all_to_all | solution.py:314
  18.9 10.1 %copy-start.1 = (f32[3,8,128]{2,1,0:T(8,128)S(1)}, f32[3,8,128]{2,1,0:T(8,128)}, u32[]{:S(2)}) copy-start(f32[3,8,128]{2,1,0:T(8,128)} %ref.5) | copy-start | bytes 36868
  18.9 10.1 %copy-start.2 = (f32[3,2,8,128]{3,2,1,0:T(8,128)S(1)}, f32[3,2,8,128]{3,2,1,0:T(8,128)}, u32[]{:S(2)}) copy-start(f32[3,2,8,128]{3,2,1,0:T(8,128)} %v.3) | copy-start | bytes 73732
  19.0 9.9 %collective-permute-start = (f32[1,128]{1,0:T(1,128)S(1)}, f32[1,128]{1,0:T(1,128)S(1)}, u32[]{:S(2)}, u32[]{:S(2)}) collective-permute-start(f32[1,128]{1,0:T(1,128)S(1)} %get-tuple-element.23), channel_id=1, source_target_pairs={{0,1},{1,2},{2,3},{3,4},{4,5},{5,6},{6,7},{7,8},{8,9},{9,10},{10,1... | collective-permute-start | bytes 1544 | tf_op jit(solution)/shard_map/ppermute | solution.py:294
  19.0 10.0 %copy-start.7 = (s32[2,1,1,8,1]{3,4,2,1,0:T(1,128)S(1)}, s32[2,1,1,8,1]{3,4,2,1,0:T(1,128)}, u32[]{:S(2)}) copy-start(s32[2,1,1,8,1]{3,4,2,1,0:T(1,128)} %param.18) | copy-start | bytes 196
  19.0 9.9 %collective-permute-start.1 = (f32[1,128]{1,0:T(1,128)S(1)}, f32[1,128]{1,0:T(1,128)S(1)}, u32[]{:S(2)}, u32[]{:S(2)}) collective-permute-start(f32[1,128]{1,0:T(1,128)S(1)} %get-tuple-element.24), channel_id=1, source_target_pairs={{1,0},{2,1},{3,2},{4,3},{5,4},{6,5},{7,6},{8,7},{9,8},{10,9},{11,1... | collective-permute-start | bytes 1544 | tf_op jit(solution)/shard_map/ppermute | solution.py:294
  29.0 6.6 %copy-start.6 = (f32[24,24]{1,0:T(8,128)S(1)}, f32[24,24]{1,0:T(8,128)}, u32[]{:S(2)}) copy-start(f32[24,24]{1,0:T(8,128)} %stiff.1) | copy-start | bytes 6916
  29.0 6.7 %collective-permute-start.2 = (f32[32,128]{1,0:T(8,128)S(1)}, f32[32,128]{1,0:T(8,128)S(1)}, u32[]{:S(2)}, u32[]{:S(2)}) collective-permute-start(f32[32,128]{1,0:T(8,128)S(1)} %get-tuple-element.25), channel_id=1, source_target_pairs={{0,32},{32,64},{64,96},{96,128},{128,160},{160,192},{192,224},{224... | collective-permute-start | bytes 49160 | tf_op jit(solution)/shard_map/ppermute | solution.py:294
  33.6 9.0 %collective-permute-start.3 = (f32[32,128]{1,0:T(8,128)S(1)}, f32[32,128]{1,0:T(8,128)S(1)}, u32[]{:S(2)}, u32[]{:S(2)}) collective-permute-start(f32[32,128]{1,0:T(8,128)S(1)} %get-tuple-element.26), channel_id=1, source_target_pairs={{32,0},{64,32},{96,64},{128,96},{160,128},{192,160},{224,192},{256... | collective-permute-start | bytes 49160 | tf_op jit(solution)/shard_map/ppermute | solution.py:294
  43.7 4.2 %collective-permute-start.4 = (f32[1,128]{1,0:T(1,128)S(1)}, f32[1,128]{1,0:T(1,128)S(1)}, u32[]{:S(2)}, u32[]{:S(2)}) collective-permute-start(f32[1,128]{1,0:T(1,128)S(1)} %get-tuple-element.40), channel_id=1, source_target_pairs={{0,1},{1,2},{2,3},{3,4},{4,5},{5,6},{6,7},{7,8},{8,9},{9,10},{10,1... | collective-permute-start | bytes 1544 | tf_op jit(solution)/shard_map/ppermute | solution.py:294
  43.7 4.3 %collective-permute-start.5 = (f32[1,128]{1,0:T(1,128)S(1)}, f32[1,128]{1,0:T(1,128)S(1)}, u32[]{:S(2)}, u32[]{:S(2)}) collective-permute-start(f32[1,128]{1,0:T(1,128)S(1)} %get-tuple-element.41), channel_id=1, source_target_pairs={{1,0},{2,1},{3,2},{4,3},{5,4},{6,5},{7,6},{8,7},{9,8},{10,9},{11,1... | collective-permute-start | bytes 1544 | tf_op jit(solution)/shard_map/ppermute | solution.py:294

commit v7 on v6

--- a/solution.py
+++ b/solution.py
@@ -13,7 +13,7 @@
 COLS = 128
 OWNERS = 32
 REPLICAS = 8
-AT_U, AT_E, AT_V, AT_M, AT_X, AT_P, AT_O, AT_L, AT_R = 0, 12, 16, 22, 24, 27, 28, 29, 30
+AT_U, AT_E, AT_V, AT_M, AT_X, AT_P, AT_O = 0, 12, 16, 22, 24, 27, 28
 MSG = 32
 
 
@@ -25,14 +25,16 @@
     return lax.broadcasted_iota(jnp.int32, shape, len(shape) - 1)
 
 
-def table_kernel(fac, pen, table, fac_, pen_, mine, sems, out_sems):
-    copies = [pltpu.make_async_copy(a, b, sems.at[n]) for n, (a, b) in enumerate(((fac, fac_), (pen, pen_)))]
+def pack_kernel(fac, pen, u, v, mass, mod, ref, pair, own, table, message, *held):
+    held, mine, sems, out_sems = held[:-3], *held[-3:]
+    copies = [pltpu.make_async_copy(a, b, sems.at[n]) for n, (a, b) in enumerate(zip((fac, pen, u, v, mass, mod, ref, pair, own), held))]
     for copy in copies:
         copy.start()
-    for copy in copies:
+    fac, pen, u, v, mass, mod, ref, pair, own = held
+    for copy in copies[:2]:
         copy.wait()
-    root = jnp.sqrt(pen_[...])
-    c, n = [[fac_[8 * (m + at) : 8 * (m + at) + 8, :] for m in range(3)] for at in (0, 3)]
+    root = jnp.sqrt(pen[...])
+    c, n = [[fac[8 * (m + at) : 8 * (m + at) + 8, :] for m in range(3)] for at in (0, 3)]
     dist = n[0] * c[0] + n[1] * c[1] + n[2] * c[2]
     words = [root * n[0], root * n[1], root * n[2], root * dist]
     for q in range(4):
@@ -42,21 +44,10 @@
     outs = [pltpu.make_async_copy(mine, table.at[pl.ds(o * REPLICAS, REPLICAS)], out_sems.at[o]) for o in range(OWNERS // REPLICAS)]
     for copy in outs:
         copy.start()
-    for copy in outs:
+    for copy in copies[2:]:
         copy.wait()
-
-
-def columns_kernel(u, mod, left, right, square):
-    for ch in range(8):
-        square[16 * ch : 16 * ch + 8, :] = u[ch // 2, ch % 2] if ch < 6 else mod[ch - 6]
-        square[16 * ch + 8 : 16 * ch + 16, :] = jnp.zeros((8, COLS), F32)
-    turned = jnp.transpose(square[...])
-    left[...] = turned[0:1, :]
-    right[...] = turned[COLS - 1 : COLS, :]
-
-
-def pack_kernel(u, v, mass, mod, ref, pair, own, from_left, from_right, up, down):
-    for out, two, one in ((down, ROWS - 2, ROWS - 1), (up, 0, 0)):
+    for base, two, one in ((0, 0, 0), (MSG, ROWS - 2, ROWS - 1)):
+        out = message.at[base : base + MSG]
         for m in range(3):
             for k in range(2):
                 ch = 2 * m + k
@@ -69,16 +60,23 @@
         out[AT_P : AT_P + 1, :] = pair[0, one : one + 1, :].astype(F32)
         out[AT_O :, :] = jnp.zeros((MSG - AT_O, COLS), F32)
         out[AT_O : AT_O + 1, 0:ROWS] = own[0].astype(F32)
-        out[AT_L : AT_L + 1, :] = from_left[...]
-        out[AT_R : AT_R + 1, :] = from_right[...]
-
-
-def extended(here, above, below):
-    here, above, below = [jnp.broadcast_to(x, (8, COLS)) for x in (here, above, below)]
-    at = lanes((8, COLS)) & 15
-    out = jnp.where(at < 12, pltpu.roll(below, 10, axis=1), 0.0)
-    out = jnp.where(at < 10, pltpu.roll(here, 2, axis=1), out)
-    return jnp.where(at < 2, pltpu.roll(above, COLS - 6, axis=1), out)[0:1]
+    for copy in outs:
+        copy.wait()
+
+
+def extend_kernel(odd, first, other, u, mod, above, below, ext, left, right):
+    here = odd[...] == 1
+    above[...] = jnp.where(here, first[0, MSG:, :], other[0, MSG:, :])
+    below[...] = jnp.where(here, other[1, :MSG, :], first[1, :MSG, :])
+    for ch in range(8):
+        at = AT_U + 2 * ch if ch < 6 else AT_E + 2 * (ch - 6)
+        ext[16 * ch : 16 * ch + 2, :] = above[at : at + 2, :]
+        ext[16 * ch + 2 : 16 * ch + 10, :] = u[ch // 2, ch % 2] if ch < 6 else mod[ch - 6]
+        ext[16 * ch + 10 : 16 * ch + 12, :] = below[at : at + 2, :]
+        ext[16 * ch + 12 : 16 * ch + 16, :] = jnp.zeros((4, COLS), F32)
+    turned = jnp.transpose(ext[...])
+    left[...] = turned[0:1, :]
+    right[...] = turned[COLS - 1 : COLS, :]
 
 
 def edge_columns(from_left, from_right):
@@ -121,21 +119,14 @@
     return slice(at, at + 1)
 
 
-def first_kernel(entries, owner, from_left, from_right, above, below, u, v, mass, mod, ref, pair, vel, dis, weight, point, index, who, scale, at_left, at_right, at_edge):
-    edges = edge_columns(
-        extended(from_left[...], above[AT_L : AT_L + 1, :], below[AT_L : AT_L + 1, :]),
-        extended(from_right[...], above[AT_R : AT_R + 1, :], below[AT_R : AT_R + 1, :]),
-    )
+def first_kernel(entries, owner, from_left, from_right, above, below, ext, v, mass, ref, pair, vel, dis, weight, point, index, who, scale, at_left, at_right, at_edge):
+    edges = edge_columns(from_left[...], from_right[...])
     zero = jnp.zeros((8, COLS), F32)
     lane = lanes((16, COLS))
     for ch in range(8):
-        at = AT_U + 2 * ch if ch < 6 else AT_E + 2 * (ch - 6)
-        at_left[ch, 0:2, :] = above[at : at + 2, :]
-        at_left[ch, 2:10, :] = u[ch // 2, ch % 2] if ch < 6 else mod[ch - 6]
-        at_left[ch, 10:12, :] = below[at : at + 2, :]
-        at_left[ch, 12:16, :] = zero[:4]
-        side = edges[16 * ch : 16 * ch + 16, :]
-        at_right[ch, 0:16, :] = with_columns(at_left[ch, 0:16, :], side)
+        here, side = ext[16 * ch : 16 * ch + 16, :], edges[16 * ch : 16 * ch + 16, :]
+        at_left[ch, 0:16, :] = here
+        at_right[ch, 0:16, :] = with_columns(here, side)
         at_edge[ch, 0:16, :] = side
         for buf in (at_left, at_right, at_edge):
             buf[ch, 16:24, :] = zero
@@ -297,26 +288,32 @@
 def shards(u, v, mass, mod, stiff, ref, facets, penalty, owners, pair):
     width = facets.shape[-1]
     owner = owners.reshape(2, 1, ROWS)
-    sources = (facets.reshape(6 * width // COLS, COLS), penalty.reshape(width // COLS, COLS))
-    table = call(
-        table_kernel,
-        struct(OWNERS, 32, COLS),
-        [HBM] * 2,
+    sources = (
+        facets.reshape(6 * width // COLS, COLS),
+        penalty.reshape(width // COLS, COLS),
+        *(u, v, mass, mod, ref, pair, owner),
+    )
+    table, message = call(
+        pack_kernel,
+        (struct(OWNERS, 32, COLS), struct(2 * MSG, COLS)),
+        [HBM] * len(sources),
         [pltpu.VMEM(x.shape, x.dtype) for x in sources]
         + [pltpu.VMEM((REPLICAS, 32, COLS), F32)]
-        + [pltpu.SemaphoreType.DMA((n,)) for n in (2, OWNERS // REPLICAS)],
+        + [pltpu.SemaphoreType.DMA((n,)) for n in (len(sources), OWNERS // REPLICAS)],
         room=60,
-        out_specs=HBM,
+        out_specs=(HBM, VMEM),
     )(*sources)
-    left, right = call(
-        columns_kernel, (struct(1, COLS), struct(1, COLS)), [VMEM] * 2, [pltpu.VMEM((128, COLS), F32)]
-    )(u, mod)
+    size = lax.axis_size("mesh")
+    pairs = [[[i, (i + 1) % size] for i in range(start, size, 2)] for start in range(2)]
+    first, other = [lax.all_gather(message, "mesh", axis_index_groups=groups) for groups in pairs]
     tables = lax.all_to_all(table, "mesh", split_axis=0, concat_axis=0, tiled=True)
+    odd = jnp.full((1, COLS), lax.axis_index("mesh") % 2, jnp.int32)
+    above, below, ext, left, right = call(
+        extend_kernel,
+        (struct(MSG, COLS), struct(MSG, COLS), struct(128, COLS), struct(1, COLS), struct(1, COLS)),
+        [VMEM] * 5,
+    )(odd, first, other, u, mod)
     from_left, from_right = swapped(right, left, "sub")
-    up, down = call(pack_kernel, (struct(MSG, COLS), struct(MSG, COLS)), [VMEM] * 9)(
-        u, v, mass, mod, ref, pair, owner, from_left, from_right
-    )
-    above, below = swapped(down, up, "mesh")
     entries, sided = call(spread_kernel, (struct(576, COLS), struct(576, COLS)), [VMEM])(stiff)
     vel, dis, weight, point, index, who, scale = call(
         first_kernel,
@@ -329,9 +326,9 @@
             struct(8, COLS, dtype=jnp.int32),
             struct(3, 24, COLS),
         ),
-        [VMEM] * 12,
+        [VMEM] * 11,
         [pltpu.VMEM((8, 24, COLS), F32)] * 3,
-    )(entries, owner, from_left, from_right, above, below, u, v, mass, mod, ref, pair)
+    )(entries, owner, from_left, from_right, above, below, ext, v, mass, ref, pair)
     new_vel, new_dis, left, right = call(
         contact_kernel,
         (struct(6, ROWS, COLS), struct(6, 16, COLS), struct(1, COLS), struct(1, COLS)),

time: 49.2 us -> 52.2 us (1.061)
  the two profiles are of different devices: /device:TPU:30 before, /device:TPU:24 now
where the time goes in v7:
time: 52.2 us; the launch traced here: 51.7 us
  starting transfers between devices  31.7 us (61%)
  blocking collectives  11.7 us (22%)
  Pallas kernels  4.82 us (9%)
  waiting for transfers between devices  2.06 us (4%)
  between operations  0.79 us (2%)
  local copies, waits for them, and re-layouts  0.7 us (1%)
    all_to_all x1, starting transfers between devices, shards(): lax.all_to_all(table, 'mesh', split_axis=0, concat_axis=0, tiled=True)  16.5 us
    ppermute x4, starting transfers between devices, swapped(): return (lax.ppermute(to_next, axis, up), lax.ppermute(to_last, axis, down))  15.2 us
    all_gather x2, blocking collectives, shards(): lax.all_gather(message, 'mesh', axis_index_groups=groups)  11.7 us
    pallas_call x1, Pallas kernels, shards(): call(pack_kernel, (struct(OWNERS, 32, COLS), struct(2 * MSG, COLS)), [HBM...  2.28 us
    ppermute x4, waiting for transfers between devices, swapped(): return (lax.ppermute(to_next, axis, up), lax.ppermute(to_last, axis, down))  2.06 us
  transfers between devices with their start and end apart: 5, of which 4 were waited for; matrix products, arithmetic and copies ran while one was open for 0% of the time, Pallas kernels for 3%

profile of v7, /device:TPU:24, one launch (start us, length us, event | category | flops | bytes accessed | tf_op | source)
XLA Modules:
  0.0 51.7 jit_solution(14480547350016467597)
XLA Ops:
  0.6 2.3 %shard_map.114 = (f32[32,32,128]{2,1,0:T(8,128)}, f32[64,128]{1,0:T(8,128)}) custom-call(f32[48,128]{1,0:T(8,128)} %bitcast.11, f32[8,128]{1,0:T(8,128)} %bitcast.12, f32[3,2,8,128]{3,2,1,0:T(8,128)} %u.3, f32[3,2,8,128]{3,2,1,0:T(8,128)} %v.3, f32[2,8,128]{2,1,0:T(8,128)} %mass.5, f32[2,8,128]{2,1,0:T(8,128)} %mod.3, f32[3,8,128]{2,1,0:T(8,128)} %ref.5, ...), custom_call_target="tpu_custom_call" | custom-call | flops 1000000 | bytes 1000000 | tf_op jit(solution)/shard_map/pallas_call | solution.py:296
  2.9 0.0 copy-start.8
  2.9 16.5 %all-to-all-start = ((f32[32,32,128]{2,1,0:T(8,128)}), f32[32,32,128]{2,1,0:T(8,128)S(1)}, u32[]{:S(2)}, u32[]{:S(2)}) async-start(f32[32,32,128]{2,1,0:T(8,128)} %get-tuple-element.33), calls=%async_computation | async-start | bytes 1048576 | tf_op jit(solution)/shard_map/all_to_all | solution.py:309
  19.4 0.0 copy-done.8
  19.5 4.6 %all-gather = f32[128,128]{1,0:T(8,128)S(1)} all-gather(f32[64,128]{1,0:T(8,128)S(1)} %copy-done.8), channel_id=2, replica_groups={{0,32},{64,96},{128,160},{192,224},{256,288},{320,352},{384,416},{448,4..., dimensions={0}, use_global_device_ids=true | all-gather | bytes 98304 | tf_op jit(solution)/shard_map/all_gather | solution.py:308
  24.1 7.1 %all-gather.1 = f32[128,128]{1,0:T(8,128)S(1)} all-gather(f32[64,128]{1,0:T(8,128)S(1)} %copy-done.8), channel_id=3, replica_groups={{32,64},{96,128},{160,192},{224,256},{288,320},{352,384},{416,448},{480..., dimensions={0}, use_global_device_ids=true | all-gather | bytes 98304 | tf_op jit(solution)/shard_map/all_gather | solution.py:308
  31.1 0.0 copy-done.1
  31.1 0.0 copy-done.5
  31.1 0.0 copy-start.2
  31.1 0.0 copy-start.4
  31.2 0.1 shard_map.115
  31.3 0.0 copy-start
  31.3 0.0 collective-permute-start
  31.3 0.0 copy-start.3
  31.3 12.2 %collective-permute-start.1 = (f32[1,128]{1,0:T(1,128)S(1)}, f32[1,128]{1,0:T(1,128)S(1)}, u32[]{:S(2)}, u32[]{:S(2)}) collective-permute-start(f32[1,128]{1,0:T(1,128)S(1)} %get-tuple-element.28), channel_id=1, source_target_pairs={{1,0},{2,1},{3,2},{4,3},{5,4},{6,5},{7,6},{8,7},{9,8},{10,9},{11,1... | collective-permute-start | bytes 1544 | tf_op jit(solution)/shard_map/ppermute | solution.py:285
  43.5 0.0 copy-done.6
  43.5 0.2 shard_map.113
  43.7 1.0 %collective-permute-done.from_left = f32[1,128]{1,0:T(1,128)S(1)} collective-permute-done((f32[1,128]{1,0:T(1,128)S(1)}, f32[1,128]{1,0:T(1,128)S(1)}, u32[]{:S(2)}, u32[]{:S(2)}) %collective-permute-start) | collective-permute-done | bytes 544 | tf_op jit(solution)/shard_map/ppermute | solution.py:285
  44.7 0.1 collective-permute-done.1.from_right
  44.8 0.0 copy-done.2
  44.8 0.0 copy-done.4
  44.8 0.0 copy-done.3
  44.8 0.7 %copy-done.7 = s32[2,1,1,8,1]{3,4,2,1,0:T(1,128)S(1)} copy-done((s32[2,1,1,8,1]{3,4,2,1,0:T(1,128)S(1)}, s32[2,1,1,8,1]{3,4,2,1,0:T(1,128)}, u32[]{:S(2)}) %copy-start.7) | copy-done | bytes 88
  45.5 0.8 %shard_map.116 = (f32[6,16,128]{2,1,0:T(8,128)S(1)}, f32[6,16,128]{2,1,0:T(8,128)S(1)}, f32[2,16,128]{2,1,0:T(8,128)S(1)}, f32[3,16,128]{2,1,0:T(8,128)S(1)}, s3...) custom-call(f32[576,128]{1,0:T(8,128)S(1)} %get-tuple-element.25.entries, ...), custom_call_target="tpu_custom_call" | custom-call | flops 1000000 | bytes 1000000 | tf_op jit(solution)/shard_map/pallas_call | solution.py:318
  46.3 0.0 all-to-all-done.table
  46.3 0.3 shard_map.117
  46.7 0.0 collective-permute-start.2
  46.7 3.0 %collective-permute-start.3 = (f32[1,128]{1,0:T(1,128)S(1)}, f32[1,128]{1,0:T(1,128)S(1)}, u32[]{:S(2)}, u32[]{:S(2)}) collective-permute-start(f32[1,128]{1,0:T(1,128)S(1)} %get-tuple-element.47), channel_id=1, source_target_pairs={{1,0},{2,1},{3,2},{4,3},{5,4},{6,5},{7,6},{8,7},{9,8},{10,9},{11,1... | collective-permute-start | bytes 1544 | tf_op jit(solution)/shard_map/ppermute | solution.py:285
  49.7 0.3 shard_map.118
  50.0 0.9 %collective-permute-done.2.from_left = f32[1,128]{1,0:T(1,128)S(1)} collective-permute-done((f32[1,128]{1,0:T(1,128)S(1)}, f32[1,128]{1,0:T(1,128)S(1)}, u32[]{:S(2)}, u32[]{:S(2)}) %collective-permute-start.2) | collective-permute-done | bytes 544 | tf_op jit(solution)/shard_map/ppermute | solution.py:285
  50.9 0.1 collective-permute-done.3.from_right
  51.0 0.8 %shard_map.119 = (f32[3,2,8,128]{3,2,1,0:T(8,128)}, f32[3,2,8,128]{3,2,1,0:T(8,128)}) custom-call(f32[6,16,128]{2,1,0:T(8,128)S(1)} %get-tuple-element.39.dis, f32[6,8,128]{2,1,0:T(8,128)S(1)} %get-tuple-element.42.base_dis, f32[6,8,128]{2,1,0:T(8,128)S(1)} %get-tuple-element.43.base_vel, f32[2,8,128]{2,1,0:T(8,128)S(1)} %get-tuple-element.44.weight, ...), custom_call_target="tpu_custom_call" | custom-call | flops 1000000 | bytes 1000000 | tf_op jit(solution)/shard_map/pallas_call | solution.py:345
  (6 shorter events, 0.0 us)
Async XLA Ops:
  2.9 16.5 %copy-start.8 = (f32[64,128]{1,0:T(8,128)S(1)}, f32[64,128]{1,0:T(8,128)}, u32[]{:S(2)}) copy-start(f32[64,128]{1,0:T(8,128)} %get-tuple-element.26) | copy-start | bytes 98308
  2.9 43.4 %all-to-all-start = ((f32[32,32,128]{2,1,0:T(8,128)}), f32[32,32,128]{2,1,0:T(8,128)S(1)}, u32[]{:S(2)}, u32[]{:S(2)}) async-start(f32[32,32,128]{2,1,0:T(8,128)} %get-tuple-element.33), calls=%async_computation | async-start | bytes 1048576 | tf_op jit(solution)/shard_map/all_to_all | solution.py:309
  24.0 7.1 %copy-start.1 = (f32[3,2,8,128]{3,2,1,0:T(8,128)S(1)}, f32[3,2,8,128]{3,2,1,0:T(8,128)}, u32[]{:S(2)}) copy-start(f32[3,2,8,128]{3,2,1,0:T(8,128)} %u.3) | copy-start | bytes 73732
  24.1 7.1 %copy-start.5 = (f32[2,8,128]{2,1,0:T(8,128)S(1)}, f32[2,8,128]{2,1,0:T(8,128)}, u32[]{:S(2)}) copy-start(f32[2,8,128]{2,1,0:T(8,128)} %mod.3) | copy-start | bytes 24580
  31.1 12.4 %copy-start.6 = (f32[24,24]{1,0:T(8,128)S(1)}, f32[24,24]{1,0:T(8,128)}, u32[]{:S(2)}) copy-start(f32[24,24]{1,0:T(8,128)} %stiff.1) | copy-start | bytes 6916
  31.1 13.7 %copy-start.2 = (f32[3,2,8,128]{3,2,1,0:T(8,128)S(1)}, f32[3,2,8,128]{3,2,1,0:T(8,128)}, u32[]{:S(2)}) copy-start(f32[3,2,8,128]{3,2,1,0:T(8,128)} %v.3) | copy-start | bytes 73732
  31.1 13.7 %copy-start.4 = (s32[2,8,128]{2,1,0:T(8,128)S(1)}, s32[2,8,128]{2,1,0:T(8,128)}, u32[]{:S(2)}) copy-start(s32[2,8,128]{2,1,0:T(8,128)} %pair.5) | copy-start | bytes 24580
  31.3 13.6 %copy-start = (f32[3,8,128]{2,1,0:T(8,128)S(1)}, f32[3,8,128]{2,1,0:T(8,128)}, u32[]{:S(2)}) copy-start(f32[3,8,128]{2,1,0:T(8,128)} %ref.5) | copy-start | bytes 36868
  31.3 13.4 %collective-permute-start = (f32[1,128]{1,0:T(1,128)S(1)}, f32[1,128]{1,0:T(1,128)S(1)}, u32[]{:S(2)}, u32[]{:S(2)}) collective-permute-start(f32[1,128]{1,0:T(1,128)S(1)} %get-tuple-element.27), channel_id=1, source_target_pairs={{0,1},{1,2},{2,3},{3,4},{4,5},{5,6},{6,7},{7,8},{8,9},{9,10},{10,1... | collective-permute-start | bytes 1544 | tf_op jit(solution)/shard_map/ppermute | solution.py:285
  31.3 13.5 %copy-start.3 = (f32[2,8,128]{2,1,0:T(8,128)S(1)}, f32[2,8,128]{2,1,0:T(8,128)}, u32[]{:S(2)}) copy-start(f32[2,8,128]{2,1,0:T(8,128)} %mass.5) | copy-start | bytes 24580
  31.3 13.5 %collective-permute-start.1 = (f32[1,128]{1,0:T(1,128)S(1)}, f32[1,128]{1,0:T(1,128)S(1)}, u32[]{:S(2)}, u32[]{:S(2)}) collective-permute-start(f32[1,128]{1,0:T(1,128)S(1)} %get-tuple-element.28), channel_id=1, source_target_pairs={{1,0},{2,1},{3,2},{4,3},{5,4},{6,5},{7,6},{8,7},{9,8},{10,9},{11,1... | collective-permute-start | bytes 1544 | tf_op jit(solution)/shard_map/ppermute | solution.py:285
  44.8 0.7 %copy-start.7 = (s32[2,1,1,8,1]{3,4,2,1,0:T(1,128)S(1)}, s32[2,1,1,8,1]{3,4,2,1,0:T(1,128)}, u32[]{:S(2)}) copy-start(s32[2,1,1,8,1]{3,4,2,1,0:T(1,128)} %param.18) | copy-start | bytes 196
  46.7 4.2 %collective-permute-start.2 = (f32[1,128]{1,0:T(1,128)S(1)}, f32[1,128]{1,0:T(1,128)S(1)}, u32[]{:S(2)}, u32[]{:S(2)}) collective-permute-start(f32[1,128]{1,0:T(1,128)S(1)} %get-tuple-element.46), channel_id=1, source_target_pairs={{0,1},{1,2},{2,3},{3,4},{4,5},{5,6},{6,7},{7,8},{8,9},{9,10},{10,1... | collective-permute-start | bytes 1544 | tf_op jit(solution)/shard_map/ppermute | solution.py:285
  46.7 4.3 %collective-permute-start.3 = (f32[1,128]{1,0:T(1,128)S(1)}, f32[1,128]{1,0:T(1,128)S(1)}, u32[]{:S(2)}, u32[]{:S(2)}) collective-permute-start(f32[1,128]{1,0:T(1,128)S(1)} %get-tuple-element.47), channel_id=1, source_target_pairs={{1,0},{2,1},{3,2},{4,3},{5,4},{6,5},{7,6},{8,7},{9,8},{10,9},{11,1... | collective-permute-start | bytes 1544 | tf_op jit(solution)/shard_map/ppermute | solution.py:285

commit v8 on v6

--- a/solution.py
+++ b/solution.py
@@ -96,15 +96,15 @@
     return [(3 * (4 * k + 2 * x + e) + m, 2 * m + k, x, e) for k in range(2) for x in range(2) for e in range(2) for m in range(3)]
 
 
-def element_sums(weight, rows_of, sides, scales, at):
+def element_sums(weight, rows_of, sides, scales, at, ends=(0, 1)):
     total = {}
     for i in range(2):
         start = at + 1 - i
-        values = {c: rows_of[e][ch, pl.ds(start + x, ROWS), :] for c, ch, x, e in corners()}
+        values = {c: rows_of[e][ch, pl.ds(start + x, ROWS), :] for c, ch, x, e in corners() if e in ends}
         for k in range(2):
             for m in range(3):
                 force = None
-                for c in range(24):
+                for c in values:
                     t = weight(k, i, m, c) * values[c]
                     force = t if force is None else force + t
                 force = force * scales[pl.ds(start + sides, ROWS), :]
@@ -193,12 +193,15 @@
         dis[ch] = at_left[ch, 1:17, :] + DT * new
 
 
-def spread_kernel(stiff, entries, sided):
+def spread_kernel(stiff, entries, own, far):
     lane = lanes((24, COLS))
     for c in range(24):
-        column = jnp.broadcast_to(stiff[:, c : c + 1], (24, COLS))
-        entries[24 * c : 24 * c + 24, :] = column
-        sided[24 * c : 24 * c + 24, :] = jnp.where(lane < 64, pltpu.roll(column, 21, axis=0), column)
+        entries[24 * c : 24 * c + 24, :] = jnp.broadcast_to(stiff[:, c : c + 1], (24, COLS))
+    for c, _, _, e in corners():
+        if e == 0:
+            on_left, on_right = [entries[24 * (c + 3 * n) : 24 * (c + 3 * n) + 24, :] for n in range(2)]
+            own[24 * c : 24 * c + 24, :] = jnp.where(lane < 64, pltpu.roll(on_right, 21, axis=0), on_left)
+            far[24 * c : 24 * c + 24, :] = jnp.where(lane < 64, pltpu.roll(on_left, 21, axis=0), on_right)
 
 
 def look_up(table, owner, index, row, out):
@@ -237,7 +240,7 @@
     right[...] = turned[COLS - 1 : COLS, :]
 
 
-def inner_kernel(who, entries, table, pair, dis, vel, mass, ref, scale, base_dis, base_vel, weight, at_right, words):
+def inner_kernel(who, entries, own, table, pair, dis, vel, mass, ref, scale, base_dis, base_vel, weight, at_right, words):
     lane = lanes((ROWS, COLS))
     for b in range(ROWS):
         look_up(table, who[3, b], pair[1, b : b + 1, :], b, words)
@@ -246,26 +249,25 @@
         at_right[ch] = pltpu.roll(dis[ch], COLS - 1, axis=1)
     straight = element_sums(by_corner(entries, 0), (dis, at_right), 1, scale.at[0], 0)
     moved = element_sums(by_corner(entries, 1), (dis, at_right), 1, scale.at[0], 0)
+    edge = element_sums(by_corner(own, 0), (dis,), 1, scale.at[2], 0, ends=(0,))
+    at_edge = (lane == 0) | (lane == COLS - 1)
     for k in range(2):
         weight[k] = DT / mass[k]
         for m in range(3):
             ch = 2 * m + k
             force = jnp.where(lane == COLS - 1, 0.0, straight[ch]) + jnp.where(lane == 0, 0.0, pltpu.roll(moved[ch], 1, axis=1))
+            force = force + jnp.where(at_edge, edge[ch], 0.0)
             net = push[m] - force if k == 0 else -force
             new = vel[ch] + weight[k] * net
             base_vel[ch] = new
             base_dis[ch] = dis[ch, 1:9, :] + DT * new
 
 
-def outer_kernel(dis, base_dis, base_vel, weight, scale, sided, from_left, from_right, out_dis, out_vel, at_left, at_right):
+def outer_kernel(base_dis, base_vel, weight, scale, far, from_left, from_right, out_dis, out_vel, side):
     edges = edge_columns(from_left[...], from_right[...])
-    lane = lanes((16, COLS))
-    for ch in range(6):
-        here, side = dis[ch], edges[16 * ch : 16 * ch + 16, :]
-        at_left[ch] = jnp.where(lane < 64, side, here)
-        at_right[ch] = jnp.where(lane < 64, here, side)
-
-    forces = element_sums(by_corner(sided, 0), (at_left, at_right), 1, scale.at[2], 0)
+    for ch in range(6):
+        side[ch] = edges[16 * ch : 16 * ch + 16, :]
+    forces = element_sums(by_corner(far, 0), (side,), 1, scale.at[2], 0, ends=(0,))
     lane = lanes((ROWS, COLS))
     for m in range(3):
         for k in range(2):
@@ -317,7 +319,7 @@
         u, v, mass, mod, ref, pair, owner, from_left, from_right
     )
     above, below = swapped(down, up, "mesh")
-    entries, sided = call(spread_kernel, (struct(576, COLS), struct(576, COLS)), [VMEM])(stiff)
+    entries, own, far = call(spread_kernel, (struct(576, COLS),) * 3, [VMEM])(stiff)
     vel, dis, weight, point, index, who, scale = call(
         first_kernel,
         (
@@ -342,15 +344,15 @@
     base_dis, base_vel, weight = call(
         inner_kernel,
         (struct(6, ROWS, COLS), struct(6, ROWS, COLS), struct(2, ROWS, COLS)),
-        [VMEM] * 9,
+        [VMEM] * 10,
         [pltpu.VMEM((6, 16, COLS), F32), pltpu.VMEM((4, 8, COLS), F32)],
-    )(who, entries, tables, pair, new_dis, new_vel, mass, ref, scale)
+    )(who, entries, own, tables, pair, new_dis, new_vel, mass, ref, scale)
     return call(
         outer_kernel,
         (struct(3, 2, ROWS, COLS), struct(3, 2, ROWS, COLS)),
-        [VMEM] * 8,
-        [pltpu.VMEM((6, 16, COLS), F32)] * 2,
-    )(new_dis, base_dis, base_vel, weight, scale, sided, from_left, from_right)
+        [VMEM] * 7,
+        [pltpu.VMEM((6, 16, COLS), F32)],
+    )(base_dis, base_vel, weight, scale, far, from_left, from_right)
 
 
 def solution(mesh):

time: 49.2 us -> 49.2 us (level)
  no operation moved by 1% of the time
where the time goes in v8:
time: 49.2 us; the launch traced here: 48.8 us
  starting transfers between devices  34.7 us (71%)
  waiting for transfers between devices  9.04 us (18%)
  Pallas kernels  4.11 us (8%)
  between operations  0.85 us (2%)
    ppermute x6, starting transfers between devices, swapped(): return (lax.ppermute(to_next, axis, up), lax.ppermute(to_last, axis, down))  18.1 us
    all_to_all x1, starting transfers between devices, shards(): lax.all_to_all(table, 'mesh', split_axis=0, concat_axis=0, tiled=True)  16.6 us
    ppermute x6, waiting for transfers between devices, swapped(): return (lax.ppermute(to_next, axis, up), lax.ppermute(to_last, axis, down))  9.04 us
    pallas_call x1, Pallas kernels, shards(): call(table_kernel, struct(OWNERS, 32, COLS), [HBM] * 2, [pltpu.VMEM(x.sha...  1.62 us
  transfers between devices with their start and end apart: 7, of which 5 were waited for; matrix products, arithmetic and copies ran while one was open for 0% of the time, Pallas kernels for 3%

profile of v8, /device:TPU:30, one launch (start us, length us, event | category | flops | bytes accessed | tf_op | source)
XLA Modules:
  0.0 48.8 jit_solution(14359457311218461622)
XLA Ops:
  0.6 1.6 %shard_map.117 = f32[32,32,128]{2,1,0:T(8,128)} custom-call(f32[48,128]{1,0:T(8,128)} %bitcast.7, f32[8,128]{1,0:T(8,128)} %bitcast.8), custom_call_target="tpu_custom_call" | custom-call | flops 1000000 | bytes 1000000 | tf_op jit(solution)/shard_map/pallas_call | solution.py:303
  2.3 0.0 copy-start
  2.3 0.0 copy-start.5
  2.3 0.0 copy-start.3
  2.3 0.0 copy-start.4
  2.3 16.6 %all-to-all-start = ((f32[32,32,128]{2,1,0:T(8,128)}), f32[32,32,128]{2,1,0:T(8,128)S(1)}, u32[]{:S(2)}, u32[]{:S(2)}) async-start(f32[32,32,128]{2,1,0:T(8,128)} %shard_map.117), calls=%async_computation | async-start | bytes 1048576 | tf_op jit(solution)/shard_map/all_to_all | solution.py:316
  18.9 0.0 copy-done
  18.9 0.0 copy-done.5
  18.9 0.0 copy-start.1
  18.9 0.0 copy-start.2
  18.9 0.1 shard_map.114
  19.0 0.0 collective-permute-start
  19.0 0.0 copy-start.7
  19.0 8.6 %collective-permute-start.1 = (f32[1,128]{1,0:T(1,128)S(1)}, f32[1,128]{1,0:T(1,128)S(1)}, u32[]{:S(2)}, u32[]{:S(2)}) collective-permute-start(f32[1,128]{1,0:T(1,128)S(1)} %get-tuple-element.25), channel_id=1, source_target_pairs={{1,0},{2,1},{3,2},{4,3},{5,4},{6,5},{7,6},{8,7},{9,8},{10,9},{11,1... | collective-permute-start | bytes 1544 | tf_op jit(solution)/shard_map/ppermute | solution.py:296
  27.7 1.2 %collective-permute-done.from_left = f32[1,128]{1,0:T(1,128)S(1)} collective-permute-done((f32[1,128]{1,0:T(1,128)S(1)}, f32[1,128]{1,0:T(1,128)S(1)}, u32[]{:S(2)}, u32[]{:S(2)}) %collective-permute-start) | collective-permute-done | bytes 544 | tf_op jit(solution)/shard_map/ppermute | solution.py:296
  28.9 0.1 collective-permute-done.1.from_right
  29.0 0.0 copy-done.3
  29.0 0.0 copy-start.6
  29.0 4.6 %collective-permute-start.2 = (f32[32,128]{1,0:T(8,128)S(1)}, f32[32,128]{1,0:T(8,128)S(1)}, u32[]{:S(2)}, u32[]{:S(2)}) collective-permute-start(f32[32,128]{1,0:T(8,128)S(1)} %get-tuple-element.26), channel_id=1, source_target_pairs={{0,32},{32,64},{64,96},{96,128},{128,160},{160,192},{192,224},{224... | collective-permute-start | bytes 49160 | tf_op jit(solution)/shard_map/ppermute | solution.py:296
  33.6 1.9 %collective-permute-start.3 = (f32[32,128]{1,0:T(8,128)S(1)}, f32[32,128]{1,0:T(8,128)S(1)}, u32[]{:S(2)}, u32[]{:S(2)}) collective-permute-start(f32[32,128]{1,0:T(8,128)S(1)} %get-tuple-element.27), channel_id=1, source_target_pairs={{32,0},{64,32},{96,64},{128,96},{160,128},{192,160},{224,192},{256... | collective-permute-start | bytes 49160 | tf_op jit(solution)/shard_map/ppermute | solution.py:296
  35.6 0.2 shard_map.113
  35.8 0.0 collective-permute-done.2.above
  35.8 6.8 %collective-permute-done.3.below = f32[32,128]{1,0:T(8,128)S(1)} collective-permute-done((f32[32,128]{1,0:T(8,128)S(1)}, f32[32,128]{1,0:T(8,128)S(1)}, u32[]{:S(2)}, u32[]{:S(2)}) %collective-permute-start.3) | collective-permute-done | bytes 16416 | tf_op jit(solution)/shard_map/ppermute | solution.py:296
  42.6 0.8 %shard_map.116 = (f32[6,16,128]{2,1,0:T(8,128)S(1)}, f32[6,16,128]{2,1,0:T(8,128)S(1)}, f32[2,16,128]{2,1,0:T(8,128)S(1)}, f32[3,16,128]{2,1,0:T(8,128)S(1)}, s3...) custom-call(f32[576,128]{1,0:T(8,128)S(1)} %get-tuple-element.23.entries, ...), custom_call_target="tpu_custom_call" | custom-call | flops 1000000 | bytes 1000000 | tf_op jit(solution)/shard_map/pallas_call | solution.py:323
  43.3 0.0 all-to-all-done.table
  43.4 0.3 shard_map.118
  43.7 0.0 collective-permute-start.4
  43.7 3.0 %collective-permute-start.5 = (f32[1,128]{1,0:T(1,128)S(1)}, f32[1,128]{1,0:T(1,128)S(1)}, u32[]{:S(2)}, u32[]{:S(2)}) collective-permute-start(f32[1,128]{1,0:T(1,128)S(1)} %get-tuple-element.43), channel_id=1, source_target_pairs={{1,0},{2,1},{3,2},{4,3},{5,4},{6,5},{7,6},{8,7},{9,8},{10,9},{11,1... | collective-permute-start | bytes 1544 | tf_op jit(solution)/shard_map/ppermute | solution.py:296
  46.7 0.4 shard_map.119
  47.1 0.9 %collective-permute-done.4.from_left = f32[1,128]{1,0:T(1,128)S(1)} collective-permute-done((f32[1,128]{1,0:T(1,128)S(1)}, f32[1,128]{1,0:T(1,128)S(1)}, u32[]{:S(2)}, u32[]{:S(2)}) %collective-permute-start.4) | collective-permute-done | bytes 544 | tf_op jit(solution)/shard_map/ppermute | solution.py:296
  47.9 0.1 collective-permute-done.5.from_right
  48.0 0.8 %shard_map.120 = (f32[3,2,8,128]{3,2,1,0:T(8,128)}, f32[3,2,8,128]{3,2,1,0:T(8,128)}) custom-call(f32[6,8,128]{2,1,0:T(8,128)S(1)} %get-tuple-element.38.base_dis, f32[6,8,128]{2,1,0:T(8,128)S(1)} %get-tuple-element.39.base_vel, f32[2,8,128]{2,1,0:T(8,128)S(1)} %get-tuple-element.40.weight, f32[3,24,128]{2,1,0:T(8,128)S(1)} %get-tuple-element.37.scale, ...), custom_call_target="tpu_custom_call" | custom-call | flops 1000000 | bytes 1000000 | tf_op jit(solution)/shard_map/pallas_call | solution.py:350
  (6 shorter events, 0.0 us)
Async XLA Ops:
  2.3 16.6 %copy-start = (f32[3,2,8,128]{3,2,1,0:T(8,128)S(1)}, f32[3,2,8,128]{3,2,1,0:T(8,128)}, u32[]{:S(2)}) copy-start(f32[3,2,8,128]{3,2,1,0:T(8,128)} %u.5) | copy-start | bytes 73732
  2.3 16.6 %copy-start.5 = (f32[2,8,128]{2,1,0:T(8,128)S(1)}, f32[2,8,128]{2,1,0:T(8,128)}, u32[]{:S(2)}) copy-start(f32[2,8,128]{2,1,0:T(8,128)} %mod.5) | copy-start | bytes 24580
  2.3 26.7 %copy-start.3 = (f32[2,8,128]{2,1,0:T(8,128)S(1)}, f32[2,8,128]{2,1,0:T(8,128)}, u32[]{:S(2)}) copy-start(f32[2,8,128]{2,1,0:T(8,128)} %mass.5) | copy-start | bytes 24580
  2.3 26.7 %copy-start.4 = (s32[2,8,128]{2,1,0:T(8,128)S(1)}, s32[2,8,128]{2,1,0:T(8,128)}, u32[]{:S(2)}) copy-start(s32[2,8,128]{2,1,0:T(8,128)} %pair.5) | copy-start | bytes 24580
  2.3 41.0 %all-to-all-start = ((f32[32,32,128]{2,1,0:T(8,128)}), f32[32,32,128]{2,1,0:T(8,128)S(1)}, u32[]{:S(2)}, u32[]{:S(2)}) async-start(f32[32,32,128]{2,1,0:T(8,128)} %shard_map.117), calls=%async_computation | async-start | bytes 1048576 | tf_op jit(solution)/shard_map/all_to_all | solution.py:316
  18.9 10.1 %copy-start.1 = (f32[3,8,128]{2,1,0:T(8,128)S(1)}, f32[3,8,128]{2,1,0:T(8,128)}, u32[]{:S(2)}) copy-start(f32[3,8,128]{2,1,0:T(8,128)} %ref.5) | copy-start | bytes 36868
  18.9 10.1 %copy-start.2 = (f32[3,2,8,128]{3,2,1,0:T(8,128)S(1)}, f32[3,2,8,128]{3,2,1,0:T(8,128)}, u32[]{:S(2)}) copy-start(f32[3,2,8,128]{3,2,1,0:T(8,128)} %v.3) | copy-start | bytes 73732
  19.0 9.9 %collective-permute-start = (f32[1,128]{1,0:T(1,128)S(1)}, f32[1,128]{1,0:T(1,128)S(1)}, u32[]{:S(2)}, u32[]{:S(2)}) collective-permute-start(f32[1,128]{1,0:T(1,128)S(1)} %get-tuple-element.24), channel_id=1, source_target_pairs={{0,1},{1,2},{2,3},{3,4},{4,5},{5,6},{6,7},{7,8},{8,9},{9,10},{10,1... | collective-permute-start | bytes 1544 | tf_op jit(solution)/shard_map/ppermute | solution.py:296
  19.0 10.0 %copy-start.7 = (s32[2,1,1,8,1]{3,4,2,1,0:T(1,128)S(1)}, s32[2,1,1,8,1]{3,4,2,1,0:T(1,128)}, u32[]{:S(2)}) copy-start(s32[2,1,1,8,1]{3,4,2,1,0:T(1,128)} %param.18) | copy-start | bytes 196
  19.0 9.9 %collective-permute-start.1 = (f32[1,128]{1,0:T(1,128)S(1)}, f32[1,128]{1,0:T(1,128)S(1)}, u32[]{:S(2)}, u32[]{:S(2)}) collective-permute-start(f32[1,128]{1,0:T(1,128)S(1)} %get-tuple-element.25), channel_id=1, source_target_pairs={{1,0},{2,1},{3,2},{4,3},{5,4},{6,5},{7,6},{8,7},{9,8},{10,9},{11,1... | collective-permute-start | bytes 1544 | tf_op jit(solution)/shard_map/ppermute | solution.py:296
  29.0 6.6 %copy-start.6 = (f32[24,24]{1,0:T(8,128)S(1)}, f32[24,24]{1,0:T(8,128)}, u32[]{:S(2)}) copy-start(f32[24,24]{1,0:T(8,128)} %stiff.1) | copy-start | bytes 6916
  29.0 6.7 %collective-permute-start.2 = (f32[32,128]{1,0:T(8,128)S(1)}, f32[32,128]{1,0:T(8,128)S(1)}, u32[]{:S(2)}, u32[]{:S(2)}) collective-permute-start(f32[32,128]{1,0:T(8,128)S(1)} %get-tuple-element.26), channel_id=1, source_target_pairs={{0,32},{32,64},{64,96},{96,128},{128,160},{160,192},{192,224},{224... | collective-permute-start | bytes 49160 | tf_op jit(solution)/shard_map/ppermute | solution.py:296
  33.6 9.0 %collective-permute-start.3 = (f32[32,128]{1,0:T(8,128)S(1)}, f32[32,128]{1,0:T(8,128)S(1)}, u32[]{:S(2)}, u32[]{:S(2)}) collective-permute-start(f32[32,128]{1,0:T(8,128)S(1)} %get-tuple-element.27), channel_id=1, source_target_pairs={{32,0},{64,32},{96,64},{128,96},{160,128},{192,160},{224,192},{256... | collective-permute-start | bytes 49160 | tf_op jit(solution)/shard_map/ppermute | solution.py:296
  43.7 4.2 %collective-permute-start.4 = (f32[1,128]{1,0:T(1,128)S(1)}, f32[1,128]{1,0:T(1,128)S(1)}, u32[]{:S(2)}, u32[]{:S(2)}) collective-permute-start(f32[1,128]{1,0:T(1,128)S(1)} %get-tuple-element.42), channel_id=1, source_target_pairs={{0,1},{1,2},{2,3},{3,4},{4,5},{5,6},{6,7},{7,8},{8,9},{9,10},{10,1... | collective-permute-start | bytes 1544 | tf_op jit(solution)/shard_map/ppermute | solution.py:296
  43.7 4.3 %collective-permute-start.5 = (f32[1,128]{1,0:T(1,128)S(1)}, f32[1,128]{1,0:T(1,128)S(1)}, u32[]{:S(2)}, u32[]{:S(2)}) collective-permute-start(f32[1,128]{1,0:T(1,128)S(1)} %get-tuple-element.43), channel_id=1, source_target_pairs={{1,0},{2,1},{3,2},{4,3},{5,4},{6,5},{7,6},{8,7},{9,8},{10,9},{11,1... | collective-permute-start | bytes 1544 | tf_op jit(solution)/shard_map/ppermute | solution.py:296

commit v9 on v8

--- a/solution.py
+++ b/solution.py
@@ -55,7 +55,7 @@
     right[...] = turned[COLS - 1 : COLS, :]
 
 
-def pack_kernel(u, v, mass, mod, ref, pair, own, from_left, from_right, up, down):
+def pack_kernel(odd, u, v, mass, mod, ref, pair, own, from_left, from_right, before, after, up, down):
     for out, two, one in ((down, ROWS - 2, ROWS - 1), (up, 0, 0)):
         for m in range(3):
             for k in range(2):
@@ -71,6 +71,9 @@
         out[AT_O : AT_O + 1, 0:ROWS] = own[0].astype(F32)
         out[AT_L : AT_L + 1, :] = from_left[...]
         out[AT_R : AT_R + 1, :] = from_right[...]
+    here = odd[...] == 1
+    before[...] = jnp.where(here, down[...], up[...])
+    after[...] = jnp.where(here, up[...], down[...])
 
 
 def extended(here, above, below):
@@ -121,7 +124,10 @@
     return slice(at, at + 1)
 
 
-def first_kernel(entries, owner, from_left, from_right, above, below, u, v, mass, mod, ref, pair, vel, dis, weight, point, index, who, scale, at_left, at_right, at_edge):
+def first_kernel(odd, entries, owner, from_left, from_right, before, after, u, v, mass, mod, ref, pair, vel, dis, weight, point, index, who, scale, at_left, at_right, at_edge, above, below):
+    here = odd[...] == 1
+    above[...] = jnp.where(here, after[...], before[...])
+    below[...] = jnp.where(here, before[...], after[...])
     edges = edge_columns(
         extended(from_left[...], above[AT_L : AT_L + 1, :], below[AT_L : AT_L + 1, :]),
         extended(from_right[...], above[AT_R : AT_R + 1, :], below[AT_R : AT_R + 1, :]),
@@ -296,6 +302,12 @@
     return lax.ppermute(to_next, axis, up), lax.ppermute(to_last, axis, down)
 
 
+def paired(array, axis, start):
+    size = lax.axis_size(axis)
+    pairs = [(i, (i + 1) % size) for i in range(start, size, 2)]
+    return lax.ppermute(array, axis, pairs + [(j, i) for i, j in pairs])
+
+
 def shards(u, v, mass, mod, stiff, ref, facets, penalty, owners, pair):
     width = facets.shape[-1]
     owner = owners.reshape(2, 1, ROWS)
@@ -315,10 +327,12 @@
     )(u, mod)
     tables = lax.all_to_all(table, "mesh", split_axis=0, concat_axis=0, tiled=True)
     from_left, from_right = swapped(right, left, "sub")
-    up, down = call(pack_kernel, (struct(MSG, COLS), struct(MSG, COLS)), [VMEM] * 9)(
-        u, v, mass, mod, ref, pair, owner, from_left, from_right
+    rows = [pltpu.VMEM((MSG, COLS), F32)] * 2
+    odd = jnp.full((1, COLS), lax.axis_index("mesh") % 2, jnp.int32)
+    before, after = call(pack_kernel, (struct(MSG, COLS), struct(MSG, COLS)), [VMEM] * 10, rows)(
+        odd, u, v, mass, mod, ref, pair, owner, from_left, from_right
     )
-    above, below = swapped(down, up, "mesh")
+    before, after = paired(before, "mesh", 1), paired(after, "mesh", 0)
     entries, own, far = call(spread_kernel, (struct(576, COLS),) * 3, [VMEM])(stiff)
     vel, dis, weight, point, index, who, scale = call(
         first_kernel,
@@ -331,9 +345,9 @@
             struct(8, COLS, dtype=jnp.int32),
             struct(3, 24, COLS),
         ),
-        [VMEM] * 12,
-        [pltpu.VMEM((8, 24, COLS), F32)] * 3,
-    )(entries, owner, from_left, from_right, above, below, u, v, mass, mod, ref, pair)
+        [VMEM] * 13,
+        [pltpu.VMEM((8, 24, COLS), F32)] * 3 + rows,
+    )(odd, entries, owner, from_left, from_right, before, after, u, v, mass, mod, ref, pair)
     new_vel, new_dis, left, right = call(
         contact_kernel,
         (struct(6, ROWS, COLS), struct(6, 16, COLS), struct(1, COLS), struct(1, COLS)),

time: 49.2 us -> 46.9 us (0.953)
  the two profiles are of different devices: /device:TPU:30 before, /device:TPU:2 now
where the time goes in v9:
time: 46.9 us; the launch traced here: 46.6 us
  starting transfers between devices  37.7 us (80%)
  Pallas kernels  4.25 us (9%)
  waiting for transfers between devices  3.69 us (8%)
  between operations  0.84 us (2%)
    all_to_all x1, starting transfers between devices, shards(): lax.all_to_all(table, 'mesh', split_axis=0, concat_axis=0, tiled=True)  16.7 us
    ppermute x4, starting transfers between devices, swapped(): return (lax.ppermute(to_next, axis, up), lax.ppermute(to_last, axis, down))  11.7 us
    ppermute x2, starting transfers between devices, paired(): return lax.ppermute(array, axis, pairs + [(j, i) for i, j in pairs])  9.26 us
    ppermute x4, waiting for transfers between devices, swapped(): return (lax.ppermute(to_next, axis, up), lax.ppermute(to_last, axis, down))  2.19 us
    pallas_call x1, Pallas kernels, shards(): call(table_kernel, struct(OWNERS, 32, COLS), [HBM] * 2, [pltpu.VMEM(x.sha...  1.62 us
    ppermute x2, waiting for transfers between devices, paired(): return lax.ppermute(array, axis, pairs + [(j, i) for i, j in pairs])  1.5 us
  transfers between devices with their start and end apart: 7, of which 5 were waited for; matrix products, arithmetic and copies ran while one was open for 0% of the time, Pallas kernels for 3%

profile of v9, /device:TPU:2, one launch (start us, length us, event | category | flops | bytes accessed | tf_op | source)
XLA Modules:
  0.0 46.6 jit_solution(3803493037824210450)
XLA Ops:
  0.6 1.6 %shard_map.117 = f32[32,32,128]{2,1,0:T(8,128)} custom-call(f32[48,128]{1,0:T(8,128)} %bitcast.7, f32[8,128]{1,0:T(8,128)} %bitcast.8), custom_call_target="tpu_custom_call" | custom-call | flops 1000000 | bytes 1000000 | tf_op jit(solution)/shard_map/pallas_call | solution.py:315
  2.3 0.0 copy-start
  2.3 0.0 copy-start.5
  2.3 16.7 %all-to-all-start = ((f32[32,32,128]{2,1,0:T(8,128)}), f32[32,32,128]{2,1,0:T(8,128)S(1)}, u32[]{:S(2)}, u32[]{:S(2)}) async-start(f32[32,32,128]{2,1,0:T(8,128)} %shard_map.117), calls=%async_computation | async-start | bytes 1048576 | tf_op jit(solution)/shard_map/all_to_all | solution.py:328
  19.0 0.0 copy-done
  19.0 0.0 copy-done.5
  19.0 0.0 copy-start.3
  19.1 0.0 copy-start.4
  19.1 0.0 copy-start.7
  19.1 0.1 shard_map.114
  19.2 0.0 copy-start.2
  19.2 0.0 collective-permute-start
  19.2 8.7 %collective-permute-start.1 = (f32[1,128]{1,0:T(1,128)S(1)}, f32[1,128]{1,0:T(1,128)S(1)}, u32[]{:S(2)}, u32[]{:S(2)}) collective-permute-start(f32[1,128]{1,0:T(1,128)S(1)} %get-tuple-element.25), channel_id=1, source_target_pairs={{1,0},{2,1},{3,2},{4,3},{5,4},{6,5},{7,6},{8,7},{9,8},{10,9},{11,1... | collective-permute-start | bytes 1544 | tf_op jit(solution)/shard_map/ppermute | solution.py:302
  27.9 1.2 %collective-permute-done.from_left = f32[1,128]{1,0:T(1,128)S(1)} collective-permute-done((f32[1,128]{1,0:T(1,128)S(1)}, f32[1,128]{1,0:T(1,128)S(1)}, u32[]{:S(2)}, u32[]{:S(2)}) %collective-permute-start) | collective-permute-done | bytes 544 | tf_op jit(solution)/shard_map/ppermute | solution.py:302
  29.1 0.1 collective-permute-done.1.from_right
  29.2 0.0 copy-done.3
  29.2 0.0 copy-done.4
  29.3 0.0 copy-start.6
  29.3 3.4 %collective-permute-start.2 = (f32[32,128]{1,0:T(8,128)S(1)}, f32[32,128]{1,0:T(8,128)S(1)}, u32[]{:S(2)}, u32[]{:S(2)}) collective-permute-start(f32[32,128]{1,0:T(8,128)S(1)} %get-tuple-element.26), channel_id=1, source_target_pairs={{32,64},{96,128},{160,192},{224,256},{288,320},{352,384},{416,448}... | collective-permute-start | bytes 49160 | tf_op jit(solution)/shard_map/ppermute | solution.py:308
  32.7 5.9 %collective-permute-start.3 = (f32[32,128]{1,0:T(8,128)S(1)}, f32[32,128]{1,0:T(8,128)S(1)}, u32[]{:S(2)}, u32[]{:S(2)}) collective-permute-start(f32[32,128]{1,0:T(8,128)S(1)} %get-tuple-element.27), channel_id=1, source_target_pairs={{0,32},{64,96},{128,160},{192,224},{256,288},{320,352},{384,416},{... | collective-permute-start | bytes 49160 | tf_op jit(solution)/shard_map/ppermute | solution.py:308
  38.6 0.2 shard_map.113
  38.8 0.0 collective-permute-done.2.before
  38.8 1.5 %collective-permute-done.3.after = f32[32,128]{1,0:T(8,128)S(1)} collective-permute-done((f32[32,128]{1,0:T(8,128)S(1)}, f32[32,128]{1,0:T(8,128)S(1)}, u32[]{:S(2)}, u32[]{:S(2)}) %collective-permute-start.3) | collective-permute-done | bytes 16416 | tf_op jit(solution)/shard_map/ppermute | solution.py:308
  40.3 0.9 %shard_map.116 = (f32[6,16,128]{2,1,0:T(8,128)S(1)}, f32[6,16,128]{2,1,0:T(8,128)S(1)}, f32[2,16,128]{2,1,0:T(8,128)S(1)}, f32[3,16,128]{2,1,0:T(8,128)S(1)}, s3...) custom-call(s32[1,128]{1,0:T(1,128)S(1)} %broadcast_in_dim.3.odd, ...), custom_call_target="tpu_custom_call" | custom-call | flops 1000000 | bytes 1000000 | tf_op jit(solution)/shard_map/pallas_call | solution.py:337
  41.1 0.0 all-to-all-done.table
  41.2 0.3 shard_map.118
  41.5 0.0 collective-permute-start.4
  41.5 3.0 %collective-permute-start.5 = (f32[1,128]{1,0:T(1,128)S(1)}, f32[1,128]{1,0:T(1,128)S(1)}, u32[]{:S(2)}, u32[]{:S(2)}) collective-permute-start(f32[1,128]{1,0:T(1,128)S(1)} %get-tuple-element.43), channel_id=1, source_target_pairs={{1,0},{2,1},{3,2},{4,3},{5,4},{6,5},{7,6},{8,7},{9,8},{10,9},{11,1... | collective-permute-start | bytes 1544 | tf_op jit(solution)/shard_map/ppermute | solution.py:302
  44.5 0.4 shard_map.119
  44.9 0.8 %collective-permute-done.4.from_left = f32[1,128]{1,0:T(1,128)S(1)} collective-permute-done((f32[1,128]{1,0:T(1,128)S(1)}, f32[1,128]{1,0:T(1,128)S(1)}, u32[]{:S(2)}, u32[]{:S(2)}) %collective-permute-start.4) | collective-permute-done | bytes 544 | tf_op jit(solution)/shard_map/ppermute | solution.py:302
  45.7 0.1 collective-permute-done.5.from_right
  45.8 0.8 %shard_map.120 = (f32[3,2,8,128]{3,2,1,0:T(8,128)}, f32[3,2,8,128]{3,2,1,0:T(8,128)}) custom-call(f32[6,8,128]{2,1,0:T(8,128)S(1)} %get-tuple-element.38.base_dis, f32[6,8,128]{2,1,0:T(8,128)S(1)} %get-tuple-element.39.base_vel, f32[2,8,128]{2,1,0:T(8,128)S(1)} %get-tuple-element.40.weight, f32[3,24,128]{2,1,0:T(8,128)S(1)} %get-tuple-element.37.scale, ...), custom_call_target="tpu_custom_call" | custom-call | flops 1000000 | bytes 1000000 | tf_op jit(solution)/shard_map/pallas_call | solution.py:364
  (7 shorter events, 0.0 us)
Async XLA Ops:
  2.3 16.8 %copy-start = (f32[3,2,8,128]{3,2,1,0:T(8,128)S(1)}, f32[3,2,8,128]{3,2,1,0:T(8,128)}, u32[]{:S(2)}) copy-start(f32[3,2,8,128]{3,2,1,0:T(8,128)} %u.5) | copy-start | bytes 73732
  2.3 16.8 %copy-start.5 = (f32[2,8,128]{2,1,0:T(8,128)S(1)}, f32[2,8,128]{2,1,0:T(8,128)}, u32[]{:S(2)}) copy-start(f32[2,8,128]{2,1,0:T(8,128)} %mod.5) | copy-start | bytes 24580
  2.3 38.9 %all-to-all-start = ((f32[32,32,128]{2,1,0:T(8,128)}), f32[32,32,128]{2,1,0:T(8,128)S(1)}, u32[]{:S(2)}, u32[]{:S(2)}) async-start(f32[32,32,128]{2,1,0:T(8,128)} %shard_map.117), calls=%async_computation | async-start | bytes 1048576 | tf_op jit(solution)/shard_map/all_to_all | solution.py:328
  19.0 10.2 %copy-start.3 = (f32[2,8,128]{2,1,0:T(8,128)S(1)}, f32[2,8,128]{2,1,0:T(8,128)}, u32[]{:S(2)}) copy-start(f32[2,8,128]{2,1,0:T(8,128)} %mass.5) | copy-start | bytes 24580
  19.1 10.2 %copy-start.4 = (s32[2,8,128]{2,1,0:T(8,128)S(1)}, s32[2,8,128]{2,1,0:T(8,128)}, u32[]{:S(2)}) copy-start(s32[2,8,128]{2,1,0:T(8,128)} %pair.5) | copy-start | bytes 24580
  19.1 10.2 %copy-start.7 = (s32[2,1,1,8,1]{3,4,2,1,0:T(1,128)S(1)}, s32[2,1,1,8,1]{3,4,2,1,0:T(1,128)}, u32[]{:S(2)}) copy-start(s32[2,1,1,8,1]{3,4,2,1,0:T(1,128)} %param.18) | copy-start | bytes 196
  19.2 10.1 %copy-start.2 = (f32[3,2,8,128]{3,2,1,0:T(8,128)S(1)}, f32[3,2,8,128]{3,2,1,0:T(8,128)}, u32[]{:S(2)}) copy-start(f32[3,2,8,128]{3,2,1,0:T(8,128)} %v.3) | copy-start | bytes 73732
  19.2 10.0 %collective-permute-start = (f32[1,128]{1,0:T(1,128)S(1)}, f32[1,128]{1,0:T(1,128)S(1)}, u32[]{:S(2)}, u32[]{:S(2)}) collective-permute-start(f32[1,128]{1,0:T(1,128)S(1)} %get-tuple-element.24), channel_id=1, source_target_pairs={{0,1},{1,2},{2,3},{3,4},{4,5},{5,6},{6,7},{7,8},{8,9},{9,10},{10,1... | collective-permute-start | bytes 1544 | tf_op jit(solution)/shard_map/ppermute | solution.py:302
  19.2 10.0 %collective-permute-start.1 = (f32[1,128]{1,0:T(1,128)S(1)}, f32[1,128]{1,0:T(1,128)S(1)}, u32[]{:S(2)}, u32[]{:S(2)}) collective-permute-start(f32[1,128]{1,0:T(1,128)S(1)} %get-tuple-element.25), channel_id=1, source_target_pairs={{1,0},{2,1},{3,2},{4,3},{5,4},{6,5},{7,6},{8,7},{9,8},{10,9},{11,1... | collective-permute-start | bytes 1544 | tf_op jit(solution)/shard_map/ppermute | solution.py:302
  27.9 1.3 %copy-start.1 = (f32[3,8,128]{2,1,0:T(8,128)S(1)}, f32[3,8,128]{2,1,0:T(8,128)}, u32[]{:S(2)}) copy-start(f32[3,8,128]{2,1,0:T(8,128)} %ref.5) | copy-start | bytes 36868
  29.3 9.3 %copy-start.6 = (f32[24,24]{1,0:T(8,128)S(1)}, f32[24,24]{1,0:T(8,128)}, u32[]{:S(2)}) copy-start(f32[24,24]{1,0:T(8,128)} %stiff.1) | copy-start | bytes 6916
  29.3 9.5 %collective-permute-start.2 = (f32[32,128]{1,0:T(8,128)S(1)}, f32[32,128]{1,0:T(8,128)S(1)}, u32[]{:S(2)}, u32[]{:S(2)}) collective-permute-start(f32[32,128]{1,0:T(8,128)S(1)} %get-tuple-element.26), channel_id=1, source_target_pairs={{32,64},{96,128},{160,192},{224,256},{288,320},{352,384},{416,448}... | collective-permute-start | bytes 49160 | tf_op jit(solution)/shard_map/ppermute | solution.py:308
  32.7 7.6 %collective-permute-start.3 = (f32[32,128]{1,0:T(8,128)S(1)}, f32[32,128]{1,0:T(8,128)S(1)}, u32[]{:S(2)}, u32[]{:S(2)}) collective-permute-start(f32[32,128]{1,0:T(8,128)S(1)} %get-tuple-element.27), channel_id=1, source_target_pairs={{0,32},{64,96},{128,160},{192,224},{256,288},{320,352},{384,416},{... | collective-permute-start | bytes 49160 | tf_op jit(solution)/shard_map/ppermute | solution.py:308
  41.5 4.2 %collective-permute-start.4 = (f32[1,128]{1,0:T(1,128)S(1)}, f32[1,128]{1,0:T(1,128)S(1)}, u32[]{:S(2)}, u32[]{:S(2)}) collective-permute-start(f32[1,128]{1,0:T(1,128)S(1)} %get-tuple-element.42), channel_id=1, source_target_pairs={{0,1},{1,2},{2,3},{3,4},{4,5},{5,6},{6,7},{7,8},{8,9},{9,10},{10,1... | collective-permute-start | bytes 1544 | tf_op jit(solution)/shard_map/ppermute | solution.py:302
  41.5 4.3 %collective-permute-start.5 = (f32[1,128]{1,0:T(1,128)S(1)}, f32[1,128]{1,0:T(1,128)S(1)}, u32[]{:S(2)}, u32[]{:S(2)}) collective-permute-start(f32[1,128]{1,0:T(1,128)S(1)} %get-tuple-element.43), channel_id=1, source_target_pairs={{1,0},{2,1},{3,2},{4,3},{5,4},{6,5},{7,6},{8,7},{9,8},{10,9},{11,1... | collective-permute-start | bytes 1544 | tf_op jit(solution)/shard_map/ppermute | solution.py:302

commit v10 on v9

--- a/solution.py
+++ b/solution.py
@@ -269,18 +269,24 @@
             base_dis[ch] = dis[ch, 1:9, :] + DT * new
 
 
-def outer_kernel(base_dis, base_vel, weight, scale, far, from_left, from_right, out_dis, out_vel, side):
+def outer_kernel(base_dis, base_vel, weight, scale, far, from_left, from_right, out_dis, out_vel, side, dis, vel, sems):
     edges = edge_columns(from_left[...], from_right[...])
     for ch in range(6):
         side[ch] = edges[16 * ch : 16 * ch + 16, :]
     forces = element_sums(by_corner(far, 0), (side,), 1, scale.at[2], 0, ends=(0,))
     lane = lanes((ROWS, COLS))
+    copies = []
     for m in range(3):
         for k in range(2):
             ch = 2 * m + k
             change = weight[k] * jnp.where((lane == 0) | (lane == COLS - 1), forces[ch], 0.0)
-            out_vel[m, k] = base_vel[ch] - change
-            out_dis[m, k] = base_dis[ch] - DT * change
+            vel[m, k] = base_vel[ch] - change
+            dis[m, k] = base_dis[ch] - DT * change
+        copies += [pltpu.make_async_copy(a.at[m], b.at[m], sems.at[n, m]) for n, (a, b) in enumerate(((dis, out_dis), (vel, out_vel)))]
+        for copy in copies[-2:]:
+            copy.start()
+    for copy in copies:
+        copy.wait()
 
 
 def call(kernel, outs, specs, scratch=(), room=16, out_specs=None, flops=1_000_000, moved=1_000_000):
@@ -365,7 +371,8 @@
         outer_kernel,
         (struct(3, 2, ROWS, COLS), struct(3, 2, ROWS, COLS)),
         [VMEM] * 7,
-        [pltpu.VMEM((6, 16, COLS), F32)],
+        [pltpu.VMEM((6, 16, COLS), F32)] + [pltpu.VMEM((3, 2, ROWS, COLS), F32)] * 2 + [pltpu.SemaphoreType.DMA((2, 3))],
+        out_specs=(HBM, HBM),
     )(base_dis, base_vel, weight, scale, far, from_left, from_right)
 
 

time: 46.9 us -> 47 us (level)
  no operation moved by 1% of the time
where the time goes in v10:
time: 47 us; the launch traced here: 46.6 us
  starting transfers between devices  37.7 us (80%)
  Pallas kernels  4.29 us (9%)
  waiting for transfers between devices  3.69 us (8%)
  between operations  0.84 us (2%)
    all_to_all x1, starting transfers between devices, shards(): lax.all_to_all(table, 'mesh', split_axis=0, concat_axis=0, tiled=True)  16.7 us
    ppermute x4, starting transfers between devices, swapped(): return (lax.ppermute(to_next, axis, up), lax.ppermute(to_last, axis, down))  11.7 us
    ppermute x2, starting transfers between devices, paired(): return lax.ppermute(array, axis, pairs + [(j, i) for i, j in pairs])  9.26 us
    ppermute x4, waiting for transfers between devices, swapped(): return (lax.ppermute(to_next, axis, up), lax.ppermute(to_last, axis, down))  2.19 us
    pallas_call x1, Pallas kernels, shards(): call(table_kernel, struct(OWNERS, 32, COLS), [HBM] * 2, [pltpu.VMEM(x.sha...  1.62 us
    ppermute x2, waiting for transfers between devices, paired(): return lax.ppermute(array, axis, pairs + [(j, i) for i, j in pairs])  1.5 us
  transfers between devices with their start and end apart: 7, of which 5 were waited for; matrix products, arithmetic and copies ran while one was open for 0% of the time, Pallas kernels for 3%

profile of v10, /device:TPU:2, one launch (start us, length us, event | category | flops | bytes accessed | tf_op | source)
XLA Modules:
  0.0 46.6 jit_solution(11329753752615732618)
XLA Ops:
  0.6 1.6 %shard_map.117 = f32[32,32,128]{2,1,0:T(8,128)} custom-call(f32[48,128]{1,0:T(8,128)} %bitcast.7, f32[8,128]{1,0:T(8,128)} %bitcast.8), custom_call_target="tpu_custom_call" | custom-call | flops 1000000 | bytes 1000000 | tf_op jit(solution)/shard_map/pallas_call | solution.py:321
  2.3 0.0 copy-start
  2.3 0.0 copy-start.5
  2.3 16.7 %all-to-all-start = ((f32[32,32,128]{2,1,0:T(8,128)}), f32[32,32,128]{2,1,0:T(8,128)S(1)}, u32[]{:S(2)}, u32[]{:S(2)}) async-start(f32[32,32,128]{2,1,0:T(8,128)} %shard_map.117), calls=%async_computation | async-start | bytes 1048576 | tf_op jit(solution)/shard_map/all_to_all | solution.py:334
  19.0 0.0 copy-done
  19.0 0.0 copy-done.5
  19.0 0.0 copy-start.3
  19.1 0.0 copy-start.4
  19.1 0.0 copy-start.7
  19.1 0.1 shard_map.114
  19.2 0.0 copy-start.2
  19.2 0.0 collective-permute-start
  19.2 8.7 %collective-permute-start.1 = (f32[1,128]{1,0:T(1,128)S(1)}, f32[1,128]{1,0:T(1,128)S(1)}, u32[]{:S(2)}, u32[]{:S(2)}) collective-permute-start(f32[1,128]{1,0:T(1,128)S(1)} %get-tuple-element.25), channel_id=1, source_target_pairs={{1,0},{2,1},{3,2},{4,3},{5,4},{6,5},{7,6},{8,7},{9,8},{10,9},{11,1... | collective-permute-start | bytes 1544 | tf_op jit(solution)/shard_map/ppermute | solution.py:308
  27.9 1.2 %collective-permute-done.from_left = f32[1,128]{1,0:T(1,128)S(1)} collective-permute-done((f32[1,128]{1,0:T(1,128)S(1)}, f32[1,128]{1,0:T(1,128)S(1)}, u32[]{:S(2)}, u32[]{:S(2)}) %collective-permute-start) | collective-permute-done | bytes 544 | tf_op jit(solution)/shard_map/ppermute | solution.py:308
  29.1 0.1 collective-permute-done.1.from_right
  29.2 0.0 copy-done.3
  29.2 0.0 copy-done.4
  29.3 0.0 copy-start.6
  29.3 3.4 %collective-permute-start.2 = (f32[32,128]{1,0:T(8,128)S(1)}, f32[32,128]{1,0:T(8,128)S(1)}, u32[]{:S(2)}, u32[]{:S(2)}) collective-permute-start(f32[32,128]{1,0:T(8,128)S(1)} %get-tuple-element.26), channel_id=1, source_target_pairs={{32,64},{96,128},{160,192},{224,256},{288,320},{352,384},{416,448}... | collective-permute-start | bytes 49160 | tf_op jit(solution)/shard_map/ppermute | solution.py:314
  32.7 5.9 %collective-permute-start.3 = (f32[32,128]{1,0:T(8,128)S(1)}, f32[32,128]{1,0:T(8,128)S(1)}, u32[]{:S(2)}, u32[]{:S(2)}) collective-permute-start(f32[32,128]{1,0:T(8,128)S(1)} %get-tuple-element.27), channel_id=1, source_target_pairs={{0,32},{64,96},{128,160},{192,224},{256,288},{320,352},{384,416},{... | collective-permute-start | bytes 49160 | tf_op jit(solution)/shard_map/ppermute | solution.py:314
  38.6 0.2 shard_map.113
  38.8 0.0 collective-permute-done.2.before
  38.8 1.5 %collective-permute-done.3.after = f32[32,128]{1,0:T(8,128)S(1)} collective-permute-done((f32[32,128]{1,0:T(8,128)S(1)}, f32[32,128]{1,0:T(8,128)S(1)}, u32[]{:S(2)}, u32[]{:S(2)}) %collective-permute-start.3) | collective-permute-done | bytes 16416 | tf_op jit(solution)/shard_map/ppermute | solution.py:314
  40.3 0.9 %shard_map.116 = (f32[6,16,128]{2,1,0:T(8,128)S(1)}, f32[6,16,128]{2,1,0:T(8,128)S(1)}, f32[2,16,128]{2,1,0:T(8,128)S(1)}, f32[3,16,128]{2,1,0:T(8,128)S(1)}, s3...) custom-call(s32[1,128]{1,0:T(1,128)S(1)} %broadcast_in_dim.3.odd, ...), custom_call_target="tpu_custom_call" | custom-call | flops 1000000 | bytes 1000000 | tf_op jit(solution)/shard_map/pallas_call | solution.py:343
  41.1 0.0 all-to-all-done.table
  41.2 0.3 shard_map.118
  41.5 0.0 collective-permute-start.4
  41.5 3.0 %collective-permute-start.5 = (f32[1,128]{1,0:T(1,128)S(1)}, f32[1,128]{1,0:T(1,128)S(1)}, u32[]{:S(2)}, u32[]{:S(2)}) collective-permute-start(f32[1,128]{1,0:T(1,128)S(1)} %get-tuple-element.43), channel_id=1, source_target_pairs={{1,0},{2,1},{3,2},{4,3},{5,4},{6,5},{7,6},{8,7},{9,8},{10,9},{11,1... | collective-permute-start | bytes 1544 | tf_op jit(solution)/shard_map/ppermute | solution.py:308
  44.5 0.4 shard_map.119
  44.9 0.8 %collective-permute-done.4.from_left = f32[1,128]{1,0:T(1,128)S(1)} collective-permute-done((f32[1,128]{1,0:T(1,128)S(1)}, f32[1,128]{1,0:T(1,128)S(1)}, u32[]{:S(2)}, u32[]{:S(2)}) %collective-permute-start.4) | collective-permute-done | bytes 544 | tf_op jit(solution)/shard_map/ppermute | solution.py:308
  45.7 0.1 collective-permute-done.5.from_right
  45.8 0.8 %shard_map.120 = (f32[3,2,8,128]{3,2,1,0:T(8,128)}, f32[3,2,8,128]{3,2,1,0:T(8,128)}) custom-call(f32[6,8,128]{2,1,0:T(8,128)S(1)} %get-tuple-element.38.base_dis, f32[6,8,128]{2,1,0:T(8,128)S(1)} %get-tuple-element.39.base_vel, f32[2,8,128]{2,1,0:T(8,128)S(1)} %get-tuple-element.40.weight, f32[3,24,128]{2,1,0:T(8,128)S(1)} %get-tuple-element.37.scale, ...), custom_call_target="tpu_custom_call" | custom-call | flops 1000000 | bytes 1000000 | tf_op jit(solution)/shard_map/pallas_call | solution.py:370
  (7 shorter events, 0.0 us)
Async XLA Ops:
  2.3 16.8 %copy-start = (f32[3,2,8,128]{3,2,1,0:T(8,128)S(1)}, f32[3,2,8,128]{3,2,1,0:T(8,128)}, u32[]{:S(2)}) copy-start(f32[3,2,8,128]{3,2,1,0:T(8,128)} %u.5) | copy-start | bytes 73732
  2.3 16.8 %copy-start.5 = (f32[2,8,128]{2,1,0:T(8,128)S(1)}, f32[2,8,128]{2,1,0:T(8,128)}, u32[]{:S(2)}) copy-start(f32[2,8,128]{2,1,0:T(8,128)} %mod.5) | copy-start | bytes 24580
  2.3 38.9 %all-to-all-start = ((f32[32,32,128]{2,1,0:T(8,128)}), f32[32,32,128]{2,1,0:T(8,128)S(1)}, u32[]{:S(2)}, u32[]{:S(2)}) async-start(f32[32,32,128]{2,1,0:T(8,128)} %shard_map.117), calls=%async_computation | async-start | bytes 1048576 | tf_op jit(solution)/shard_map/all_to_all | solution.py:334
  19.0 10.2 %copy-start.3 = (f32[2,8,128]{2,1,0:T(8,128)S(1)}, f32[2,8,128]{2,1,0:T(8,128)}, u32[]{:S(2)}) copy-start(f32[2,8,128]{2,1,0:T(8,128)} %mass.5) | copy-start | bytes 24580
  19.1 10.2 %copy-start.4 = (s32[2,8,128]{2,1,0:T(8,128)S(1)}, s32[2,8,128]{2,1,0:T(8,128)}, u32[]{:S(2)}) copy-start(s32[2,8,128]{2,1,0:T(8,128)} %pair.5) | copy-start | bytes 24580
  19.1 10.2 %copy-start.7 = (s32[2,1,1,8,1]{3,4,2,1,0:T(1,128)S(1)}, s32[2,1,1,8,1]{3,4,2,1,0:T(1,128)}, u32[]{:S(2)}) copy-start(s32[2,1,1,8,1]{3,4,2,1,0:T(1,128)} %param.18) | copy-start | bytes 196
  19.2 10.1 %copy-start.2 = (f32[3,2,8,128]{3,2,1,0:T(8,128)S(1)}, f32[3,2,8,128]{3,2,1,0:T(8,128)}, u32[]{:S(2)}) copy-start(f32[3,2,8,128]{3,2,1,0:T(8,128)} %v.3) | copy-start | bytes 73732
  19.2 10.0 %collective-permute-start = (f32[1,128]{1,0:T(1,128)S(1)}, f32[1,128]{1,0:T(1,128)S(1)}, u32[]{:S(2)}, u32[]{:S(2)}) collective-permute-start(f32[1,128]{1,0:T(1,128)S(1)} %get-tuple-element.24), channel_id=1, source_target_pairs={{0,1},{1,2},{2,3},{3,4},{4,5},{5,6},{6,7},{7,8},{8,9},{9,10},{10,1... | collective-permute-start | bytes 1544 | tf_op jit(solution)/shard_map/ppermute | solution.py:308
  19.2 10.0 %collective-permute-start.1 = (f32[1,128]{1,0:T(1,128)S(1)}, f32[1,128]{1,0:T(1,128)S(1)}, u32[]{:S(2)}, u32[]{:S(2)}) collective-permute-start(f32[1,128]{1,0:T(1,128)S(1)} %get-tuple-element.25), channel_id=1, source_target_pairs={{1,0},{2,1},{3,2},{4,3},{5,4},{6,5},{7,6},{8,7},{9,8},{10,9},{11,1... | collective-permute-start | bytes 1544 | tf_op jit(solution)/shard_map/ppermute | solution.py:308
  27.9 1.3 %copy-start.1 = (f32[3,8,128]{2,1,0:T(8,128)S(1)}, f32[3,8,128]{2,1,0:T(8,128)}, u32[]{:S(2)}) copy-start(f32[3,8,128]{2,1,0:T(8,128)} %ref.5) | copy-start | bytes 36868
  29.3 9.3 %copy-start.6 = (f32[24,24]{1,0:T(8,128)S(1)}, f32[24,24]{1,0:T(8,128)}, u32[]{:S(2)}) copy-start(f32[24,24]{1,0:T(8,128)} %stiff.1) | copy-start | bytes 6916
  29.3 9.5 %collective-permute-start.2 = (f32[32,128]{1,0:T(8,128)S(1)}, f32[32,128]{1,0:T(8,128)S(1)}, u32[]{:S(2)}, u32[]{:S(2)}) collective-permute-start(f32[32,128]{1,0:T(8,128)S(1)} %get-tuple-element.26), channel_id=1, source_target_pairs={{32,64},{96,128},{160,192},{224,256},{288,320},{352,384},{416,448}... | collective-permute-start | bytes 49160 | tf_op jit(solution)/shard_map/ppermute | solution.py:314
  32.7 7.6 %collective-permute-start.3 = (f32[32,128]{1,0:T(8,128)S(1)}, f32[32,128]{1,0:T(8,128)S(1)}, u32[]{:S(2)}, u32[]{:S(2)}) collective-permute-start(f32[32,128]{1,0:T(8,128)S(1)} %get-tuple-element.27), channel_id=1, source_target_pairs={{0,32},{64,96},{128,160},{192,224},{256,288},{320,352},{384,416},{... | collective-permute-start | bytes 49160 | tf_op jit(solution)/shard_map/ppermute | solution.py:314
  41.5 4.2 %collective-permute-start.4 = (f32[1,128]{1,0:T(1,128)S(1)}, f32[1,128]{1,0:T(1,128)S(1)}, u32[]{:S(2)}, u32[]{:S(2)}) collective-permute-start(f32[1,128]{1,0:T(1,128)S(1)} %get-tuple-element.42), channel_id=1, source_target_pairs={{0,1},{1,2},{2,3},{3,4},{4,5},{5,6},{6,7},{7,8},{8,9},{9,10},{10,1... | collective-permute-start | bytes 1544 | tf_op jit(solution)/shard_map/ppermute | solution.py:308
  41.5 4.3 %collective-permute-start.5 = (f32[1,128]{1,0:T(1,128)S(1)}, f32[1,128]{1,0:T(1,128)S(1)}, u32[]{:S(2)}, u32[]{:S(2)}) collective-permute-start(f32[1,128]{1,0:T(1,128)S(1)} %get-tuple-element.43), channel_id=1, source_target_pairs={{1,0},{2,1},{3,2},{4,3},{5,4},{6,5},{7,6},{8,7},{9,8},{10,9},{11,1... | collective-permute-start | bytes 1544 | tf_op jit(solution)/shard_map/ppermute | solution.py:308
